TPU v7x, 32 devices: a whole 2x2x4 slice. The times are simulated.
32 devices in a mesh: section: 2 (over core), expert: 4 (over z), tensor: 4 (over y, x).
Axes of the slice: x: 2, y: 2, z: 4, core: 2. Of those that a mesh axis runs over, the one named last changes fastest.
Arguments:
- boundary: bfloat16 [2, 2, 512, 2048], P('section', None, 'expert'), may hold values from -6 to 6
- seq_lengths: int32 [2, 2, 4, 4], P('section', None, 'expert'), may hold values from 1 to 64, 128 in all within a row
- expert_ids: int32 [2, 2, 512, 8], P('section', None, 'expert'), may hold values from 0 to 15, all different within a row; in each aligned block of 128 rows (0 to 127, 128 to 255, ..., all dimensions but the last counted through in order) at most 96 rows name the same one
- route_weights: float32 [2, 2, 512, 8], P('section', None, 'expert'), may hold values from 0.1 to 0.4
- attn_gain: float32 [2, 2048], P('section'), may hold values from 0.25 to 1.75
- moe_gain: float32 [2, 2048], P('section'), may hold values from 0.25 to 1.75
- query_gain: float32 [2, 128], P('section'), may hold values from 0.25 to 1.75
- key_norm_gain: float32 [2, 128], P('section'), may hold values from 0.25 to 1.75
- w_query: bfloat16 [2, 2048, 4096], P('section', 'expert', 'tensor'), may hold values from -0.125 to 0.125
- key_weight: bfloat16 [2, 2048, 512], P('section', 'expert', 'tensor'), may hold values from -0.125 to 0.125
- value_weight: bfloat16 [2, 2048, 512], P('section', 'expert', 'tensor'), may hold values from -0.125 to 0.125
- w_output: bfloat16 [2, 4096, 2048], P('section', 'tensor', 'expert'), may hold values from -0.5 to 0.5
- w_gate: bfloat16 [2, 16, 768, 2048], P('section', 'expert', 'tensor'), may hold values from -0.125 to 0.125
- w_up: bfloat16 [2, 16, 768, 2048], P('section', 'expert', 'tensor'), may hold values from -0.125 to 0.125
- w_down: bfloat16 [2, 16, 768, 2048], P('section', 'expert', 'tensor'), may hold values from -0.4375 to 0.4375
Outputs:
- ends: bfloat16 [2, 2, 512, 2048], P('section', None, 'expert')
- grad_attn_gain: float32 [2, 2048], P('section')
- grad_moe_gain: float32 [2, 2048], P('section')
- grad_query_gain: float32 [2, 128], P('section')
- grad_key_gain: float32 [2, 128], P('section')
- grad_w_query: float32 [2, 2048, 4096], P('section', 'expert', 'tensor')
- grad_w_key: float32 [2, 2048, 512], P('section', 'expert', 'tensor')
- grad_w_value: float32 [2, 2048, 512], P('section', 'expert', 'tensor')
- grad_w_output: float32 [2, 4096, 2048], P('section', 'tensor', 'expert')
- grad_w_gate: float32 [2, 16, 768, 2048], P('section', 'expert', 'tensor')
- grad_w_up: float32 [2, 16, 768, 2048], P('section', 'expert', 'tensor')
- grad_w_down: float32 [2, 16, 768, 2048], P('section', 'expert', 'tensor')
Inputs may be any that keep to these rules, and one draw needn't show every extreme that they name: `expert_ids`: within the 128 rows of one block (one layer, micro-batch and index of the expert axis), no expert is named by more than 96 tokens, a bound that some block reaches. `seq_lengths`: each row sums to 128; the longest sequence of each row has exactly 64 tokens.
All inputs are finite; a program needn't handle non-finite values.
Results may differ from a plain program's by a relative error of at most 0.03.
Values may be sent and summed in bfloat16 or wider, within the bound.
A program may use at most 256 MiB of HBM per device.

v0:
```python
import math

import jax
import jax.numpy as jnp
from jax import lax
from jax.sharding import PartitionSpec as P

EPSILON = 1e-06
THETA = 1000000.0


def passed_along(shard, axis, by):
    count = lax.axis_size(axis)
    pairs = [(i, i + by) for i in range(count) if 0 <= i + by < count]
    return lax.ppermute(shard, axis, pairs)


def norm_rows(value_rows, gain):
    factor = lax.rsqrt(jnp.mean(value_rows * value_rows, axis=-1, keepdims=True) + EPSILON)
    unit_rows = value_rows * factor
    return (unit_rows * gain, unit_rows, factor)


def norm_back(grad_rows, gain, unit_rows, factor):
    weighted = grad_rows * gain
    inner = jnp.mean(weighted * unit_rows, axis=-1, keepdims=True)
    gain_term = jnp.sum((grad_rows * unit_rows).reshape(-1, unit_rows.shape[-1]), axis=0)
    return (factor * (weighted - unit_rows * inner), gain_term)


def rotate_half(value_rows):
    middle = value_rows.shape[-1] // 2
    return jnp.concatenate([-value_rows[..., middle:], value_rows[..., :middle]], axis=-1)


def rotate_back(value_rows):
    middle = value_rows.shape[-1] // 2
    return jnp.concatenate([value_rows[..., middle:], -value_rows[..., :middle]], axis=-1)


def rope_tables(places, head_size):
    steps_half = jnp.arange(head_size // 2, dtype=jnp.float32)
    inverse = jnp.exp(steps_half * (-2.0 * math.log(THETA) / head_size))
    angle_table = places.astype(jnp.float32)[:, None] * inverse[None, :]
    angle_table = jnp.concatenate([angle_table, angle_table], axis=-1)
    return (jnp.cos(angle_table), jnp.sin(angle_table))


def block_layout(seq_lengths, row_count):
    seq_ends = jnp.cumsum(seq_lengths)
    seq_starts = seq_ends - seq_lengths
    places = jnp.arange(row_count, dtype=jnp.int32)
    segment = jnp.sum((places[:, None] >= seq_ends[None, :]).astype(jnp.int32), axis=1)
    numbers = jnp.arange(seq_lengths.shape[0], dtype=jnp.int32)
    offset = jnp.sum(
        jnp.where(segment[:, None] == numbers[None, :], seq_starts[None, :], 0), axis=1
    )
    return (segment, places - offset)


def route_slots(expert_rows, expert_count, capacity):
    flat_ids = expert_rows.reshape(-1)
    numbers = jnp.arange(expert_count, dtype=jnp.int32)
    onehot = (flat_ids[:, None] == numbers[None, :]).astype(jnp.int32)
    earlier = jnp.cumsum(onehot, axis=0) - onehot
    return flat_ids * capacity + jnp.sum(earlier * onehot, axis=1)


def raw_scores(query_rot, key_rot, allowed, score_scale):
    scores = (
        jnp.einsum("tgjd,sgd->gjts", query_rot, key_rot, preferred_element_type=jnp.float32)
        * score_scale
    )
    return jnp.where(allowed, scores, -1e30)


def on_device(
    boundary,
    seq_lengths,
    expert_ids,
    route_weights,
    attn_gain,
    moe_gain,
    query_gain,
    key_norm_gain,
    w_query,
    key_weight,
    value_weight,
    w_output,
    w_gate,
    w_up,
    w_down,
):
    micro_count = boundary.shape[1]
    row_count = boundary.shape[2]
    model_width = boundary.shape[3]
    groups = lax.axis_size("expert")
    section_index = lax.axis_index("section")
    first_section = section_index == 0
    head_size = query_gain.shape[1]
    kv_local = key_weight.shape[2] // head_size
    heads_local = w_query.shape[2] // head_size
    group_size = heads_local // kv_local
    local_experts = w_gate.shape[1]
    top_count = expert_ids.shape[3]
    expert_count = local_experts * groups
    capacity = 3 * row_count * top_count // (2 * expert_count)
    slot_count = expert_count * capacity
    score_scale = 1.0 / math.sqrt(head_size)
    gain_attn = attn_gain[0]
    gain_moe = moe_gain[0]
    gain_query = query_gain[0]
    gain_key = key_norm_gain[0]
    weight_gate = w_gate[0]
    weight_up = w_up[0]
    weight_down = w_down[0]
    full_query, full_key, full_value, full_output = (
        lax.all_gather(w_query[0], "expert", axis=0, tiled=True),
        lax.all_gather(key_weight[0], "expert", axis=0, tiled=True),
        lax.all_gather(value_weight[0], "expert", axis=0, tiled=True),
        lax.all_gather(w_output[0], "expert", axis=1, tiled=True),
    )
    places = jnp.arange(row_count, dtype=jnp.int32)
    causal = places[None, :] <= places[:, None]
    kept_rounds = []
    outputs_late = []
    carried = jnp.zeros((row_count, model_width), jnp.bfloat16)
    for step_index in range(micro_count + 1):
        own_input = boundary[0, min(step_index, micro_count - 1)]
        if step_index == micro_count:
            own_input = jnp.zeros_like(own_input)
        inputs = jnp.where(first_section, own_input, carried)
        pick = jnp.clip(step_index - section_index, 0, micro_count - 1)
        lengths_now = lax.dynamic_index_in_dim(seq_lengths[0, :, 0], pick, 0, keepdims=False)
        ids_now = lax.dynamic_index_in_dim(expert_ids[0], pick, 0, keepdims=False)
        forward_gates_now = lax.dynamic_index_in_dim(route_weights[0], pick, 0, keepdims=False)
        segment, positions = block_layout(lengths_now, row_count)
        forward_cosine, forward_sine_table = rope_tables(positions, head_size)
        forward_allowed = causal & (segment[:, None] == segment[None, :])
        hidden_in = inputs.astype(jnp.float32)
        normed, forward_attn_unit, forward_attn_factor = norm_rows(hidden_in, gain_attn)
        forward_normed_low = normed.astype(jnp.bfloat16)
        query_rows = jnp.dot(
            forward_normed_low, full_query, preferred_element_type=jnp.float32
        ).reshape(row_count, heads_local, head_size)
        heads_key = jnp.dot(
            forward_normed_low, full_key, preferred_element_type=jnp.float32
        ).reshape(row_count, kv_local, head_size)
        forward_value_low = (
            jnp.dot(forward_normed_low, full_value, preferred_element_type=jnp.float32)
            .astype(jnp.bfloat16)
            .reshape(row_count, kv_local, head_size)
        )
        query_normed, forward_query_unit, forward_query_factor = norm_rows(query_rows, gain_query)
        key_normed, forward_key_unit, forward_key_factor = norm_rows(heads_key, gain_key)
        forward_query_rot = (
            (
                query_normed * forward_cosine[:, None, :]
                + rotate_half(query_normed) * forward_sine_table[:, None, :]
            )
            .astype(jnp.bfloat16)
            .reshape(row_count, kv_local, group_size, head_size)
        )
        forward_key_rot = (
            key_normed * forward_cosine[:, None, :]
            + rotate_half(key_normed) * forward_sine_table[:, None, :]
        ).astype(jnp.bfloat16)
        scores = raw_scores(forward_query_rot, forward_key_rot, forward_allowed, score_scale)
        score_peak = jnp.max(scores, axis=-1, keepdims=True)
        forward_log_total = score_peak + jnp.log(
            jnp.sum(jnp.exp(scores - score_peak), axis=-1, keepdims=True)
        )
        probs_low = jnp.exp(scores - forward_log_total).astype(jnp.bfloat16)
        heads_out = jnp.einsum(
            "gjts,sgd->tgjd", probs_low, forward_value_low, preferred_element_type=jnp.float32
        )
        forward_heads_low = heads_out.astype(jnp.bfloat16).reshape(
            row_count, heads_local * head_size
        )
        attn_out = lax.psum(
            jnp.dot(forward_heads_low, full_output, preferred_element_type=jnp.float32), "tensor"
        )
        after_attn = hidden_in + attn_out
        moe_in, forward_moe_unit, forward_moe_factor = norm_rows(after_attn, gain_moe)
        moe_low = moe_in.astype(jnp.bfloat16)
        forward_route_slot = route_slots(ids_now, expert_count, capacity)
        route_count = forward_route_slot.shape[0]
        forward_slot_table = (
            jnp.full((slot_count,), route_count, jnp.int32)
            .at[forward_route_slot]
            .set(jnp.arange(route_count, dtype=jnp.int32))
        )
        padded = jnp.concatenate([moe_low, jnp.zeros((1, model_width), jnp.bfloat16)], axis=0)
        outgoing = jnp.take(padded, forward_slot_table // top_count, axis=0).reshape(
            groups, local_experts * capacity, model_width
        )
        forward_arrived = lax.all_to_all(
            outgoing, "expert", split_axis=0, concat_axis=0, tiled=True
        ).reshape(groups, local_experts, capacity, model_width)
        forward_gate_pre = jnp.einsum(
            "secd,efd->secf", forward_arrived, weight_gate, preferred_element_type=jnp.float32
        )
        forward_up_pre = jnp.einsum(
            "secd,efd->secf", forward_arrived, weight_up, preferred_element_type=jnp.float32
        )
        forward_hidden_low = (jax.nn.silu(forward_gate_pre) * forward_up_pre).astype(jnp.bfloat16)
        partial_out = jnp.einsum(
            "secf,efd->secd", forward_hidden_low, weight_down, preferred_element_type=jnp.float32
        ).reshape(groups, local_experts * capacity, model_width)
        returned = lax.all_to_all(
            partial_out.astype(jnp.bfloat16), "expert", split_axis=0, concat_axis=0, tiled=True
        ).astype(partial_out.dtype)
        returned = returned.reshape(slot_count, returned.shape[2])
        picked = jnp.take(returned, forward_route_slot, axis=0).reshape(
            row_count, top_count, returned.shape[1]
        )
        combined = jnp.sum(forward_gates_now[:, :, None] * picked, axis=1)
        result = after_attn + lax.psum(combined.astype(jnp.bfloat16), "tensor").astype(jnp.float32)
        forward_kept = (
            forward_attn_unit,
            forward_attn_factor,
            forward_normed_low,
            forward_query_unit,
            forward_query_factor,
            forward_key_unit,
            forward_key_factor,
            forward_query_rot,
            forward_key_rot,
            forward_value_low,
            forward_log_total,
            forward_heads_low,
            forward_moe_unit,
            forward_moe_factor,
            forward_route_slot,
            forward_slot_table,
            forward_arrived,
            forward_gate_pre,
            forward_up_pre,
            forward_hidden_low,
            forward_gates_now,
            forward_cosine,
            forward_sine_table,
            forward_allowed,
        )
        result, kept = (result, forward_kept)
        kept_rounds.append(kept)
        low_result = result.astype(jnp.bfloat16)
        if step_index > 0:
            outputs_late.append(low_result)
        if step_index < micro_count:
            carried = passed_along(low_result, "section", 1)
    totals = (
        jnp.zeros_like(gain_attn),
        jnp.zeros_like(gain_moe),
        jnp.zeros_like(gain_query),
        jnp.zeros_like(gain_key),
        jnp.zeros(full_query.shape, jnp.float32),
        jnp.zeros(full_key.shape, jnp.float32),
        jnp.zeros(full_value.shape, jnp.float32),
        jnp.zeros(full_output.shape, jnp.float32),
        jnp.zeros(weight_gate.shape, jnp.float32),
        jnp.zeros(weight_up.shape, jnp.float32),
        jnp.zeros(weight_down.shape, jnp.float32),
    )
    grads_early = [None] * micro_count
    grad_carried = jnp.zeros((row_count, model_width), jnp.bfloat16)
    for step_index in range(micro_count + 1):
        later_index = micro_count - 1 - step_index
        own_grad = boundary[0, max(later_index, 0)]
        if later_index < 0:
            own_grad = jnp.zeros_like(own_grad)
        grad_in = jnp.where(first_section, grad_carried, own_grad)
        (
            attn_unit,
            attn_factor,
            normed_low,
            query_unit,
            query_factor,
            key_unit,
            key_factor,
            query_rot,
            key_rot,
            value_low,
            log_total,
            heads_low,
            moe_unit,
            moe_factor,
            route_slot,
            slot_table,
            arrived,
            gate_pre,
            up_pre,
            hidden_low,
            gates_now,
            cosine,
            sine_table,
            allowed,
        ) = kept_rounds[micro_count - step_index]
        grad_y = grad_in.astype(jnp.float32)
        gate_column = jnp.concatenate([gates_now.reshape(-1), jnp.zeros((1,), jnp.float32)])
        grad_padded = jnp.concatenate([grad_y, jnp.zeros((1, model_width), jnp.float32)], axis=0)
        slot_gate = jnp.take(gate_column, slot_table)
        slot_grad = jnp.take(grad_padded, slot_table // top_count, axis=0)
        grad_send = (
            (slot_gate[:, None] * slot_grad)
            .astype(jnp.bfloat16)
            .reshape(groups, local_experts * capacity, model_width)
        )
        grad_arrived = lax.all_to_all(
            grad_send, "expert", split_axis=0, concat_axis=0, tiled=True
        ).reshape(groups, local_experts, capacity, model_width)
        grad_hidden = jnp.einsum(
            "secd,efd->secf", grad_arrived, weight_down, preferred_element_type=jnp.float32
        )
        sigmoid_gate = jax.nn.sigmoid(gate_pre)
        grad_gate = (
            grad_hidden * up_pre * sigmoid_gate * (1.0 + gate_pre * (1.0 - sigmoid_gate))
        ).astype(jnp.bfloat16)
        grad_up = (grad_hidden * gate_pre * sigmoid_gate).astype(jnp.bfloat16)
        total_down = jnp.einsum(
            "secf,secd->efd", hidden_low, grad_arrived, preferred_element_type=jnp.float32
        )
        total_gate = jnp.einsum(
            "secf,secd->efd", grad_gate, arrived, preferred_element_type=jnp.float32
        )
        total_up = jnp.einsum(
            "secf,secd->efd", grad_up, arrived, preferred_element_type=jnp.float32
        )
        grad_rows = (
            jnp.einsum("secf,efd->secd", grad_gate, weight_gate, preferred_element_type=jnp.float32)
            + jnp.einsum("secf,efd->secd", grad_up, weight_up, preferred_element_type=jnp.float32)
        ).reshape(groups, local_experts * capacity, model_width)
        grad_back = lax.all_to_all(
            grad_rows.astype(jnp.bfloat16), "expert", split_axis=0, concat_axis=0, tiled=True
        ).astype(grad_rows.dtype)
        grad_back = grad_back.reshape(slot_count, grad_back.shape[2])
        grad_moe = jnp.sum(
            jnp.take(grad_back, route_slot, axis=0).reshape(
                row_count, top_count, grad_back.shape[1]
            ),
            axis=1,
        )
        grad_mid, term_moe = norm_back(grad_moe, gain_moe, moe_unit, moe_factor)
        grad_after = grad_y + lax.psum(grad_mid.astype(jnp.bfloat16), "tensor").astype(jnp.float32)
        grad_attn = grad_after.astype(jnp.bfloat16)
        total_output = jnp.einsum(
            "te,td->ed", heads_low, grad_attn, preferred_element_type=jnp.float32
        )
        grad_heads = (
            jnp.einsum("td,ed->te", grad_attn, full_output, preferred_element_type=jnp.float32)
            .astype(jnp.bfloat16)
            .reshape(row_count, kv_local, group_size, head_size)
        )
        probs = jnp.exp(raw_scores(query_rot, key_rot, allowed, score_scale) - log_total)
        grad_value = (
            jnp.einsum(
                "gjts,tgjd->sgd",
                probs.astype(jnp.bfloat16),
                grad_heads,
                preferred_element_type=jnp.float32,
            )
            .astype(jnp.bfloat16)
            .reshape(row_count, kv_local * head_size)
        )
        grad_probs = jnp.einsum(
            "tgjd,sgd->gjts", grad_heads, value_low, preferred_element_type=jnp.float32
        )
        grad_scores = (
            probs * (grad_probs - jnp.sum(probs * grad_probs, axis=-1, keepdims=True))
        ).astype(jnp.bfloat16)
        grad_qrot = (
            jnp.einsum("gjts,sgd->tgjd", grad_scores, key_rot, preferred_element_type=jnp.float32)
            * score_scale
        ).reshape(row_count, heads_local, head_size)
        grad_krot = (
            jnp.einsum("gjts,tgjd->sgd", grad_scores, query_rot, preferred_element_type=jnp.float32)
            * score_scale
        )
        grad_qnorm = grad_qrot * cosine[:, None, :] + rotate_back(
            grad_qrot * sine_table[:, None, :]
        )
        grad_knorm = grad_krot * cosine[:, None, :] + rotate_back(
            grad_krot * sine_table[:, None, :]
        )
        grad_qraw, term_query = norm_back(grad_qnorm, gain_query, query_unit, query_factor)
        grad_kraw, term_key = norm_back(grad_knorm, gain_key, key_unit, key_factor)
        grad_query = grad_qraw.astype(jnp.bfloat16).reshape(row_count, heads_local * head_size)
        grad_key = grad_kraw.astype(jnp.bfloat16).reshape(row_count, kv_local * head_size)
        total_query = jnp.einsum(
            "td,te->de", normed_low, grad_query, preferred_element_type=jnp.float32
        )
        total_key = jnp.einsum(
            "td,te->de", normed_low, grad_key, preferred_element_type=jnp.float32
        )
        total_value = jnp.einsum(
            "td,te->de", normed_low, grad_value, preferred_element_type=jnp.float32
        )
        grad_normed = (
            jnp.einsum("te,de->td", grad_query, full_query, preferred_element_type=jnp.float32)
            + jnp.einsum("te,de->td", grad_key, full_key, preferred_element_type=jnp.float32)
            + jnp.einsum("te,de->td", grad_value, full_value, preferred_element_type=jnp.float32)
        )
        grad_low, term_attn = norm_back(grad_normed, gain_attn, attn_unit, attn_factor)
        grad_x = grad_after + lax.psum(grad_low.astype(jnp.bfloat16), "tensor").astype(jnp.float32)
        terms = (
            term_attn,
            term_moe,
            term_query,
            term_key,
            total_query,
            total_key,
            total_value,
            total_output,
            total_gate,
            total_up,
            total_down,
        )
        grad_x, totals = (grad_x, jax.tree.map(jnp.add, totals, terms))
        low_grad = grad_x.astype(jnp.bfloat16)
        if step_index > 0:
            grads_early[micro_count - step_index] = low_grad
        if step_index < micro_count:
            grad_carried = passed_along(low_grad, "section", -1)
    ends = jnp.where(first_section, jnp.stack(grads_early), jnp.stack(outputs_late))[None]
    sum_query, sum_key, sum_value, sum_output = (
        lax.psum_scatter(
            totals[4].astype(jnp.bfloat16), "expert", scatter_dimension=0, tiled=True
        ).astype(jnp.float32),
        lax.psum_scatter(
            totals[5].astype(jnp.bfloat16), "expert", scatter_dimension=0, tiled=True
        ).astype(jnp.float32),
        lax.psum_scatter(
            totals[6].astype(jnp.bfloat16), "expert", scatter_dimension=0, tiled=True
        ).astype(jnp.float32),
        lax.psum_scatter(
            totals[7].astype(jnp.bfloat16), "expert", scatter_dimension=1, tiled=True
        ).astype(jnp.float32),
    )
    gain_attn_sum, gain_moe_sum, gain_query_sum, gain_key_sum = lax.psum(
        (totals[0], totals[1], totals[2], totals[3]), ("expert", "tensor")
    )
    return (
        ends,
        gain_attn_sum[None],
        gain_moe_sum[None],
        gain_query_sum[None],
        gain_key_sum[None],
        sum_query[None],
        sum_key[None],
        sum_value[None],
        sum_output[None],
        totals[8][None],
        totals[9][None],
        totals[10][None],
    )


def solution(mesh):
    return jax.shard_map(
        on_device,
        mesh=mesh,
        in_specs=(
            P("section", None, "expert", None),
            P("section", None, "expert", None),
            P("section", None, "expert", None),
            P("section", None, "expert", None),
            P("section", None),
            P("section", None),
            P("section", None),
            P("section", None),
            P("section", "expert", "tensor"),
            P("section", "expert", "tensor"),
            P("section", "expert", "tensor"),
            P("section", "tensor", "expert"),
            P("section", "expert", "tensor", None),
            P("section", "expert", "tensor", None),
            P("section", "expert", "tensor", None),
        ),
        out_specs=(
            P("section", None, "expert", None),
            P("section", None),
            P("section", None),
            P("section", None),
            P("section", None),
            P("section", "expert", "tensor"),
            P("section", "expert", "tensor"),
            P("section", "expert", "tensor"),
            P("section", "tensor", "expert"),
            P("section", "expert", "tensor", None),
            P("section", "expert", "tensor", None),
            P("section", "expert", "tensor", None),
        ),
        check_vma=False,
    )
```

profile of v0, /device:TPU:0, one launch (start us, length us, event | category | flops | bytes accessed | tf_op | source)
XLA Modules:
  0.0 3030.3 jit_solution(2209323344177196242)
XLA Ops:
  10.0 22.6 all-gather.1
  41.3 21.5 all-gather
  65.8 37.9 %all-gather.7.cloned.1.call-done = bf16[1,2048,1024]{2,1,0:T(8,128)(2,1)} async-done(((bf16[1,512,1024]{2,1,0:T(8,128)(2,1)}), bf16[1,2048,1024]{2,1,0:T(8,128)(2,1)}) %all-gather.7.cloned.1.call-update) | async-done | bytes 4194320 | tf_op jit(solution)/shard_map/all_gather | solution.py:118
  116.9 68.5 %all-gather.9.cloned.1.call-done = bf16[1,1024,2048]{2,1,0:T(8,128)(2,1)} async-done(((bf16[1,1024,512]{2,1,0:T(8,128)(2,1)}), bf16[1,1024,2048]{2,1,0:T(8,128)(2,1)}) %all-gather.9.cloned.1.call-update) | async-done | bytes 4194320 | tf_op jit(solution)/shard_map/all_gather | solution.py:121
  206.0 34.6 %all-reduce.20.cloned.1.call-done = f32[128,2048]{1,0:T(8,128)} async-done(((f32[128,2048]{1,0:T(8,128)}), f32[128,2048]{1,0:T(8,128)}) %all-reduce.20.cloned.1.call-update) | async-done | bytes 1048592 | tf_op jit(solution)/shard_map/psum | solution.py:180
  244.3 13.8 gather_fusion
  261.5 142.9 %all_to_all.60 = bf16[4,384,2048]{2,1,0:T(8,128)(2,1)S(1)} all-to-all(bf16[4,384,2048]{2,1,0:T(8,128)(2,1)S(1)} %bitcast.1010), channel_id=1, replica_groups=mesh['section'=2,'expert'=4,'tensor'=4] {'expert'}, dimensions={0} | all-to-all | bytes 12582912 | tf_op jit(solution)/shard_map/all_to_all | solution.py:197
  423.0 136.6 %all-to-all-done.1 = bf16[4,384,2048]{2,1,0:T(8,128)(2,1)} async-done(((bf16[4,384,2048]{2,1,0:T(8,128)(2,1)}), bf16[4,384,2048]{2,1,0:T(8,128)(2,1)}, u32[]{:S(2)}, u32[]{:S(2)}) %all-to-all-start.1) | async-done | bytes 6291488 | tf_op jit(solution)/shard_map/all_to_all | solution.py:210
  589.2 43.3 %all-reduce.22.cloned.1.call-done = bf16[128,2048]{1,0:T(8,128)(2,1)} async-done(((bf16[128,2048]{1,0:T(8,128)(2,1)}), bf16[128,2048]{1,0:T(8,128)(2,1)}) %all-reduce.22.cloned.1.call-update) | async-done | bytes 524304 | tf_op jit(solution)/shard_map/psum | solution.py:218
  695.8 40.6 %all-reduce.24.cloned.1.call-done = f32[128,2048]{1,0:T(8,128)} async-done(((f32[128,2048]{1,0:T(8,128)}), f32[128,2048]{1,0:T(8,128)}) %all-reduce.24.cloned.1.call-update) | async-done | bytes 1048592 | tf_op jit(solution)/shard_map/psum | solution.py:180
  757.2 143.0 %all_to_all.61 = bf16[4,384,2048]{2,1,0:T(8,128)(2,1)S(1)} all-to-all(bf16[4,384,2048]{2,1,0:T(8,128)(2,1)S(1)} %bitcast.1011), channel_id=1, replica_groups=mesh['section'=2,'expert'=4,'tensor'=4] {'expert'}, dimensions={0} | all-to-all | bytes 12582912 | tf_op jit(solution)/shard_map/all_to_all | solution.py:197
  933.7 13.8 gather_fusion.5
  947.6 107.5 %all-to-all-done.3 = bf16[4,384,2048]{2,1,0:T(8,128)(2,1)} async-done(((bf16[4,384,2048]{2,1,0:T(8,128)(2,1)}), bf16[4,384,2048]{2,1,0:T(8,128)(2,1)}, u32[]{:S(2)}, u32[]{:S(2)}) %all-to-all-start.3) | async-done | bytes 6291488 | tf_op jit(solution)/shard_map/all_to_all | solution.py:210
  1098.5 29.6 all-reduce.26.cloned.1.call-done
  1164.9 53.0 %all-reduce.28.cloned.1.call-done = f32[128,2048]{1,0:T(8,128)} async-done(((f32[128,2048]{1,0:T(8,128)}), f32[128,2048]{1,0:T(8,128)}) %all-reduce.28.cloned.1.call-update) | async-done | bytes 1048592 | tf_op jit(solution)/shard_map/psum | solution.py:180
  1221.4 13.8 gather_fusion.6
  1252.5 132.8 %all-to-all-done.5 = bf16[4,384,2048]{2,1,0:T(8,128)(2,1)} async-done(((bf16[4,384,2048]{2,1,0:T(8,128)(2,1)}), bf16[4,384,2048]{2,1,0:T(8,128)(2,1)}, u32[]{:S(2)}, u32[]{:S(2)}) %all-to-all-start.5) | async-done | bytes 6291488 | tf_op jit(solution)/shard_map/all_to_all | solution.py:197
  1424.9 131.5 %all-to-all-done.6 = bf16[4,384,2048]{2,1,0:T(8,128)(2,1)} async-done(((bf16[4,384,2048]{2,1,0:T(8,128)(2,1)}), bf16[4,384,2048]{2,1,0:T(8,128)(2,1)}, u32[]{:S(2)}, u32[]{:S(2)}) %all-to-all-start.6) | async-done | bytes 6291488 | tf_op jit(solution)/shard_map/all_to_all | solution.py:333
  1585.1 114.4 %all-to-all-done.11 = bf16[4,384,2048]{2,1,0:T(8,128)(2,1)} async-done(((bf16[4,384,2048]{2,1,0:T(8,128)(2,1)}), bf16[4,384,2048]{2,1,0:T(8,128)(2,1)}, u32[]{:S(2)}, u32[]{:S(2)}) %all-to-all-start.11) | async-done | bytes 6291488 | tf_op jit(solution)/shard_map/all_to_all | solution.py:210
  1738.0 40.9 %all-reduce.30.cloned.1.call-done = bf16[128,2048]{1,0:T(8,128)(2,1)} async-done(((bf16[128,2048]{1,0:T(8,128)(2,1)}), bf16[128,2048]{1,0:T(8,128)(2,1)}) %all-reduce.30.cloned.1.call-update) | async-done | bytes 524304 | tf_op jit(solution)/shard_map/psum | solution.py:344
  1807.5 45.4 %all-reduce.32.cloned.1.call-done = bf16[128,2048]{1,0:T(8,128)(2,1)} async-done(((bf16[128,2048]{1,0:T(8,128)(2,1)}), bf16[128,2048]{1,0:T(8,128)(2,1)}) %all-reduce.32.cloned.1.call-update) | async-done | bytes 524304 | tf_op jit(solution)/shard_map/psum | solution.py:404
  1868.9 13.8 gather_fusion.9
  1888.4 143.9 %all_to_all.62 = bf16[4,384,2048]{2,1,0:T(8,128)(2,1)S(1)} all-to-all(bf16[4,384,2048]{2,1,0:T(8,128)(2,1)S(1)} %bitcast.1008), channel_id=1, replica_groups=mesh['section'=2,'expert'=4,'tensor'=4] {'expert'}, dimensions={0} | all-to-all | bytes 12582912 | tf_op jit(solution)/shard_map/all_to_all | solution.py:309
  2048.7 141.4 %all_to_all.63 = bf16[4,384,2048]{2,1,0:T(8,128)(2,1)S(1)} all-to-all(bf16[4,384,2048]{2,1,0:T(8,128)(2,1)S(1)} %bitcast.1001), channel_id=1, replica_groups=mesh['section'=2,'expert'=4,'tensor'=4] {'expert'}, dimensions={0} | all-to-all | bytes 12582912 | tf_op jit(solution)/shard_map/all_to_all | solution.py:333
  2221.2 41.5 %all-reduce.34.cloned.1.call-done = bf16[128,2048]{1,0:T(8,128)(2,1)} async-done(((bf16[128,2048]{1,0:T(8,128)(2,1)}), bf16[128,2048]{1,0:T(8,128)(2,1)}) %all-reduce.34.cloned.1.call-update) | async-done | bytes 524304 | tf_op jit(solution)/shard_map/psum | solution.py:344
  2291.3 45.5 %all-reduce.36.cloned.1.call-done = bf16[128,2048]{1,0:T(8,128)(2,1)} async-done(((bf16[128,2048]{1,0:T(8,128)(2,1)}), bf16[128,2048]{1,0:T(8,128)(2,1)}) %all-reduce.36.cloned.1.call-update) | async-done | bytes 524304 | tf_op jit(solution)/shard_map/psum | solution.py:404
  2351.5 13.8 gather_fusion.12
  2371.0 144.0 %all_to_all.64 = bf16[4,384,2048]{2,1,0:T(8,128)(2,1)S(1)} all-to-all(bf16[4,384,2048]{2,1,0:T(8,128)(2,1)S(1)} %bitcast.1009), channel_id=1, replica_groups=mesh['section'=2,'expert'=4,'tensor'=4] {'expert'}, dimensions={0} | all-to-all | bytes 12582912 | tf_op jit(solution)/shard_map/all_to_all | solution.py:309
  2552.9 125.5 %all-to-all-done.10 = bf16[4,384,2048]{2,1,0:T(8,128)(2,1)} async-done(((bf16[4,384,2048]{2,1,0:T(8,128)(2,1)}), bf16[4,384,2048]{2,1,0:T(8,128)(2,1)}, u32[]{:S(2)}, u32[]{:S(2)}) %all-to-all-start.10) | async-done | bytes 6291488 | tf_op jit(solution)/shard_map/all_to_all | solution.py:333
  2714.9 37.9 %all-reduce.38.cloned.1.call-done = bf16[128,2048]{1,0:T(8,128)(2,1)} async-done(((bf16[128,2048]{1,0:T(8,128)(2,1)}), bf16[128,2048]{1,0:T(8,128)(2,1)}) %all-reduce.38.cloned.1.call-update) | async-done | bytes 524304 | tf_op jit(solution)/shard_map/psum | solution.py:344
  2866.7 79.1 %all-reduce.6 = (f32[1,2048]{1,0:T(1,128)}, f32[1,2048]{1,0:T(1,128)}, f32[1,128]{1,0:T(1,128)}, f32[1,128]{1,0:T(1,128)}) all-reduce(f32[1,2048]{1,0:T(1,128)S(1)} %bitcast.1106, f32[1,2048]{1,0:T(1,128)S(1)} %bitcast.1105, ...), channel_id=1, replica_groups=mesh['section'=2,'expert'=4,'tensor'=4] {'expert','tensor'}, use_global_device_ids=true, to_apply=%region_75.80 | all-reduce | flops 4352 | bytes 34816 | tf_op jit(solution)/shard_map/psum | solution.py:439
  2957.8 63.0 %reduce-scatter.5.cloned.1.call-done = bf16[512,1024]{1,0:T(8,128)(2,1)} async-done(((bf16[2048,1024]{1,0:T(8,128)(2,1)}), bf16[512,1024]{1,0:T(8,128)(2,1)}) %reduce-scatter.5.cloned.1.call-update) | async-done | bytes 1048592 | tf_op jit(solution)/shard_map/reduce_scatter | solution.py:426
  (878 shorter events, 775.1 us)
Async XLA Ops:
  7.2 404.6 %copy-start = (bf16[1,4,192,2048]{3,2,1,0:T(8,128)(2,1)S(1)}, bf16[1,4,192,2048]{3,2,1,0:T(8,128)(2,1)}, u32[]{:S(2)}) copy-start(bf16[1,4,192,2048]{3,2,1,0:T(8,128)(2,1)} %param.37) | copy-start | bytes 9437188
  7.2 96.6 %all-gather.7.cloned.1.call-start = ((), (), s32[]{:S(2)}) async-start(), calls=%async_computation.30 | async-start | bytes 5242880 | tf_op jit(solution)/shard_map/all_gather | solution.py:118
  8.0 177.5 %all-gather.9.cloned.1.call-start = ((), (), s32[]{:S(2)}) async-start(), calls=%async_computation.31 | async-start | bytes 5242880 | tf_op jit(solution)/shard_map/all_gather | solution.py:121
  8.7 231.9 %all-reduce.20.cloned.1.call-start = ((), (), s32[]{:S(2)}) async-start(), calls=%async_computation.16 | async-start | bytes 2097152 | tf_op jit(solution)/shard_map/psum | solution.py:180
  416.9 142.6 %all-to-all-start.1 = ((bf16[4,384,2048]{2,1,0:T(8,128)(2,1)}), bf16[4,384,2048]{2,1,0:T(8,128)(2,1)}, u32[]{:S(2)}, u32[]{:S(2)}) async-start(bf16[4,384,2048]{2,1,0:T(8,128)(2,1)} %bitcast.998), calls=%async_computation.1 | async-start | bytes 12582912 | tf_op jit(solution)/shard_map/all_to_all | solution.py:210
  422.2 210.3 %all-reduce.22.cloned.1.call-start = ((), (), s32[]{:S(2)}) async-start(), calls=%async_computation.17 | async-start | bytes 1048576 | tf_op jit(solution)/shard_map/psum | solution.py:218
  422.3 495.5 %copy-start.157 = (f32[1,1,128,8]{2,3,1,0:T(8,128)}, f32[1,1,128,8]{2,3,1,0:T(8,128)S(1)}, u32[]{:S(2)}) copy-start(f32[1,1,128,8]{2,3,1,0:T(8,128)S(1)} %get-tuple-element.128) | copy-start | bytes 12292
  422.3 495.6 %copy-start.159 = (f32[1,1,128,8]{2,3,1,0:T(8,128)}, f32[1,1,128,8]{2,3,1,0:T(8,128)S(1)}, u32[]{:S(2)}) copy-start(f32[1,1,128,8]{2,3,1,0:T(8,128)S(1)} %get-tuple-element.126) | copy-start | bytes 12292
  422.9 159.0 %copy-start.184 = (pred[1024]{0:T(1024)(128)(4,1)}, pred[1024]{0:T(1024)(128)(4,1)S(1)}, u32[]{:S(2)}) copy-start(pred[1024]{0:T(1024)(128)(4,1)S(1)} %compare_and_fusion.5) | copy-start | bytes 3076
  589.0 147.4 %all-reduce.24.cloned.1.call-start = ((), (), s32[]{:S(2)}) async-start(), calls=%async_computation.18 | async-start | bytes 2097152 | tf_op jit(solution)/shard_map/psum | solution.py:180
  634.8 9.6 collective-permute-start
  912.6 142.5 %all-to-all-start.3 = ((bf16[4,384,2048]{2,1,0:T(8,128)(2,1)}), bf16[4,384,2048]{2,1,0:T(8,128)(2,1)}, u32[]{:S(2)}, u32[]{:S(2)}) async-start(bf16[4,384,2048]{2,1,0:T(8,128)(2,1)} %bitcast.996), calls=%async_computation.3 | async-start | bytes 12582912 | tf_op jit(solution)/shard_map/all_to_all | solution.py:210
  917.8 210.3 %all-reduce.26.cloned.1.call-start = ((), (), s32[]{:S(2)}) async-start(), calls=%async_computation.19 | async-start | bytes 1048576 | tf_op jit(solution)/shard_map/psum | solution.py:218
  1093.0 148.4 %all-to-all-start.4 = ((bf16[4,384,2048]{2,1,0:T(8,128)(2,1)}), bf16[4,384,2048]{2,1,0:T(8,128)(2,1)}, u32[]{:S(2)}, u32[]{:S(2)}) async-start(bf16[4,384,2048]{2,1,0:T(8,128)(2,1)} %bitcast.1002), calls=%async_computation.4 | async-start | bytes 12582912 | tf_op jit(solution)/shard_map/all_to_all | solution.py:309
  1098.4 119.5 %all-reduce.28.cloned.1.call-start = ((), (), s32[]{:S(2)}) async-start(), calls=%async_computation.20 | async-start | bytes 2097152 | tf_op jit(solution)/shard_map/psum | solution.py:180
  1129.6 3.1 collective-permute-start.1
  1241.4 144.0 %all-to-all-start.5 = ((bf16[4,384,2048]{2,1,0:T(8,128)(2,1)}), bf16[4,384,2048]{2,1,0:T(8,128)(2,1)}, u32[]{:S(2)}, u32[]{:S(2)}) async-start(bf16[4,384,2048]{2,1,0:T(8,128)(2,1)} %bitcast.1007), calls=%async_computation.5 | async-start | bytes 12582912 | tf_op jit(solution)/shard_map/all_to_all | solution.py:197
  1413.0 143.4 %all-to-all-start.6 = ((bf16[4,384,2048]{2,1,0:T(8,128)(2,1)}), bf16[4,384,2048]{2,1,0:T(8,128)(2,1)}, u32[]{:S(2)}, u32[]{:S(2)}) async-start(bf16[4,384,2048]{2,1,0:T(8,128)(2,1)} %bitcast.1000), calls=%async_computation.6 | async-start | bytes 12582912 | tf_op jit(solution)/shard_map/all_to_all | solution.py:333
  1556.4 143.0 %all-to-all-start.11 = ((bf16[4,384,2048]{2,1,0:T(8,128)(2,1)}), bf16[4,384,2048]{2,1,0:T(8,128)(2,1)}, u32[]{:S(2)}, u32[]{:S(2)}) async-start(bf16[4,384,2048]{2,1,0:T(8,128)(2,1)} %bitcast.997), calls=%async_computation.11 | async-start | bytes 12582912 | tf_op jit(solution)/shard_map/all_to_all | solution.py:210
  1561.8 217.1 %all-reduce.30.cloned.1.call-start = ((), (), s32[]{:S(2)}) async-start(), calls=%async_computation.21 | async-start | bytes 1048576 | tf_op jit(solution)/shard_map/psum | solution.py:344
  1735.3 117.6 %all-reduce.32.cloned.1.call-start = ((), (), s32[]{:S(2)}) async-start(), calls=%async_computation.22 | async-start | bytes 1048576 | tf_op jit(solution)/shard_map/psum | solution.py:404
  1807.5 455.3 %all-reduce.34.cloned.1.call-start = ((), (), s32[]{:S(2)}) async-start(), calls=%async_computation.23 | async-start | bytes 1048576 | tf_op jit(solution)/shard_map/psum | solution.py:344
  1855.3 10.2 collective-permute-start.2
  2219.1 117.7 %all-reduce.36.cloned.1.call-start = ((), (), s32[]{:S(2)}) async-start(), calls=%async_computation.24 | async-start | bytes 1048576 | tf_op jit(solution)/shard_map/psum | solution.py:404
  2339.4 9.9 collective-permute-start.3
  2534.6 143.8 %all-to-all-start.10 = ((bf16[4,384,2048]{2,1,0:T(8,128)(2,1)}), bf16[4,384,2048]{2,1,0:T(8,128)(2,1)}, u32[]{:S(2)}, u32[]{:S(2)}) async-start(bf16[4,384,2048]{2,1,0:T(8,128)(2,1)} %bitcast.999), calls=%async_computation.10 | async-start | bytes 12582912 | tf_op jit(solution)/shard_map/all_to_all | solution.py:333
  2540.0 212.8 %all-reduce.38.cloned.1.call-start = ((), (), s32[]{:S(2)}) async-start(), calls=%async_computation.25 | async-start | bytes 1048576 | tf_op jit(solution)/shard_map/psum | solution.py:344
  2709.1 236.7 %reduce-scatter.9.cloned.1.call-start = ((), (), s32[]{:S(2)}) async-start(), calls=%async_computation.28 | async-start | bytes 655360 | tf_op jit(solution)/shard_map/reduce_scatter | solution.py:432
  2762.3 185.2 %reduce-scatter.7.cloned.1.call-start = ((), (), s32[]{:S(2)}) async-start(), calls=%async_computation.27 | async-start | bytes 655360 | tf_op jit(solution)/shard_map/reduce_scatter | solution.py:429
  2774.4 174.6 %all-reduce.40.cloned.1.call-start = ((), (), s32[]{:S(2)}) async-start(), calls=%async_computation.32 | async-start | bytes 2097152 | tf_op jit(solution)/shard_map/psum | solution.py:404
  2782.0 172.9 %reduce-scatter.11.cloned.1.call-start = ((), (), s32[]{:S(2)}) async-start(), calls=%async_computation.29 | async-start | bytes 5242880 | tf_op jit(solution)/shard_map/reduce_scatter | solution.py:435
  2791.7 229.1 %reduce-scatter.5.cloned.1.call-start = ((), (), s32[]{:S(2)}) async-start(), calls=%async_computation.26 | async-start | bytes 5242880 | tf_op jit(solution)/shard_map/reduce_scatter | solution.py:426
  (217 other events, 4893.5 us)
Sparse Core Ops, SparseCore 0:
  9.6 94.1 all-gather.6
  105.4 80.0 all-gather.8
  189.5 51.0 all-reduce.19
  589.1 43.4 all-reduce.21
  683.7 52.5 all-reduce.23
  1084.6 43.4 all-reduce.25
  1165.0 52.8 all-reduce.27
  1735.4 43.4 all-reduce.29
  1807.6 45.3 all-reduce.31
  2219.2 43.4 all-reduce.33
  2291.5 45.3 all-reduce.35
  2709.2 43.4 all-reduce.37
  2762.4 21.6 reduce-scatter.8
  2786.8 19.7 reduce-scatter.6
  2810.1 50.9 all-reduce.39
  2863.3 77.9 reduce-scatter.10
  2943.5 77.2 reduce-scatter.4
where the time goes:
time: 3040 us; the launch traced here: 3030 us
  waiting for transfers between devices  1330 us (44%)
  blocking collectives  838 us (28%)
  local copies, waits for them, and re-layouts  316 us (10%)
  matrix products  245 us (8%)
  other arithmetic  234 us (8%)
  starting transfers between devices  47 us (2%)
    all_to_all x3, waiting for transfers between devices, on_device(): lax.all_to_all(partial_out.astype(jnp.bfloat16), 'expert', split_axis=0,...  358 us
    all_to_all x2, blocking collectives, on_device(): lax.all_to_all(grad_send, 'expert', split_axis=0, concat_axis=0, tiled=True)  288 us
    all_to_all x2, blocking collectives, on_device(): lax.all_to_all(outgoing, 'expert', split_axis=0, concat_axis=0, tiled=True)  286 us
    all_to_all x2, waiting for transfers between devices, on_device(): lax.all_to_all(grad_rows.astype(jnp.bfloat16), 'expert', split_axis=0, co...  257 us
    all_to_all x1, blocking collectives, on_device(): lax.all_to_all(grad_rows.astype(jnp.bfloat16), 'expert', split_axis=0, co...  141 us
    all_to_all x1, waiting for transfers between devices, on_device(): lax.all_to_all(outgoing, 'expert', split_axis=0, concat_axis=0, tiled=True)  133 us
    psum x3, waiting for transfers between devices, on_device(): lax.psum(jnp.dot(forward_heads_low, full_output, preferred_element_type=j...  128 us
    psum x3, waiting for transfers between devices, on_device(): lax.psum(grad_mid.astype(jnp.bfloat16), 'tensor').astype(jnp.float32)  120 us
  transfers between devices with their start and end apart: 28, of which 20 were waited for; matrix products, arithmetic and copies ran while one was open for 11% of the time, Pallas kernels for 0%

commit v1 on v0

v1 whole, which is shorter than its diff:
```python
import functools
import math

import jax
import jax.numpy as jnp
from jax import lax
from jax.experimental import pallas as pl
from jax.experimental.pallas import tpu as pltpu
from jax.sharding import PartitionSpec as P

EPSILON = 1e-06
THETA = 1000000.0
LANES = 128
TERM_ROWS = 24
TERM_COLS = 256
MESH = pl.DeviceIdType.MESH
F32 = jnp.float32
BF16 = jnp.bfloat16
VMEM_LIMIT = 60 * 1024 * 1024

ANY = pl.BlockSpec(memory_space=pl.ANY)
VM = pl.BlockSpec(memory_space=pltpu.VMEM)


def partner(index, k, count):
    out, bit = 0, 1
    while bit < count:
        out = out + bit * lax.rem(lax.div(index, bit) + lax.div(k, bit), 2)
        bit *= 2
    return out


def rows_at(start, size):
    return pl.ds(pl.multiple_of(start, size), size)


def remote(src, dst, send_sem, recv_sem, **where):
    return pltpu.make_async_remote_copy(
        src_ref=src,
        dst_ref=dst,
        send_sem=send_sem,
        recv_sem=recv_sem,
        device_id=where,
        device_id_type=MESH,
    )


def greet(peers):
    barrier = pltpu.get_barrier_semaphore()
    for where in peers:
        pl.semaphore_signal(barrier, inc=1, device_id=where, device_id_type=MESH)
    pl.semaphore_wait(barrier, len(peers))


def layer_peers(z, t, nz, nt):
    i32 = jnp.int32
    peers = [{"expert": partner(z, i32(k), nz)} for k in range(1, nz)]
    peers += [{"tensor": partner(t, i32(k), nt)} for k in range(1, nt)]
    return peers


def dot(a, b):
    return lax.dot_general(a, b, (((1,), (0,)), ((), ())), preferred_element_type=F32)


def dot_nt(a, b):
    return lax.dot_general(a, b, (((1,), (1,)), ((), ())), preferred_element_type=F32)


def dot_tn(a, b):
    return lax.dot_general(a, b, (((0,), (0,)), ((), ())), preferred_element_type=F32)


def unit_rows(value):
    factor = lax.rsqrt(jnp.mean(value * value, axis=-1, keepdims=True) + EPSILON)
    return value * factor, factor


def norm_back(grad, gain, unit, factor):
    weighted = grad * gain
    inner = jnp.mean(weighted * unit, axis=-1, keepdims=True)
    return factor * (weighted - unit * inner), jnp.sum(grad * unit, axis=0, keepdims=True)


def expert_gates(gate_rows, first_expert, local_experts, width):
    rows = gate_rows.shape[0]
    lane = lax.broadcasted_iota(jnp.int32, gate_rows.shape, 1)
    column = lax.broadcasted_iota(jnp.int32, (rows, local_experts * width), 1)
    out = None
    for e in range(local_experts):
        one = jnp.sum(jnp.where(lane == first_expert + e, gate_rows, 0.0), axis=1, keepdims=True)
        wide = jnp.broadcast_to(one, column.shape)
        out = wide if out is None else jnp.where(column >= e * width, wide, out)
    return out


def write_terms(terms_ref, row, vector):
    for i in range(vector.shape[1] // TERM_COLS):
        terms_ref[row + i : row + i + 1, :] = vector[:, i * TERM_COLS : (i + 1) * TERM_COLS]


def exchange_sems(nz, nt):
    dma = pltpu.SemaphoreType.DMA
    return [dma((nz,)), dma((nz,)), dma((nz, nt)), dma((nz, nt))] * 2 + [dma((nt,)), dma((nt,))]


def exchange_scratch(nz, nt, rows, block, width):
    return [
        pltpu.VMEM((nz, block, width), BF16),
        pltpu.VMEM((nz, block, width), BF16),
        pltpu.VMEM((block, width), F32),
        pltpu.VMEM((nz, nt, rows, width), BF16),
        pltpu.VMEM((nz, rows, width), BF16),
        pltpu.VMEM((nz, rows, width), BF16),
        pltpu.VMEM((rows, width), F32),
        pltpu.VMEM((block, width), BF16),
    ] + exchange_sems(nz, nt)


def exchange(z, t, nz, nt, rows, own_rows, scratch, ready, work):
    (full, outgoing, part, came_near, passed, came_far, total, _) = scratch[:8]
    (gz_send, gz_recv, gt_send, gt_recv, rz_send, rz_recv, rt_send, rt_recv) = scratch[8:16]
    i32 = jnp.int32
    mine = rows_at(t * rows, rows)

    def far_copy(k):
        return remote(
            full.at[z, mine],
            full.at[z, mine],
            gz_send.at[k],
            gz_recv.at[k],
            expert=partner(z, i32(k), nz),
        )

    def near_copy(k, source, j):
        return remote(
            full.at[source, mine],
            full.at[source, mine],
            gt_send.at[k, j],
            gt_recv.at[k, j],
            tensor=partner(t, i32(j), nt),
        )

    def near_arrival(k, source, j):
        theirs = rows_at(partner(t, i32(j), nt) * rows, rows)
        return remote(
            full.at[source, theirs],
            full.at[source, theirs],
            gt_send.at[k, j],
            gt_recv.at[k, j],
            tensor=partner(t, i32(j), nt),
        )

    def far_arrival(k):
        source = partner(z, i32(k), nz)
        return remote(
            full.at[source, mine],
            full.at[source, mine],
            gz_send.at[k],
            gz_recv.at[k],
            expert=source,
        )

    def part_copy(k, j):
        peer = partner(t, i32(j), nt)
        return remote(
            outgoing.at[k, rows_at(peer * rows, rows)],
            came_near.at[k, j],
            rt_send.at[k, j],
            rt_recv.at[k, j],
            tensor=peer,
        )

    def sum_copy(k):
        return remote(
            passed.at[k],
            came_far.at[k],
            rz_send.at[k],
            rz_recv.at[k],
            expert=partner(z, k, nz),
        )

    full[z, mine] = own_rows
    for k in range(1, nz):
        far_copy(k).start()
    for j in range(1, nt):
        near_copy(0, z, j).start()

    ready()

    def produce(k, source):
        for j in range(1, nt):
            near_arrival(k, source, j).wait_recv()
        part[...] = work(k, source, full[source])
        outgoing[k] = part[...].astype(BF16)
        for j in range(1, nt):
            part_copy(k, j).start()
        return part[mine]

    def collect(k):
        out = passed_own[k]
        for j in range(1, nt):
            part_copy(k, j).wait_recv()
            out = out + came_near[k, j].astype(F32)
        return out

    passed_own = scratch[18]
    passed_own[0] = produce(i32(0), z)
    for k in range(1, nz):
        far_arrival(k).wait_recv()
        for j in range(1, nt):
            near_copy(k, partner(z, i32(k), nz), j).start()

    def step(k, carry):
        passed_own[k] = produce(k, partner(z, k, nz))

        @pl.when(k >= 2)
        def _():
            passed[k - 1] = collect(k - 1).astype(BF16)
            sum_copy(k - 1).start()

        return carry

    lax.fori_loop(1, nz, step, 0)
    passed[nz - 1] = collect(nz - 1).astype(BF16)
    sum_copy(i32(nz - 1)).start()
    total[...] = collect(0)
    for k in range(1, nz):
        sum_copy(i32(k)).wait_recv()
        total[...] += came_far[k].astype(F32)

    def finish():
        for k in range(1, nz):
            far_copy(k).wait_send()
            sum_copy(i32(k)).wait_send()
        for k in range(nz):
            source = partner(z, i32(k), nz)
            for j in range(1, nt):
                near_copy(k, source, j).wait_send()
                part_copy(k, j).wait_send()

    return finish


def spread_rows(t, nt, rows, block_ref, send_sem, recv_sem):
    i32 = jnp.int32
    mine = rows_at(t * rows, rows)
    for j in range(1, nt):
        remote(
            block_ref.at[mine],
            block_ref.at[mine],
            send_sem.at[j],
            recv_sem.at[j],
            tensor=partner(t, i32(j), nt),
        ).start()

    def wait():
        for j in range(1, nt):
            peer = partner(t, i32(j), nt)
            theirs = rows_at(peer * rows, rows)
            copy = remote(
                block_ref.at[theirs],
                block_ref.at[theirs],
                send_sem.at[j],
                recv_sem.at[j],
                tensor=peer,
            )
            copy.wait_send()
            copy.wait_recv()

    return wait


def reduce_rows(t, nt, rows, part, outgoing, came, send_sem, recv_sem):
    i32 = jnp.int32
    outgoing[...] = part[...].astype(BF16)

    def copy(j):
        peer = partner(t, i32(j), nt)
        return remote(
            outgoing.at[rows_at(peer * rows, rows)],
            came.at[j],
            send_sem.at[j],
            recv_sem.at[j],
            tensor=peer,
        )

    for j in range(1, nt):
        copy(j).start()
    total = part[rows_at(t * rows, rows)]
    for j in range(1, nt):
        copy(j).wait_recv()
        total = total + came[j].astype(F32)
    for j in range(1, nt):
        copy(j).wait_send()
    return total


def start_kernel(
    nz, nt, boundary, tabs, gates, gains, wq, wk, wv, wo, wg, wu, wd,
    ends_out, tabs_out, gates_out, gains_out, wq_out, wk_out, wv_out, wo_out, sg_out, su_out, sd_out,
    own_sem, sib_send, sib_recv, gate_send, gate_recv,
    right_send, right_recv, left_send, left_recv, pass_send, pass_recv,
):
    s, z = lax.axis_index("section"), lax.axis_index("expert")
    other = 1 - s
    i32 = jnp.int32
    peers = [{"section": other}]
    for k in range(1, nz):
        zz = partner(z, i32(k), nz)
        peers += [{"expert": zz}, {"section": other, "expert": zz}]

    shard_in, shard_out = (wq, wk, wv, wo), (wq_out, wk_out, wv_out, wo_out)

    def place(a, layer, owner):
        out = shard_out[a]
        if a < 3:
            size = shard_in[a].shape[0]
            return out.at[layer, rows_at(owner * size, size)]
        size = shard_in[a].shape[1]
        return out.at[layer, :, rows_at(owner * size, size)]

    count = len(shard_in)
    own = [pltpu.make_async_copy(shard_in[a], place(a, s, z), own_sem.at[a]) for a in range(count)]
    own += [
        pltpu.make_async_copy(boundary.at[s], ends_out.at[s], own_sem.at[4]),
        pltpu.make_async_copy(tabs.at[s], tabs_out.at[s], own_sem.at[5]),
        pltpu.make_async_copy(gates.at[s], gates_out.at[s, z], own_sem.at[6]),
        pltpu.make_async_copy(gains, gains_out.at[s], own_sem.at[7]),
    ]
    for copy in own:
        copy.start()
    greet(peers)

    def hop(a, owner, step, right, src=None):
        spot = place(a, s, owner)
        sends, recvs = (right_send, right_recv) if right else (left_send, left_recv)
        target = z + 1 if right else z - 1
        return remote(
            spot if src is None else src, spot, sends.at[a, step], recvs.at[a, step], expert=target
        )

    def hand(a, owner, src=None):
        spot = place(a, s, owner)
        return remote(
            spot if src is None else src,
            spot,
            pass_send.at[a, owner],
            pass_recv.at[a, owner],
            section=other,
        )

    def handed(a, owner):
        spot = place(a, other, owner)
        return remote(spot, spot, pass_send.at[a, owner], pass_recv.at[a, owner], section=other)

    for a in range(count):

        @pl.when(z + 1 < nz)
        def _():
            hop(a, z, 1, True, shard_in[a]).start()

        @pl.when(z >= 1)
        def _():
            hop(a, z, 1, False, shard_in[a]).start()

        hand(a, z, shard_in[a]).start()

    sib = [
        remote(boundary.at[other], ends_out.at[s], sib_send.at[0], sib_recv.at[0], section=other),
        remote(tabs.at[other], tabs_out.at[s], sib_send.at[1], sib_recv.at[1], section=other),
        remote(gains, gains_out.at[s], sib_send.at[2], sib_recv.at[2], section=other),
        remote(wg, sg_out, sib_send.at[3], sib_recv.at[3], section=other),
        remote(wu, su_out, sib_send.at[4], sib_recv.at[4], section=other),
        remote(wd, sd_out, sib_send.at[5], sib_recv.at[5], section=other),
    ]
    for copy in sib:
        copy.start()

    def gate_copy(d, k):
        zz = partner(z, i32(k), nz)
        section = s if d == 0 else other
        return remote(
            gates.at[section],
            gates_out.at[s, z],
            gate_send.at[d, k],
            gate_recv.at[d, k],
            section=section,
            expert=zz,
        )

    def gate_arrival(d, k):
        zz = partner(z, i32(k), nz)
        section = s if d == 0 else other
        return remote(
            gates.at[section],
            gates_out.at[section, zz],
            gate_send.at[d, k],
            gate_recv.at[d, k],
            section=section,
            expert=zz,
        )

    for d in range(2):
        for k in range(nz):
            if d or k:
                gate_copy(d, k).start()

    for step in range(1, nz):
        for a in range(count):

            @pl.when(z >= step)
            def _():
                hop(a, z - step, step, True).wait_recv()
                hand(a, z - step).start()

            @pl.when((z >= step) & (z + 1 < nz))
            def _():
                hop(a, z - step, step + 1, True).start()

            @pl.when(z + step < nz)
            def _():
                hop(a, z + step, step, False).wait_recv()
                hand(a, z + step).start()

            @pl.when((z + step < nz) & (z >= 1))
            def _():
                hop(a, z + step, step + 1, False).start()

    for copy in own:
        copy.wait()
    for i, copy in enumerate(sib):
        copy.wait_send()
    sib_in = [
        remote(boundary.at[other], ends_out.at[other], sib_send.at[0], sib_recv.at[0], section=other),
        remote(tabs.at[other], tabs_out.at[other], sib_send.at[1], sib_recv.at[1], section=other),
        remote(gains, gains_out.at[other], sib_send.at[2], sib_recv.at[2], section=other),
    ] + sib[3:]
    for copy in sib_in:
        copy.wait_recv()
    for d in range(2):
        for k in range(nz):
            if d or k:
                gate_copy(d, k).wait_send()
                gate_arrival(d, k).wait_recv()
    for a in range(count):
        for owner in range(nz):
            hand(a, owner).wait_send()
            handed(a, owner).wait_recv()
        for step in range(1, nz):

            @pl.when((z >= step - 1) & (z + 1 < nz))
            def _():
                hop(a, z - (step - 1), step, True).wait_send()

            @pl.when((z + step - 1 < nz) & (z >= 1))
            def _():
                hop(a, z + (step - 1), step, False).wait_send()


def heads_to_rows(value, heads, size):
    return jnp.concatenate([value[:, h * size : (h + 1) * size] for h in range(heads)], axis=0)


def rows_to_heads(value, heads, block):
    return jnp.concatenate([value[h * block : (h + 1) * block] for h in range(heads)], axis=1)


def split_gains(gains, layer, width, size):
    row = gains[layer]
    return (
        row[:, :width],
        row[:, width : 2 * width],
        row[:, 2 * width : 2 * width + size],
        row[:, 2 * width + size :],
    )


def tiled(value, times):
    return jnp.concatenate([value] * times, axis=0)


def half_turn(value):
    return pltpu.roll(value, value.shape[-1] // 2, value.ndim - 1)


def attend_kernel(
    layer, source, nz, nt, heads,
    x_ref, tabs, gains, wq, wk, wv, wo,
    h1_ref, b_ref, a_ref, q_ref, k_ref, v_ref, qr_ref, kr_ref, o_ref,
    wq_s, wk_s, wv_s, wo_s, part, outgoing, came, w_sem, s_sem, r_sem,
):
    z, t = lax.axis_index("expert"), lax.axis_index("tensor")
    loads = [
        pltpu.make_async_copy(src.at[layer], dst, w_sem.at[i])
        for i, (src, dst) in enumerate(((wq, wq_s), (wk, wk_s), (wv, wv_s), (wo, wo_s)))
    ]
    for load in loads:
        load.start()
    i32 = jnp.int32
    greet([{"tensor": partner(t, i32(j), nt)} for j in range(1, nt)])

    block = x_ref.shape[1]
    rows = block // nt
    size = tabs.shape[-1]
    g_attn, g_moe, g_query, g_key = split_gains(gains, layer, x_ref.shape[2], size)
    cos, sin, bias = tabs[layer, 0], tabs[layer, 1], tabs[layer, 2]
    unit, _ = unit_rows(x_ref[source].astype(F32))
    a_ref[...] = (unit * g_attn).astype(BF16)
    loads[0].wait()
    q = dot(a_ref[...], wq_s[...])
    q_ref[...] = q
    loads[1].wait()
    loads[2].wait()
    k = dot(a_ref[...], wk_s[...])
    k_ref[...] = k
    v = dot(a_ref[...], wv_s[...]).astype(BF16)
    v_ref[...] = v
    qn = unit_rows(heads_to_rows(q, heads, size))[0] * g_query
    kn = unit_rows(k)[0] * g_key
    qr = (qn * tiled(cos, heads) + half_turn(qn) * tiled(sin, heads)).astype(BF16)
    kr = (kn * cos + half_turn(kn) * sin).astype(BF16)
    qr_ref[...] = qr
    kr_ref[...] = kr
    scores = dot_nt(qr, kr) * (1.0 / math.sqrt(size)) + tiled(bias, heads)
    peak = jnp.max(scores, axis=-1, keepdims=True)
    weight = jnp.exp(scores - peak)
    probs = weight * (1.0 / jnp.sum(weight, axis=-1, keepdims=True))
    o = dot(probs.astype(BF16), v).astype(BF16)
    o_ref[...] = rows_to_heads(o, heads, block)
    loads[3].wait()
    part[...] = dot(o_ref[...], wo_s[...])
    total = reduce_rows(t, nt, rows, part, outgoing, came, s_sem, r_sem)
    h1 = x_ref[source, rows_at(t * rows, rows)].astype(F32) + total
    h1_ref[...] = h1
    b_ref[...] = (unit_rows(h1)[0] * g_moe).astype(BF16)


def load_experts(layer, s, own, sibling, scratch, sems):
    def copies(refs):
        return [pltpu.make_async_copy(r, d, sems.at[i]) for i, (r, d) in enumerate(zip(refs, scratch))]

    @pl.when(s == layer)
    def _():
        for copy in copies(own):
            copy.start()

    @pl.when(s != layer)
    def _():
        for copy in copies(sibling):
            copy.start()

    return copies(own)


def experts_kernel(
    layer, nz, nt, local_experts,
    b_ref, h1_ref, gates, wg, wu, wd, sg, su, sd,
    y_ref, b_out, g_out, u_out,
    wg_s, wu_s, wd_s, g_s, u_s, w_sem, o_sem, own_part, *scratch,
):
    s, z, t = lax.axis_index("section"), lax.axis_index("expert"), lax.axis_index("tensor")
    rows = b_ref.shape[0]
    loads = load_experts(layer, s, (wg, wu, wd), (sg, su, sd), (wg_s, wu_s, wd_s), w_sem)
    greet(layer_peers(z, t, nz, nt))
    scratch = list(scratch) + [own_part]
    width = wg.shape[0] // local_experts

    def ready():
        for load in loads:
            load.wait()

    def work(k, origin, rows_in):
        gate_pre = dot_nt(rows_in, wg_s[...])
        up_pre = dot_nt(rows_in, wu_s[...])
        g_s[origin] = gate_pre
        u_s[origin] = up_pre
        weight = expert_gates(gates[layer, origin], z * local_experts, local_experts, width)
        hidden = (gate_pre * jax.nn.sigmoid(gate_pre) * up_pre * weight).astype(BF16)
        return dot(hidden, wd_s[...])

    finish = exchange(z, t, nz, nt, rows, b_ref[...], scratch, ready, work)
    full, total, whole = scratch[0], scratch[6], scratch[7]
    saves = [
        pltpu.make_async_copy(full, b_out, o_sem.at[0]),
        pltpu.make_async_copy(g_s, g_out, o_sem.at[1]),
        pltpu.make_async_copy(u_s, u_out, o_sem.at[2]),
    ]
    for save in saves:
        save.start()
    whole[rows_at(t * rows, rows)] = (h1_ref[...] + total[...]).astype(BF16)
    wait = spread_rows(t, nt, rows, whole, scratch[16], scratch[17])
    finish()
    wait()
    y_ref[0] = whole[...]
    for save in saves:
        save.wait()


def experts_back_kernel(
    layer, nz, nt, local_experts,
    dy_ref, h1_ref, gains, gates, g_in, u_in, wg, wu, wd, sg, su, sd,
    dat_ref, dh1_ref, term_ref, dy_out, hid_out, dg_out, du_out,
    wg_s, wu_s, wd_s, g_s, u_s, hid_s, dg_s, du_s, w_sem, g_sem, u_sem, o_sem, own_part, *scratch,
):
    s, z, t = lax.axis_index("section"), lax.axis_index("expert"), lax.axis_index("tensor")
    rows = dy_ref.shape[0]
    loads = load_experts(layer, s, (wd, wg, wu), (sd, sg, su), (wd_s, wg_s, wu_s), w_sem)

    def kept(k):
        origin, slot = partner(z, k, nz), lax.rem(k, 2)
        return (
            pltpu.make_async_copy(g_in.at[origin], g_s.at[slot], g_sem.at[slot]),
            pltpu.make_async_copy(u_in.at[origin], u_s.at[slot], u_sem.at[slot]),
        )

    for load in kept(jnp.int32(0)):
        load.start()
    greet(layer_peers(z, t, nz, nt))
    scratch = list(scratch) + [own_part]
    width = wg.shape[0] // local_experts

    def ready():
        for load in loads:
            load.wait()

    def work(k, origin, rows_in):
        for load in kept(k):
            load.wait()

        @pl.when(k + 1 < nz)
        def _():
            for load in kept(k + 1):
                load.start()

        slot = lax.rem(k, 2)
        gate_pre, up_pre = g_s[slot], u_s[slot]
        weight = expert_gates(gates[layer, origin], z * local_experts, local_experts, width)
        sigmoid = jax.nn.sigmoid(gate_pre)
        silu = gate_pre * sigmoid
        hid_s[origin] = (silu * up_pre * weight).astype(BF16)
        grad_hidden = dot_nt(rows_in, wd_s[...]) * weight
        dg_s[origin] = (grad_hidden * up_pre * sigmoid * (1.0 + gate_pre * (1.0 - sigmoid))).astype(BF16)
        du_s[origin] = (grad_hidden * silu).astype(BF16)
        return dot(dg_s[origin], wg_s[...]) + dot(du_s[origin], wu_s[...])

    finish = exchange(z, t, nz, nt, rows, dy_ref[...], scratch, ready, work)
    full, total, whole = scratch[0], scratch[6], scratch[7]
    saves = [
        pltpu.make_async_copy(full, dy_out, o_sem.at[0]),
        pltpu.make_async_copy(hid_s, hid_out, o_sem.at[1]),
        pltpu.make_async_copy(dg_s, dg_out, o_sem.at[2]),
        pltpu.make_async_copy(du_s, du_out, o_sem.at[3]),
    ]
    for save in saves:
        save.start()
    unit, factor = unit_rows(h1_ref[...])
    width = dy_ref.shape[1]
    back, term = norm_back(total[...], gains[layer, :, width : 2 * width], unit, factor)
    dh1 = dy_ref[...].astype(F32) + back
    dh1_ref[...] = dh1
    term_ref[...] = term
    whole[rows_at(t * rows, rows)] = dh1.astype(BF16)
    wait = spread_rows(t, nt, rows, whole, scratch[16], scratch[17])
    finish()
    wait()
    dat_ref[...] = whole[...]
    for save in saves:
        save.wait()


def attend_back_kernel(
    layer, source, nz, nt, heads,
    x_ref, tabs, gains, dat_ref, dh1_ref, term_moe,
    q_ref, k_ref, v_ref, qr_ref, kr_ref, wq, wk, wv, wo,
    dxr_ref, dx_ref, dqkv_ref, terms_ref,
    wq_s, wk_s, wv_s, wo_s, part, outgoing, came, whole, w_sem, s_sem, r_sem, gs_sem, gr_sem,
):
    z, t = lax.axis_index("expert"), lax.axis_index("tensor")
    loads = [
        pltpu.make_async_copy(src.at[layer], dst, w_sem.at[i])
        for i, (src, dst) in enumerate(((wo, wo_s), (wq, wq_s), (wk, wk_s), (wv, wv_s)))
    ]
    for load in loads:
        load.start()
    i32 = jnp.int32
    greet([{"tensor": partner(t, i32(j), nt)} for j in range(1, nt)])

    block = x_ref.shape[1]
    rows = block // nt
    size = tabs.shape[-1]
    g_attn, _, g_query, g_key = split_gains(gains, layer, x_ref.shape[2], size)
    scale = 1.0 / math.sqrt(size)
    cos, sin, bias = tabs[layer, 0], tabs[layer, 1], tabs[layer, 2]
    cos_all, sin_all = tiled(cos, heads), tiled(sin, heads)
    qr, kr, v = qr_ref[...], kr_ref[...], v_ref[...]
    scores = dot_nt(qr, kr) * scale + tiled(bias, heads)
    peak = jnp.max(scores, axis=-1, keepdims=True)
    weight = jnp.exp(scores - peak)
    probs = weight * (1.0 / jnp.sum(weight, axis=-1, keepdims=True))
    loads[0].wait()
    do = heads_to_rows(dot_nt(dat_ref[...], wo_s[...]).astype(BF16), heads, size)
    dv = dot_tn(probs.astype(BF16), do).astype(BF16)
    dp = dot_nt(do, v)
    ds = (probs * (dp - jnp.sum(probs * dp, axis=-1, keepdims=True))).astype(BF16)
    dqr = dot(ds, kr) * scale
    dkr = dot_tn(ds, qr) * scale
    dqn = dqr * cos_all - half_turn(dqr) * sin_all
    dkn = dkr * cos - half_turn(dkr) * sin
    q_unit, q_factor = unit_rows(heads_to_rows(q_ref[...], heads, size))
    k_unit, k_factor = unit_rows(k_ref[...])
    dq, term_query = norm_back(dqn, g_query, q_unit, q_factor)
    dk, term_key = norm_back(dkn, g_key, k_unit, k_factor)
    dq = rows_to_heads(dq.astype(BF16), heads, block)
    dk = dk.astype(BF16)
    dqkv_ref[:, : heads * size] = dq
    dqkv_ref[:, heads * size : (heads + 1) * size] = dk
    dqkv_ref[:, (heads + 1) * size :] = dv
    for load in loads[1:]:
        load.wait()
    part[...] = dot_nt(dq, wq_s[...]) + dot_nt(dk, wk_s[...]) + dot_nt(dv, wv_s[...])
    total = reduce_rows(t, nt, rows, part, outgoing, came, s_sem, r_sem)
    mine = rows_at(t * rows, rows)
    unit, factor = unit_rows(x_ref[source, mine].astype(F32))
    back, term_attn = norm_back(total, g_attn, unit, factor)
    dx = (dh1_ref[...] + back).astype(BF16)
    dxr_ref[...] = dx
    whole[mine] = dx
    wait = spread_rows(t, nt, rows, whole, gs_sem, gr_sem)
    terms_ref[...] = jnp.zeros_like(terms_ref)
    write_terms(terms_ref, 0, term_moe[...])
    write_terms(terms_ref, 8, term_attn)
    terms_ref[16:17, :size] = term_query
    terms_ref[16:17, size : 2 * size] = term_key
    wait()
    dx_ref[...] = whole[...]


def collect_kernel(
    nz, nt, names,
    *refs,
):
    s, z, t = lax.axis_index("section"), lax.axis_index("expert"), lax.axis_index("tensor")
    count = len(names)
    sets = (refs[:count], refs[count : 2 * count])
    outs = refs[2 * count : 3 * count]
    terms_out = refs[3 * count]
    terms_in, terms_near, send, recv, own_sem, near_send, near_recv = refs[3 * count + 1 :]
    other = 1 - s
    i32 = jnp.int32
    peers = [{"section": other}]
    for k in range(1, nz):
        zz = partner(z, i32(k), nz)
        peers += [{"expert": zz}, {"section": other, "expert": zz}]
    peers += [{"tensor": partner(t, i32(j), nt)} for j in range(1, nt)]
    greet(peers)

    jobs = [(d, k, a) for a in range(count) for k in range(nz) for d in range(2)]
    jobs = [(d, k, a) for d, k, a in jobs if k == 0 or names[a][1] != "near"]

    def source_of(layer, k, a):
        src, kind = sets[layer][a], names[a][1]
        if kind == "slice":
            cols = outs[a].shape[-1]
            return src.at[:, rows_at(partner(z, i32(k), nz) * cols, cols)]
        return src

    def target_of(section, origin, a):
        if names[a][1] == "near":
            return outs[a].at[section]
        if names[a][1] == "terms":
            return terms_in.at[section, origin]
        return outs[a].at[section, origin]

    def copy_of(d, k, a, layer):
        section = s if d == 0 else other
        if d == 0 and k == 0:
            return pltpu.make_async_copy(source_of(layer, k, a), target_of(s, z, a), own_sem.at[a])
        return remote(
            source_of(layer, k, a),
            target_of(s, z, a),
            send.at[a, d, k],
            recv.at[a, d, k],
            section=section,
            expert=partner(z, i32(k), nz),
        )

    def arrival_of(d, k, a):
        section = s if d == 0 else other
        zz = partner(z, i32(k), nz)
        return remote(
            source_of(0, k, a),
            target_of(section, zz, a),
            send.at[a, d, k],
            recv.at[a, d, k],
            section=section,
            expert=zz,
        )

    for d, k, a in jobs:

        @pl.when(s == d)
        def _():
            copy_of(d, k, a, 0).start()

        @pl.when(s != d)
        def _():
            copy_of(d, k, a, 1).start()

    for d, k, a in jobs:
        if d == 0 and k == 0:
            copy_of(d, k, a, 0).wait()
        else:
            copy_of(d, k, a, 0).wait_send()
            arrival_of(d, k, a).wait_recv()

    total = None
    for section in range(2):
        for origin in range(nz):
            one = terms_in[section, origin]
            total = one if total is None else total + one
    terms_near[0] = total

    def near(j):
        return remote(
            terms_near.at[0],
            terms_near.at[j],
            near_send.at[j],
            near_recv.at[j],
            tensor=partner(t, i32(j), nt),
        )

    for j in range(1, nt):
        near(j).start()
    for j in range(1, nt):
        near(j).wait_recv()
        total = total + terms_near[j]
    for j in range(1, nt):
        near(j).wait_send()
    terms_out[...] = total


def shape_of(shape, dtype):
    return jax.ShapeDtypeStruct(tuple(shape), dtype)


def params(collective_id):
    return pltpu.CompilerParams(
        collective_id=collective_id, has_side_effects=True, vmem_limit_bytes=VMEM_LIMIT
    )


def block_tables(lengths, block, size):
    ends = jnp.cumsum(lengths)
    starts = ends - lengths
    places = jnp.arange(block, dtype=jnp.int32)
    segment = jnp.sum((places[:, None] >= ends[None, :]).astype(jnp.int32), axis=1)
    numbers = jnp.arange(lengths.shape[0], dtype=jnp.int32)
    offset = jnp.sum(jnp.where(segment[:, None] == numbers[None, :], starts[None, :], 0), axis=1)
    half = jnp.arange(size // 2, dtype=F32)
    inverse = jnp.exp(half * (-2.0 * math.log(THETA) / size))
    angle = (places - offset).astype(F32)[:, None] * inverse[None, :]
    cos, sin = jnp.cos(angle), jnp.sin(angle)
    allowed = (places[None, :] <= places[:, None]) & (segment[:, None] == segment[None, :])
    bias = jnp.where(allowed, 0.0, -1e30).astype(F32)
    return jnp.stack(
        [
            jnp.concatenate([cos, cos], axis=-1),
            jnp.concatenate([-sin, sin], axis=-1),
            bias,
        ]
    )


def on_device(
    boundary, seq_lengths, expert_ids, route_weights, attn_gain, moe_gain, query_gain, key_norm_gain,
    w_query, key_weight, value_weight, w_output, w_gate, w_up, w_down,
):
    nz, nt = lax.axis_size("expert"), lax.axis_size("tensor")
    micro, block, width = boundary.shape[1:]
    size = query_gain.shape[1]
    heads = w_query.shape[2] // size
    local_experts = w_gate.shape[1]
    hidden = local_experts * w_gate.shape[2]
    experts = local_experts * nz
    rows = block // nt
    q_cols = heads * size
    assert micro == 2 and key_weight.shape[2] == size and experts <= LANES
    dma = pltpu.SemaphoreType.DMA

    tabs = jax.vmap(lambda lengths: block_tables(lengths, block, size))(seq_lengths[0, :, 0])
    lanes = jnp.arange(LANES, dtype=jnp.int32)
    gates = jnp.sum(
        jnp.where(expert_ids[0][..., None] == lanes, route_weights[0][..., None], 0.0), axis=2
    )
    wg, wu, wd = (w[0].reshape(hidden, width) for w in (w_gate, w_up, w_down))
    wq, wk, wv, wo = w_query[0], key_weight[0], value_weight[0], w_output[0]

    gains = jnp.concatenate([attn_gain, moe_gain, query_gain, key_norm_gain], axis=1)

    (edges, tabs_all, gates_all, gains_all, wq_all, wk_all, wv_all, wo_all, sg, su, sd) = pl.pallas_call(
        functools.partial(start_kernel, nz, nt),
        out_shape=(
            shape_of((2, block, width), BF16),
            shape_of((2, 3, block, size), F32),
            shape_of((2, nz, block, LANES), F32),
            shape_of((2,) + gains.shape, F32),
            shape_of((2, width, q_cols), BF16),
            shape_of((2, width, size), BF16),
            shape_of((2, width, size), BF16),
            shape_of((2, q_cols, width), BF16),
            shape_of((hidden, width), BF16),
            shape_of((hidden, width), BF16),
            shape_of((hidden, width), BF16),
        ),
        in_specs=[ANY] * 11,
        out_specs=(ANY,) * 11,
        scratch_shapes=[
            dma((8,)), dma((6,)), dma((6,)), dma((2, nz)), dma((2, nz)),
            dma((4, nz)), dma((4, nz)), dma((4, nz)), dma((4, nz)), dma((4, nz)), dma((4, nz)),
        ],
        compiler_params=params(0),
        name="start",
    )(boundary[0], tabs, gates, gains, wq, wk, wv, wo, wg, wu, wd)

    attn_weights = (wq_all, wk_all, wv_all, wo_all)
    expert_weights = (wg, wu, wd, sg, su, sd)
    attn_scratch = [
        pltpu.VMEM((width, q_cols), BF16),
        pltpu.VMEM((width, size), BF16),
        pltpu.VMEM((width, size), BF16),
        pltpu.VMEM((q_cols, width), BF16),
        pltpu.VMEM((block, width), F32),
        pltpu.VMEM((block, width), BF16),
        pltpu.VMEM((nt, rows, width), BF16),
    ]
    expert_scratch = [pltpu.VMEM((hidden, width), BF16)] * 3 + [pltpu.VMEM((nz, block, hidden), F32)] * 2
    own_part = pltpu.VMEM((nz, rows, width), F32)

    def attend(layer, x, source):
        return pl.pallas_call(
            functools.partial(attend_kernel, layer, source, nz, nt, heads),
            out_shape=(
                shape_of((rows, width), F32),
                shape_of((rows, width), BF16),
                shape_of((block, width), BF16),
                shape_of((block, q_cols), F32),
                shape_of((block, size), F32),
                shape_of((block, size), BF16),
                shape_of((heads * block, size), BF16),
                shape_of((block, size), BF16),
                shape_of((block, q_cols), BF16),
            ),
            in_specs=[VM] * 3 + [ANY] * 4,
            out_specs=(VM,) * 9,
            scratch_shapes=attn_scratch + [dma((4,)), dma((nt,)), dma((nt,))],
            compiler_params=params(1 + layer),
            name=f"attend_{layer}",
        )(x, tabs_all, gains_all, *attn_weights)

    def run_experts(layer, b, h1):
        return pl.pallas_call(
            functools.partial(experts_kernel, layer, nz, nt, local_experts),
            out_shape=(
                shape_of((1, block, width), BF16),
                shape_of((nz, block, width), BF16),
                shape_of((nz, block, hidden), F32),
                shape_of((nz, block, hidden), F32),
            ),
            in_specs=[VM] * 3 + [ANY] * 6,
            out_specs=(VM, ANY, ANY, ANY),
            scratch_shapes=expert_scratch
            + [dma((3,)), dma((3,)), own_part]
            + exchange_scratch(nz, nt, rows, block, width),
            compiler_params=params(3 + layer),
            name=f"experts_{layer}",
        )(b, h1, gates_all, *expert_weights)

    def experts_back(layer, dy, h1, gate_pre, up_pre):
        return pl.pallas_call(
            functools.partial(experts_back_kernel, layer, nz, nt, local_experts),
            out_shape=(
                shape_of((block, width), BF16),
                shape_of((rows, width), F32),
                shape_of((1, width), F32),
                shape_of((nz, block, width), BF16),
                shape_of((nz, block, hidden), BF16),
                shape_of((nz, block, hidden), BF16),
                shape_of((nz, block, hidden), BF16),
            ),
            in_specs=[VM] * 4 + [ANY] * 8,
            out_specs=(VM, VM, VM, ANY, ANY, ANY, ANY),
            scratch_shapes=expert_scratch[:3]
            + [pltpu.VMEM((2, block, hidden), F32)] * 2
            + [pltpu.VMEM((nz, block, hidden), BF16)] * 3
            + [dma((3,)), dma((2,)), dma((2,)), dma((4,)), own_part]
            + exchange_scratch(nz, nt, rows, block, width),
            compiler_params=params(5 + layer),
            name=f"experts_back_{layer}",
        )(dy, h1, gains_all, gates_all, gate_pre, up_pre, *expert_weights)

    def attend_back(layer, x, source, dat, dh1, term_moe, q, k, v, qr, kr):
        return pl.pallas_call(
            functools.partial(attend_back_kernel, layer, source, nz, nt, heads),
            out_shape=(
                shape_of((rows, width), BF16),
                shape_of((block, width), BF16),
                shape_of((block, q_cols + 2 * size), BF16),
                shape_of((TERM_ROWS, TERM_COLS), F32),
            ),
            in_specs=[VM] * 11 + [ANY] * 4,
            out_specs=(VM,) * 4,
            scratch_shapes=attn_scratch
            + [pltpu.VMEM((block, width), BF16)]
            + [dma((4,)), dma((nt,)), dma((nt,)), dma((nt,)), dma((nt,))],
            compiler_params=params(7 + layer),
            name=f"attend_back_{layer}",
        )(x, tabs_all, gains_all, dat, dh1, term_moe, q, k, v, qr, kr, *attn_weights)

    h1_0, b_0, a_0, q_0, k_0, v_0, qr_0, kr_0, o_0 = attend(0, edges, 0)
    x_1, ball_0, gp_0, up_0 = run_experts(0, b_0, h1_0)
    h1_1, b_1, a_1, q_1, k_1, v_1, qr_1, kr_1, o_1 = attend(1, x_1, 0)
    y_1, ball_1, gp_1, up_1 = run_experts(1, b_1, h1_1)

    dy_1 = lax.dynamic_slice_in_dim(edges[1], lax.axis_index("tensor") * rows, rows, 0)
    dat_1, dh1_1, tm_1, dyall_1, hid_1, dg_1, du_1 = experts_back(1, dy_1, h1_1, gp_1, up_1)
    dxr_1, _, dqkv_1, terms_1 = attend_back(
        1, x_1, 0, dat_1, dh1_1, tm_1, q_1, k_1, v_1, qr_1, kr_1
    )
    dat_0, dh1_0, tm_0, dyall_0, hid_0, dg_0, du_0 = experts_back(0, dxr_1, h1_0, gp_0, up_0)
    _, dx_0, dqkv_0, terms_0 = attend_back(
        0, edges, 0, dat_0, dh1_0, tm_0, q_0, k_0, v_0, qr_0, kr_0
    )

    set_0 = (ball_0, dyall_0, hid_0, dg_0, du_0, dx_0, a_0, o_0, dat_0, dqkv_0, terms_0)
    set_1 = (ball_1, dyall_1, hid_1, dg_1, du_1, y_1[0], a_1, o_1, dat_1, dqkv_1, terms_1)
    kinds = ("near",) * 6 + ("slice", "whole", "slice", "whole", "terms")
    names = tuple((str(i), kind) for i, kind in enumerate(kinds))
    out_shapes = []
    for kind, value in zip(kinds, set_0):
        if kind == "near":
            out_shapes.append(shape_of((2,) + value.shape, value.dtype))
        elif kind == "slice":
            out_shapes.append(shape_of((2, nz, block, width // nz), value.dtype))
        elif kind == "whole":
            out_shapes.append(shape_of((2, nz) + value.shape, value.dtype))
        else:
            out_shapes.append(shape_of((8, LANES), F32))
    out_shapes.append(shape_of((TERM_ROWS, TERM_COLS), F32))
    count = len(kinds)
    collected = pl.pallas_call(
        functools.partial(collect_kernel, nz, nt, names),
        out_shape=tuple(out_shapes),
        in_specs=[ANY] * (2 * count),
        out_specs=(ANY,) * count + (VM,),
        scratch_shapes=[
            pltpu.VMEM((2, nz, TERM_ROWS, TERM_COLS), F32),
            pltpu.VMEM((nt, TERM_ROWS, TERM_COLS), F32),
            dma((count, 2, nz)),
            dma((count, 2, nz)),
            dma((count,)),
            dma((nt,)),
            dma((nt,)),
        ],
        compiler_params=params(9),
        name="collect",
    )(*set_0, *set_1)
    (b_all, dy_all, hid, dg, du, ends, a_all, o_all, dat_all, dqkv_all, _, terms) = collected

    def flat(value):
        return value.reshape(-1, value.shape[-1])

    def weight_grad(left, right):
        return lax.dot_general(
            flat(left), flat(right), (((0,), (0,)), ((), ())), preferred_element_type=F32
        )

    def expert_grad(left, right):
        return weight_grad(left, right).reshape(w_gate.shape)

    dqkv_all = flat(dqkv_all)
    a_all = flat(a_all)
    grad_query = weight_grad(a_all, dqkv_all[:, :q_cols])
    grad_key = weight_grad(a_all, dqkv_all[:, q_cols : q_cols + size])
    grad_value = weight_grad(a_all, dqkv_all[:, q_cols + size :])
    return (
        ends[None],
        terms[8:16].reshape(1, width),
        terms[:8].reshape(1, width),
        terms[16:17, :size],
        terms[16:17, size : 2 * size],
        grad_query[None],
        grad_key[None],
        grad_value[None],
        weight_grad(o_all, dat_all)[None],
        expert_grad(dg, b_all),
        expert_grad(du, b_all),
        expert_grad(hid, dy_all),
    )


def solution(mesh):
    return jax.shard_map(
        on_device,
        mesh=mesh,
        in_specs=(
            P("section", None, "expert", None),
            P("section", None, "expert", None),
            P("section", None, "expert", None),
            P("section", None, "expert", None),
            P("section", None),
            P("section", None),
            P("section", None),
            P("section", None),
            P("section", "expert", "tensor"),
            P("section", "expert", "tensor"),
            P("section", "expert", "tensor"),
            P("section", "tensor", "expert"),
            P("section", "expert", "tensor", None),
            P("section", "expert", "tensor", None),
            P("section", "expert", "tensor", None),
        ),
        out_specs=(
            P("section", None, "expert", None),
            P("section", None),
            P("section", None),
            P("section", None),
            P("section", None),
            P("section", "expert", "tensor"),
            P("section", "expert", "tensor"),
            P("section", "expert", "tensor"),
            P("section", "tensor", "expert"),
            P("section", "expert", "tensor", None),
            P("section", "expert", "tensor", None),
            P("section", "expert", "tensor", None),
        ),
        check_vma=False,
    )
```

time: 3040 us -> 820 us (0.27)
  waiting for transfers between devices: 1330 us -> 0 us
  blocking collectives: 838 us -> 0 us
  Pallas kernels: 0 us -> 763 us
  local copies, waits for them, and re-layouts: 316 us -> 12.4 us
  other arithmetic: 234 us -> 6.03 us
  matrix products: 245 us -> 30.2 us
  starting transfers between devices: 47 us -> 0 us
    pallas_call x0 -> x10, Pallas kernels: none -> 763 us  [the longest x1 249 us: on_device(): pl.pallas_call(functools.partial(collect_kernel, nz, nt, names), out_shap...]
    all_to_all x7 -> x0, waiting for transfers between devices: 748 us -> none  [the longest x3 358 us: on_device(): lax.all_to_all(partial_out.astype(jnp.bfloat16), 'expert', split_axis=0,...]
    all_to_all x5 -> x0, blocking collectives: 715 us -> none  [the longest x2 288 us: on_device(): lax.all_to_all(grad_send, 'expert', split_axis=0, concat_axis=0, tiled=True)]
    psum x11 -> x0, waiting for transfers between devices: 413 us -> none  [the longest x3 128 us: on_device(): lax.psum(jnp.dot(forward_heads_low, full_output, preferred_element_type=j...]
    dot_general x81 -> x7, matrix products: 245 us -> 30.2 us  [weight_grad(): lax.dot_general(flat(left), flat(right), (((0,), (0,)), ((), ())), prefer...]
    gather x15 -> x0, local copies, waits for them, and re-layouts: 189 us -> none  [the longest x3 41.5 us: on_device(): slot_grad = jnp.take(grad_padded, slot_table // top_count, axis=0)]
    all_gather x2 -> x0, waiting for transfers between devices: 106 us -> none  [the longest x1 68.5 us: on_device(): lax.all_gather(w_output[0], 'expert', axis=1, tiled=True)]
    psum x1 -> x0, blocking collectives: 79.1 us -> none  [on_device(): lax.psum((totals[0], totals[1], totals[2], totals[3]), ('expert', 'tensor'))]
  transfers between devices with their start and end apart: 28 -> 0, of which waited for: 20 -> 0; matrix products, arithmetic and copies ran while one was open for 11% -> 0% of each run, Pallas kernels for 0% -> 0%
where the time goes in v1:
time: 820 us; the launch traced here: 813 us
  Pallas kernels  763 us (93%)
  matrix products  30.2 us (4%)
  local copies, waits for them, and re-layouts  12.4 us (2%)
    pallas_call x1, Pallas kernels, on_device(): pl.pallas_call(functools.partial(collect_kernel, nz, nt, names), out_shap...  249 us
    pallas_call x1, Pallas kernels, on_device(): pl.pallas_call(functools.partial(start_kernel, nz, nt), out_shape=(shape_...  171 us
    pallas_call x2, Pallas kernels, run_experts(): pl.pallas_call(functools.partial(experts_kernel, layer, nz, nt, local_exp...  134 us
    pallas_call x2, Pallas kernels, experts_back(): pl.pallas_call(functools.partial(experts_back_kernel, layer, nz, nt, loca...  129 us
    pallas_call x2, Pallas kernels, attend_back(): pl.pallas_call(functools.partial(attend_back_kernel, layer, source, nz, n...  48.4 us
    pallas_call x2, Pallas kernels, attend(): pl.pallas_call(functools.partial(attend_kernel, layer, source, nz, nt, he...  31.6 us
    dot_general x7, matrix products, weight_grad(): lax.dot_general(flat(left), flat(right), (((0,), (0,)), ((), ())), prefer...  30.2 us

profile of v1, /device:TPU:0, one launch (start us, length us, event | category | flops | bytes accessed | tf_op | source)
XLA Modules:
  0.0 812.9 jit_solution(13858639873762514045)
XLA Ops:
  0.7 0.9 reduce_window_sum.11
  1.6 0.7 sub.20
  2.4 1.4 pad_maximum_fusion.gains
  3.9 0.8 copy.35
  4.7 0.8 copy.36
  5.5 1.4 select_reduce_fusion.gates
  7.6 0.8 maximum_bitcast_fusion.tabs
  8.4 170.9 %start.1 = (bf16[2,128,2048]{2,1,0:T(8,128)(2,1)}, f32[2,3,128,128]{3,2,1,0:T(8,128)}, f32[2,4,128,128]{3,2,1,0:T(8,128)}, f32[2,1,4352]{2,1,0:T(1,128)}, bf16[2...) custom-call(bf16[2,128,2048]{2,1,0:T(8,128)(2,1)} %bitcast.108, ...), custom_call_target="tpu_custom_call" | custom-call | tf_op jit(solution)/shard_map/start/pallas_call | solution.py:901
  179.3 1.1 slice.24
  181.0 17.3 %attend_0.1 = (f32[32,2048]{1,0:T(8,128)}, bf16[32,2048]{1,0:T(8,128)(2,1)}, bf16[128,2048]{1,0:T(8,128)(2,1)}, f32[128,1024]{1,0:T(8,128)}, f32[128,128]{1,0:T(...) custom-call(bf16[2,128,2048]{2,1,0:T(8,128)(2,1)} %get-tuple-element, ...), custom_call_target="tpu_custom_call" | custom-call | tf_op jit(solution)/shard_map/attend_0/pallas_call | solution.py:941
  198.3 65.7 %experts_0.1 = (bf16[1,128,2048]{2,1,0:T(8,128)(2,1)}, bf16[4,128,2048]{2,1,0:T(8,128)(2,1)}, f32[4,128,768]{2,1,0:T(8,128)}, f32[4,128,768]{2,1,0:T(8,128)}) custom-call(bf16[32,2048]{1,0:T(8,128)(2,1)} %get-tuple-element.87.b_ref, f32[32,2048]{1,0:T(8,128)} %get-tuple-element.88.h1_ref, f32[2,4,128,128]{3,2,1,0:T(8,128)} %get-tuple-element.89.gates, ...), custom_call_target="tpu_custom_call" | custom-call | tf_op jit(solution)/shard_map/experts_0/pallas_call | solution.py:962
  264.0 14.3 %attend_1.1 = (f32[32,2048]{1,0:T(8,128)}, bf16[32,2048]{1,0:T(8,128)(2,1)}, bf16[128,2048]{1,0:T(8,128)(2,1)}, f32[128,1024]{1,0:T(8,128)}, f32[128,128]{1,0:T(...) custom-call(bf16[1,128,2048]{2,1,0:T(8,128)(2,1)} %get-tuple-element, ...), custom_call_target="tpu_custom_call" | custom-call | tf_op jit(solution)/shard_map/attend_1/pallas_call | solution.py:941
  278.3 68.4 %experts_1.1 = (bf16[1,128,2048]{2,1,0:T(8,128)(2,1)}, bf16[4,128,2048]{2,1,0:T(8,128)(2,1)}, f32[4,128,768]{2,1,0:T(8,128)}, f32[4,128,768]{2,1,0:T(8,128)}) custom-call(bf16[32,2048]{1,0:T(8,128)(2,1)} %get-tuple-element.96.b_ref, f32[32,2048]{1,0:T(8,128)} %get-tuple-element.95.h1_ref, f32[2,4,128,128]{3,2,1,0:T(8,128)} %get-tuple-element.89.gates, ...), custom_call_target="tpu_custom_call" | custom-call | tf_op jit(solution)/shard_map/experts_1/pallas_call | solution.py:962
  346.8 63.9 %experts_back_1.1 = (bf16[128,2048]{1,0:T(8,128)(2,1)}, f32[32,2048]{1,0:T(8,128)}, f32[1,2048]{1,0:T(1,128)}, bf16[4,128,2048]{2,1,0:T(8,128)(2,1)}, bf16[4,128...) custom-call(bf16[32,2048]{1,0:T(8,128)(2,1)} %dynamic-slice_bitcast_fusion.dy_ref, ...), custom_call_target="tpu_custom_call" | custom-call | tf_op jit(solution)/shard_map/experts_back_1/pallas_call | solution.py:980
  410.6 26.2 %attend_back_1.1 = (bf16[32,2048]{1,0:T(8,128)(2,1)}, bf16[128,2048]{1,0:T(8,128)(2,1)}, bf16[128,1280]{1,0:T(8,128)(2,1)}, f32[24,256]{1,0:T(8,128)}) custom-call(bf16[1,128,2048]{2,1,0:T(8,128)(2,1)} %get-tuple-element.94.x_ref, f32[2,3,128,128]{3,2,1,0:T(8,128)} %get-tuple-element.81.tabs, f32[2,1,4352]{2,1,0:T(1,128)} %get-tuple-element.82.gains, ...), custom_call_target="tpu_custom_call" | custom-call | tf_op jit(solution)/shard_map/attend_back_1/pallas_call | solution.py:1003
  436.9 65.0 %experts_back_0.1 = (bf16[128,2048]{1,0:T(8,128)(2,1)}, f32[32,2048]{1,0:T(8,128)}, f32[1,2048]{1,0:T(1,128)}, bf16[4,128,2048]{2,1,0:T(8,128)(2,1)}, bf16[4,128...) custom-call(bf16[32,2048]{1,0:T(8,128)(2,1)} %get-tuple-element.107.dy_ref, ...), custom_call_target="tpu_custom_call" | custom-call | tf_op jit(solution)/shard_map/experts_back_0/pallas_call | solution.py:980
  501.8 22.1 %attend_back_0.1 = (bf16[32,2048]{1,0:T(8,128)(2,1)}, bf16[128,2048]{1,0:T(8,128)(2,1)}, bf16[128,1280]{1,0:T(8,128)(2,1)}, f32[24,256]{1,0:T(8,128)}) custom-call(bf16[2,128,2048]{2,1,0:T(8,128)(2,1)} %get-tuple-element.80.x_ref, f32[2,3,128,128]{3,2,1,0:T(8,128)} %get-tuple-element.81.tabs, f32[2,1,4352]{2,1,0:T(1,128)} %get-tuple-element.82.gains, ...), custom_call_target="tpu_custom_call" | custom-call | tf_op jit(solution)/shard_map/attend_back_0/pallas_call | solution.py:1003
  524.0 249.5 %collect.1 = (bf16[2,4,128,2048]{3,2,1,0:T(8,128)(2,1)}, bf16[2,4,128,2048]{3,2,1,0:T(8,128)(2,1)}, bf16[2,4,128,768]{3,2,1,0:T(8,128)(2,1)}, bf16[2,4,128,768]{...) custom-call(bf16[4,128,2048]{2,1,0:T(8,128)(2,1)} %get-tuple-element, ...), custom_call_target="tpu_custom_call" | custom-call | tf_op jit(solution)/shard_map/collect/pallas_call | solution.py:1051
  773.5 1.3 fusion.8
  774.7 0.7 slice_bitcast_fusion
  776.7 2.4 convolution_bitcast_fusion.4
  779.1 2.4 convolution_bitcast_fusion.5
  781.6 4.3 fusion.2
  785.9 1.6 copy.38
  787.5 1.6 copy.39
  789.1 0.7 copy.40
  789.9 7.8 convolution_bitcast_fusion
  797.8 2.6 convolution_bitcast_fusion.3
  800.4 0.8 copy-done.7
  801.2 5.3 convolution_bitcast_fusion.1
  806.5 5.3 convolution_bitcast_fusion.2
  811.7 1.0 copy.46
  (30 shorter events, 2.9 us)
Async XLA Ops:
  773.4 8.1 copy-start
  781.6 4.3 copy-start.3
  785.9 1.6 copy-start.2
  787.5 1.6 copy-start.1
  789.9 7.8 copy-start.8
  789.9 7.8 copy-start.9
  797.8 2.6 copy-start.5
  797.8 3.4 copy-start.7
  801.2 5.3 copy-start.4
  806.5 5.3 copy-start.6

commit v2 on v1

v2 whole, which is shorter than its diff:
```python
import functools
import math

import jax
import jax.numpy as jnp
from jax import lax
from jax.experimental import pallas as pl
from jax.experimental.pallas import tpu as pltpu
from jax.sharding import PartitionSpec as P

EPSILON = 1e-06
THETA = 1000000.0
LANES = 128
TERM_ROWS = 24
TERM_COLS = 256
MESH = pl.DeviceIdType.MESH
F32 = jnp.float32
BF16 = jnp.bfloat16
VMEM_LIMIT = 60 * 1024 * 1024

ANY = pl.BlockSpec(memory_space=pl.ANY)
VM = pl.BlockSpec(memory_space=pltpu.VMEM)


def partner(index, k, count):
    out, bit = 0, 1
    while bit < count:
        out = out + bit * lax.rem(lax.div(index, bit) + lax.div(k, bit), 2)
        bit *= 2
    return out


def rows_at(start, size):
    return pl.ds(pl.multiple_of(start, size), size)


def remote(src, dst, send_sem, recv_sem, **where):
    return pltpu.make_async_remote_copy(
        src_ref=src,
        dst_ref=dst,
        send_sem=send_sem,
        recv_sem=recv_sem,
        device_id=where,
        device_id_type=MESH,
    )


def greet(peers):
    barrier = pltpu.get_barrier_semaphore()
    for where in peers:
        pl.semaphore_signal(barrier, inc=1, device_id=where, device_id_type=MESH)
    pl.semaphore_wait(barrier, len(peers))


def layer_peers(z, t, nz, nt):
    i32 = jnp.int32
    peers = [{"expert": partner(z, i32(k), nz)} for k in range(1, nz)]
    peers += [{"tensor": partner(t, i32(k), nt)} for k in range(1, nt)]
    return peers


def dot(a, b):
    return lax.dot_general(a, b, (((1,), (0,)), ((), ())), preferred_element_type=F32)


def dot_nt(a, b):
    return lax.dot_general(a, b, (((1,), (1,)), ((), ())), preferred_element_type=F32)


def dot_tn(a, b):
    return lax.dot_general(a, b, (((0,), (0,)), ((), ())), preferred_element_type=F32)


def unit_rows(value):
    factor = lax.rsqrt(jnp.mean(value * value, axis=-1, keepdims=True) + EPSILON)
    return value * factor, factor


def norm_back(grad, gain, unit, factor):
    weighted = grad * gain
    inner = jnp.mean(weighted * unit, axis=-1, keepdims=True)
    return factor * (weighted - unit * inner), jnp.sum(grad * unit, axis=0, keepdims=True)


def expert_gates(gate_rows, first_expert, local_experts, width):
    rows = gate_rows.shape[0]
    lane = lax.broadcasted_iota(jnp.int32, gate_rows.shape, 1)
    column = lax.broadcasted_iota(jnp.int32, (rows, local_experts * width), 1)
    out = None
    for e in range(local_experts):
        one = jnp.sum(jnp.where(lane == first_expert + e, gate_rows, 0.0), axis=1, keepdims=True)
        wide = jnp.broadcast_to(one, column.shape)
        out = wide if out is None else jnp.where(column >= e * width, wide, out)
    return out


def write_terms(terms_ref, row, vector):
    for i in range(vector.shape[1] // TERM_COLS):
        terms_ref[row + i : row + i + 1, :] = vector[:, i * TERM_COLS : (i + 1) * TERM_COLS]


def exchange_sems(nz, nt):
    dma = pltpu.SemaphoreType.DMA
    return [dma((nz,)), dma((nz,)), dma((nz, nt)), dma((nz, nt))] * 2 + [dma((nt,)), dma((nt,))]


def exchange_scratch(nz, nt, rows, block, width):
    return [
        pltpu.VMEM((nz, block, width), BF16),
        pltpu.VMEM((nz, block, width), BF16),
        pltpu.VMEM((block, width), F32),
        pltpu.VMEM((nz, nt, rows, width), BF16),
        pltpu.VMEM((nz, rows, width), BF16),
        pltpu.VMEM((nz, rows, width), BF16),
        pltpu.VMEM((rows, width), F32),
        pltpu.VMEM((block, width), BF16),
    ] + exchange_sems(nz, nt)


def exchange(z, t, nz, nt, rows, own_rows, scratch, ready, work, moves):
    (full, outgoing, part, came_near, passed, came_far, total, _) = scratch[:8]
    (gz_send, gz_recv, gt_send, gt_recv, rz_send, rz_recv, rt_send, rt_recv) = scratch[8:16]
    i32 = jnp.int32
    mine = rows_at(t * rows, rows)

    def far_copy(k):
        return remote(
            full.at[z, mine],
            full.at[z, mine],
            gz_send.at[k],
            gz_recv.at[k],
            expert=partner(z, i32(k), nz),
        )

    def near_copy(k, source, j):
        return remote(
            full.at[source, mine],
            full.at[source, mine],
            gt_send.at[k, j],
            gt_recv.at[k, j],
            tensor=partner(t, i32(j), nt),
        )

    def near_arrival(k, source, j):
        theirs = rows_at(partner(t, i32(j), nt) * rows, rows)
        return remote(
            full.at[source, theirs],
            full.at[source, theirs],
            gt_send.at[k, j],
            gt_recv.at[k, j],
            tensor=partner(t, i32(j), nt),
        )

    def far_arrival(k):
        source = partner(z, i32(k), nz)
        return remote(
            full.at[source, mine],
            full.at[source, mine],
            gz_send.at[k],
            gz_recv.at[k],
            expert=source,
        )

    def part_copy(k, j):
        peer = partner(t, i32(j), nt)
        return remote(
            outgoing.at[k, rows_at(peer * rows, rows)],
            came_near.at[k, j],
            rt_send.at[k, j],
            rt_recv.at[k, j],
            tensor=peer,
        )

    def sum_copy(k):
        return remote(
            passed.at[k],
            came_far.at[k],
            rz_send.at[k],
            rz_recv.at[k],
            expert=partner(z, k, nz),
        )

    full[z, mine] = own_rows
    for k in range(1, nz):
        far_copy(k).start()
    for j in range(1, nt):
        near_copy(0, z, j).start()
    for move in moves:
        move.start()

    ready()

    def produce(k, source):
        for j in range(1, nt):
            near_arrival(k, source, j).wait_recv()
        part[...] = work(k, source, full[source])
        outgoing[k] = part[...].astype(BF16)
        for j in range(1, nt):
            part_copy(k, j).start()
        return part[mine]

    def collect(k):
        out = passed_own[k]
        for j in range(1, nt):
            part_copy(k, j).wait_recv()
            out = out + came_near[k, j].astype(F32)
        return out

    passed_own = scratch[18]
    passed_own[0] = produce(i32(0), z)
    for k in range(1, nz):
        far_arrival(k).wait_recv()
        for j in range(1, nt):
            near_copy(k, partner(z, i32(k), nz), j).start()

    def step(k, carry):
        passed_own[k] = produce(k, partner(z, k, nz))

        @pl.when(k >= 2)
        def _():
            passed[k - 1] = collect(k - 1).astype(BF16)
            sum_copy(k - 1).start()

        return carry

    lax.fori_loop(1, nz, step, 0)
    for move in moves:
        move.poll(1)
    passed[nz - 1] = collect(nz - 1).astype(BF16)
    sum_copy(i32(nz - 1)).start()
    for move in moves:
        move.poll(2)
    total[...] = collect(0)
    for k in range(1, nz):
        sum_copy(i32(k)).wait_recv()
        total[...] += came_far[k].astype(F32)

    def finish():
        for k in range(1, nz):
            far_copy(k).wait_send()
            sum_copy(i32(k)).wait_send()
        for k in range(nz):
            source = partner(z, i32(k), nz)
            for j in range(1, nt):
                near_copy(k, source, j).wait_send()
                part_copy(k, j).wait_send()

    return finish


def spread_rows(t, nt, rows, block_ref, send_sem, recv_sem):
    i32 = jnp.int32
    mine = rows_at(t * rows, rows)
    for j in range(1, nt):
        remote(
            block_ref.at[mine],
            block_ref.at[mine],
            send_sem.at[j],
            recv_sem.at[j],
            tensor=partner(t, i32(j), nt),
        ).start()

    def wait():
        for j in range(1, nt):
            peer = partner(t, i32(j), nt)
            theirs = rows_at(peer * rows, rows)
            copy = remote(
                block_ref.at[theirs],
                block_ref.at[theirs],
                send_sem.at[j],
                recv_sem.at[j],
                tensor=peer,
            )
            copy.wait_send()
            copy.wait_recv()

    return wait


def reduce_rows(t, nt, rows, part, outgoing, came, send_sem, recv_sem):
    i32 = jnp.int32
    outgoing[...] = part[...].astype(BF16)

    def copy(j):
        peer = partner(t, i32(j), nt)
        return remote(
            outgoing.at[rows_at(peer * rows, rows)],
            came.at[j],
            send_sem.at[j],
            recv_sem.at[j],
            tensor=peer,
        )

    for j in range(1, nt):
        copy(j).start()
    total = part[rows_at(t * rows, rows)]
    for j in range(1, nt):
        copy(j).wait_recv()
        total = total + came[j].astype(F32)
    for j in range(1, nt):
        copy(j).wait_send()
    return total


def all_peers(s, z, t, nz, nt):
    i32 = jnp.int32
    peers = [{"section": 1 - s}]
    for k in range(1, nz):
        zz = partner(z, i32(k), nz)
        peers += [{"expert": zz}, {"section": 1 - s, "expert": zz}]
    return peers + [{"tensor": partner(t, i32(j), nt)} for j in range(1, nt)]


class Relay:
    def __init__(self, layer, spots, nz):
        self.layer, self.spots, self.nz = layer, spots, nz

    def scratch(self, count):
        dma = pltpu.SemaphoreType.DMA
        return [dma((count,))] + [dma((count, self.nz))] * 6

    def bind(self, shards, outs, sems):
        self.s, self.z = lax.axis_index("section"), lax.axis_index("expert")
        self.shards, self.outs, self.sems = shards, outs, sems
        self.source = self.s == self.layer
        self.count = len(shards)
        return self

    def place(self, a, owner):
        dim = self.spots[a]
        size = self.shards[a].shape[dim]
        window = rows_at(owner * size, size)
        return self.outs[a].at[window] if dim == 0 else self.outs[a].at[:, window]

    def home(self, a):
        return pltpu.make_async_copy(self.shards[a], self.place(a, self.z), self.sems[0].at[a])

    def hop(self, a, owner, step, right, own=False):
        spot = self.place(a, owner)
        send, recv = self.sems[1:3] if right else self.sems[3:5]
        return remote(
            self.shards[a] if own else spot,
            spot,
            send.at[a, step],
            recv.at[a, step],
            expert=self.z + 1 if right else self.z - 1,
        )

    def hand(self, a, owner, own=False):
        spot = self.place(a, owner)
        return remote(
            self.shards[a] if own else spot,
            spot,
            self.sems[5].at[a, owner],
            self.sems[6].at[a, owner],
            section=1 - self.s,
        )

    def begin_side(self, a, right):
        @pl.when(self.source & ((self.z + 1 < self.nz) if right else (self.z >= 1)))
        def _():
            self.hop(a, self.z, 1, right, True).start()

    def begin_home(self, a):
        @pl.when(self.source)
        def _():
            self.home(a).start()
            self.hand(a, self.z, True).start()

    def begin(self, a):
        self.begin_side(a, True)
        self.begin_side(a, False)
        self.begin_home(a)

    def step(self, a, k):
        z, nz = self.z, self.nz

        @pl.when(self.source & (z >= k))
        def _():
            self.hop(a, z - k, k, True).wait_recv()

            @pl.when(z + 1 < nz)
            def _():
                self.hop(a, z - k, k + 1, True).start()

            self.hand(a, z - k).start()

        @pl.when(self.source & (z + k < nz))
        def _():
            self.hop(a, z + k, k, False).wait_recv()

            @pl.when(z >= 1)
            def _():
                self.hop(a, z + k, k + 1, False).start()

            self.hand(a, z + k).start()

    def settle(self, a):
        @pl.when(self.source)
        def _():
            self.home(a).wait()

        @pl.when(jnp.logical_not(self.source))
        def _():
            for owner in range(self.nz):
                self.hand(a, owner).wait_recv()

    def end(self, a):
        z, nz = self.z, self.nz

        @pl.when(self.source)
        def _():
            for owner in range(nz):
                self.hand(a, owner).wait_send()
            for step in range(1, nz):

                @pl.when((z >= step - 1) & (z + 1 < nz))
                def _():
                    self.hop(a, z - (step - 1), step, True).wait_send()

                @pl.when((z + step - 1 < nz) & (z >= 1))
                def _():
                    self.hop(a, z + (step - 1), step, False).wait_send()

    def start(self):
        for a in range(self.count):
            self.begin(a)

    def poll(self, turn):
        if turn < self.nz - 1:
            for a in range(self.count):
                self.step(a, turn)

    def finish(self):
        for k in range(min(3, self.nz - 1), self.nz):
            for a in range(self.count):
                self.step(a, k)
        for a in range(self.count):
            self.settle(a)
            self.end(a)


class Gather:
    def __init__(self, layer, nz, sliced=False):
        self.layer, self.nz, self.sliced = layer, nz, sliced

    def scratch(self):
        dma = pltpu.SemaphoreType.DMA
        return [dma((1,)), dma((self.nz,)), dma((2, self.nz))]

    def bind(self, src, out, sems):
        self.s, self.z = lax.axis_index("section"), lax.axis_index("expert")
        self.src, self.out, self.sems = src, out, sems
        return self

    def copy(self, k, local, section=None, origin=None):
        zz = partner(self.z, jnp.int32(k), self.nz)
        src = self.src
        if self.sliced:
            cols = self.out.shape[-1]
            src = src.at[:, rows_at(zz * cols, cols)]
        section = self.s if section is None else section
        spot = self.out.at[section, self.z if origin is None else origin]
        if local:
            return pltpu.make_async_copy(src, spot, self.sems[0].at[0])
        return remote(
            src,
            spot,
            self.sems[1].at[k],
            self.sems[2].at[section, k],
            section=jnp.int32(self.layer),
            expert=zz,
        )

    def start(self):
        for k in range(1, self.nz):
            self.copy(k, False).start()

        @pl.when(self.s == self.layer)
        def _():
            self.copy(0, True).start()

        @pl.when(self.s != self.layer)
        def _():
            self.copy(0, False).start()

    def poll(self, turn):
        pass

    def arrive(self):
        @pl.when(self.s == self.layer)
        def _():
            self.copy(0, True).wait()
            for section in range(2):
                for k in range(self.nz):
                    if k or section != self.layer:
                        zz = partner(self.z, jnp.int32(k), self.nz)
                        self.copy(k, False, section, zz).wait_recv()

    def leave(self):
        for k in range(1, self.nz):
            self.copy(k, False).wait_send()

        @pl.when(self.s != self.layer)
        def _():
            self.copy(0, False).wait_send()

    def finish(self):
        self.arrive()
        self.leave()


class Near:
    def __init__(self, layer, both=False):
        self.layer, self.both = layer, both

    def scratch(self):
        dma = pltpu.SemaphoreType.DMA
        return [dma((1,)), dma((1,)), dma((1,))]

    def bind(self, src, out, sems):
        self.s, self.src, self.out, self.sems = lax.axis_index("section"), src, out, sems
        return self

    def local(self):
        return pltpu.make_async_copy(self.src, self.out.at[self.layer], self.sems[0].at[0])

    def copy(self):
        return remote(
            self.src,
            self.out.at[1 - self.layer] if self.both else self.out,
            self.sems[1].at[0],
            self.sems[2].at[0],
            section=jnp.int32(self.layer),
        )

    def start(self):
        if self.both:

            @pl.when(self.s == self.layer)
            def _():
                self.local().start()

        @pl.when(self.s != self.layer)
        def _():
            self.copy().start()

    def poll(self, turn):
        pass

    def finish(self):
        @pl.when(self.s == self.layer)
        def _():
            if self.both:
                self.local().wait()
            remote(
                self.src,
                self.out.at[1 - self.layer] if self.both else self.out,
                self.sems[1].at[0],
                self.sems[2].at[0],
                section=1 - self.s,
            ).wait_recv()

        @pl.when(self.s != self.layer)
        def _():
            self.copy().wait_send()


def heads_to_rows(value, heads, size):
    return jnp.concatenate([value[:, h * size : (h + 1) * size] for h in range(heads)], axis=0)


def rows_to_heads(value, heads, block):
    return jnp.concatenate([value[h * block : (h + 1) * block] for h in range(heads)], axis=1)


def split_gains(row, width, size):
    return (
        row[:, :width],
        row[:, width : 2 * width],
        row[:, 2 * width : 2 * width + size],
        row[:, 2 * width + size :],
    )


def tiled(value, times):
    return jnp.concatenate([value] * times, axis=0)


def half_turn(value):
    return pltpu.roll(value, value.shape[-1] // 2, value.ndim - 1)


def attend_body(t, nt, heads, x_ref, tables, gains, outs, scratch, wait_qkv, wait_out):
    (h1_ref, b_ref, a_ref, q_ref, k_ref, v_ref, qr_ref, kr_ref, o_ref) = outs
    (wq_s, wk_s, wv_s, wo_s, part, outgoing, came, s_sem, r_sem) = scratch
    block, width = x_ref.shape
    rows = block // nt
    cos, sin, bias = tables
    size = cos.shape[-1]
    g_attn, g_moe, g_query, g_key = split_gains(gains, width, size)
    unit, _ = unit_rows(x_ref[...].astype(F32))
    a_ref[...] = (unit * g_attn).astype(BF16)
    wait_qkv()
    q = dot(a_ref[...], wq_s[...])
    q_ref[...] = q
    k = dot(a_ref[...], wk_s[...])
    k_ref[...] = k
    v = dot(a_ref[...], wv_s[...]).astype(BF16)
    v_ref[...] = v
    qn = unit_rows(heads_to_rows(q, heads, size))[0] * g_query
    kn = unit_rows(k)[0] * g_key
    qr = (qn * tiled(cos, heads) + half_turn(qn) * tiled(sin, heads)).astype(BF16)
    kr = (kn * cos + half_turn(kn) * sin).astype(BF16)
    qr_ref[...] = qr
    kr_ref[...] = kr
    scores = dot_nt(qr, kr) * (1.0 / math.sqrt(size)) + tiled(bias, heads)
    peak = jnp.max(scores, axis=-1, keepdims=True)
    weight = jnp.exp(scores - peak)
    probs = weight * (1.0 / jnp.sum(weight, axis=-1, keepdims=True))
    o = dot(probs.astype(BF16), v).astype(BF16)
    o_ref[...] = rows_to_heads(o, heads, block)
    wait_out()
    part[...] = dot(o_ref[...], wo_s[...])
    total = reduce_rows(t, nt, rows, part, outgoing, came, s_sem, r_sem)
    h1 = x_ref[rows_at(t * rows, rows)].astype(F32) + total
    h1_ref[...] = h1
    b_ref[...] = (unit_rows(h1)[0] * g_moe).astype(BF16)


def start_attend_kernel(nz, nt, heads, relay, ins, outs, scratch):
    s, z, t = lax.axis_index("section"), lax.axis_index("expert"), lax.axis_index("tensor")
    boundary, tabs, gates, gains, wq, wk, wv, wo, wg, wu, wd = ins
    edges, tabs_out, gates_out, gains_out = outs[:4]
    gathered, (sg, su, sd), results = outs[4:8], outs[8:11], outs[11:]
    x_s, tabs_s, gains_s, w_sem, in_sem, own_sem, sib_send, sib_recv, gate_send, gate_recv = scratch[:10]
    relay.bind((wq, wk, wv, wo), gathered, scratch[10:17])
    attn_scratch = scratch[17:]
    other = 1 - s
    i32 = jnp.int32

    own = [
        pltpu.make_async_copy(boundary.at[s], edges.at[s], own_sem.at[0]),
        pltpu.make_async_copy(tabs.at[s], tabs_out.at[s], own_sem.at[1]),
        pltpu.make_async_copy(gains, gains_out.at[s], own_sem.at[2]),
        pltpu.make_async_copy(gates.at[s], gates_out.at[s, z], own_sem.at[3]),
    ]
    for copy in own:
        copy.start()
    greet(all_peers(s, z, t, nz, nt))

    def sibling(i, src, dst):
        return remote(src, dst, sib_send.at[i], sib_recv.at[i], section=other)

    pairs = [
        (boundary.at[other], edges.at[s], edges.at[other]),
        (tabs.at[other], tabs_out.at[s], tabs_out.at[other]),
        (gains, gains_out.at[s], gains_out.at[other]),
        (wg, sg, sg),
        (wu, su, su),
        (wd, sd, sd),
    ]
    for i in range(3):
        sibling(i, *pairs[i][:2]).start()
    for a in range(3):
        relay.begin(a)
    relay.begin_home(3)

    @pl.when(z == 0)
    def _():
        relay.begin_side(3, True)

    @pl.when(z == nz - 1)
    def _():
        relay.begin_side(3, False)

    def gate_copy(d, k, arrival=False):
        zz = partner(z, i32(k), nz)
        section = s if d == 0 else other
        return remote(
            gates.at[section],
            gates_out.at[section, zz] if arrival else gates_out.at[s, z],
            gate_send.at[d, k],
            gate_recv.at[d, k],
            section=section,
            expert=zz,
        )

    turns = [(d, k) for d in range(2) for k in range(nz) if d or k]
    for d, k in turns:
        gate_copy(d, k).start()
    for i in range(3, 6):
        sibling(i, *pairs[i][:2]).start()

    for copy in own:
        copy.wait()
    for i in range(3):
        sibling(i, pairs[i][0], pairs[i][2]).wait_recv()
    loads = [
        pltpu.make_async_copy(edges.at[0], x_s, in_sem.at[0]),
        pltpu.make_async_copy(tabs_out.at[0], tabs_s, in_sem.at[1]),
        pltpu.make_async_copy(gains_out.at[0], gains_s, in_sem.at[2]),
    ]
    for load in loads:
        load.start()
    for load in loads:
        load.wait()

    def bring(a):
        return pltpu.make_async_copy(gathered[a], attn_scratch[a], w_sem.at[a])

    def wait_qkv():
        for k in range(1, nz):
            for a in range(3):
                relay.step(a, k)

            @pl.when((z == k) & (z < nz - 1))
            def _():
                relay.begin_side(3, True)

            @pl.when((z == nz - 1 - k) & (z > 0))
            def _():
                relay.begin_side(3, False)

        for a in range(3):
            relay.settle(a)
            bring(a).start()
        for a in range(3):
            bring(a).wait()

    def wait_out():
        for k in range(1, nz):
            relay.step(3, k)
        relay.settle(3)
        bring(3).start()
        bring(3).wait()

    tables = (tabs_s[0], tabs_s[1], tabs_s[2])
    attend_body(t, nt, heads, x_s, tables, gains_s[...], results, attn_scratch, wait_qkv, wait_out)
    for i in range(6):
        sibling(i, *pairs[i][:2]).wait_send()
    for i in range(3, 6):
        sibling(i, pairs[i][0], pairs[i][2]).wait_recv()
    for d, k in turns:
        gate_copy(d, k).wait_send()
        gate_copy(d, k, True).wait_recv()
    for a in range(4):
        relay.end(a)


def attend_kernel(layer, nz, nt, heads, relay, ins, outs, scratch):
    s, z, t = lax.axis_index("section"), lax.axis_index("expert"), lax.axis_index("tensor")
    x_ref, tabs, gains, wq, wk, wv, wo = ins
    w_sem = scratch[0]
    relay.bind((wo,), outs[:1], scratch[1:8])
    attn_scratch = scratch[8:]
    loads = [
        pltpu.make_async_copy(src, dst, w_sem.at[i])
        for i, (src, dst) in enumerate(zip((wq, wk, wv, outs[0]), attn_scratch))
    ]
    for load in loads[:3]:
        load.start()
    greet(all_peers(s, z, t, nz, nt))
    relay.begin(0)

    def wait_qkv():
        for load in loads[:3]:
            load.wait()

    def wait_out():
        for k in range(1, nz):
            relay.step(0, k)
        relay.settle(0)
        loads[3].start()
        loads[3].wait()

    tables = (tabs[layer, 0], tabs[layer, 1], tabs[layer, 2])
    attend_body(
        t, nt, heads, x_ref, tables, gains[layer], outs[1:], attn_scratch, wait_qkv, wait_out
    )
    relay.end(0)


def load_experts(layer, s, own, sibling, scratch, sems):
    def copies(refs):
        return [pltpu.make_async_copy(r, d, sems.at[i]) for i, (r, d) in enumerate(zip(refs, scratch))]

    @pl.when(s == layer)
    def _():
        for copy in copies(own):
            copy.start()

    @pl.when(s != layer)
    def _():
        for copy in copies(sibling):
            copy.start()

    return copies(own)


def experts_kernel(layer, nz, nt, local_experts, bind, ins, outs, scratch):
    s, z, t = lax.axis_index("section"), lax.axis_index("expert"), lax.axis_index("tensor")
    b_ref, h1_ref, gates, wg, wu, wd, sg, su, sd = ins[:9]
    y_ref, b_out, g_out, u_out = outs[:4]
    wg_s, wu_s, wd_s, g_s, u_s, w_sem, o_sem, own_part = scratch[:8]
    spaces, rest = list(scratch[8:26]) + [own_part], scratch[26:]
    moves = bind(ins[9:], outs[4:], rest)
    rows = b_ref.shape[0]
    loads = load_experts(layer, s, (wg, wu, wd), (sg, su, sd), (wg_s, wu_s, wd_s), w_sem)
    greet(all_peers(s, z, t, nz, nt))
    width = wg.shape[0] // local_experts

    def ready():
        for load in loads:
            load.wait()

    def work(k, origin, rows_in):
        gate_pre = dot_nt(rows_in, wg_s[...])
        up_pre = dot_nt(rows_in, wu_s[...])
        g_s[origin] = gate_pre
        u_s[origin] = up_pre
        weight = expert_gates(gates[layer, origin], z * local_experts, local_experts, width)
        hidden = (gate_pre * jax.nn.sigmoid(gate_pre) * up_pre * weight).astype(BF16)
        return dot(hidden, wd_s[...])

    finish = exchange(z, t, nz, nt, rows, b_ref[...], spaces, ready, work, moves)
    full, total, whole = spaces[0], spaces[6], spaces[7]
    saves = [
        pltpu.make_async_copy(full, b_out, o_sem.at[0]),
        pltpu.make_async_copy(g_s, g_out, o_sem.at[1]),
        pltpu.make_async_copy(u_s, u_out, o_sem.at[2]),
    ]
    for save in saves:
        save.start()
    whole[rows_at(t * rows, rows)] = (h1_ref[...] + total[...]).astype(BF16)
    wait = spread_rows(t, nt, rows, whole, spaces[16], spaces[17])
    finish()
    wait()
    y_ref[...] = whole[...]
    for save in saves:
        save.wait()
    for move in moves:
        move.finish()


def experts_back_kernel(layer, nz, nt, local_experts, bind, ins, outs, scratch):
    s, z, t = lax.axis_index("section"), lax.axis_index("expert"), lax.axis_index("tensor")
    dy_ref, h1_ref, gains, gates, g_in, u_in, wg, wu, wd, sg, su, sd = ins[:12]
    dat_ref, dh1_ref, term_ref, dy_out, hid_out, dg_out, du_out = outs[:7]
    wg_s, wu_s, wd_s, g_s, u_s, hid_s, dg_s, du_s, w_sem, g_sem, u_sem, o_sem, own_part = scratch[:13]
    spaces, rest = list(scratch[13:31]) + [own_part], scratch[31:]
    moves = bind(ins[12:], outs[7:], rest)
    rows, model_width = dy_ref.shape
    loads = load_experts(layer, s, (wd, wg, wu), (sd, sg, su), (wd_s, wg_s, wu_s), w_sem)

    def kept(k):
        origin, slot = partner(z, k, nz), lax.rem(k, 2)
        return (
            pltpu.make_async_copy(g_in.at[origin], g_s.at[slot], g_sem.at[slot]),
            pltpu.make_async_copy(u_in.at[origin], u_s.at[slot], u_sem.at[slot]),
        )

    for load in kept(jnp.int32(0)):
        load.start()
    greet(all_peers(s, z, t, nz, nt))
    width = wg.shape[0] // local_experts

    def ready():
        for load in loads:
            load.wait()

    def work(k, origin, rows_in):
        for load in kept(k):
            load.wait()

        @pl.when(k + 1 < nz)
        def _():
            for load in kept(k + 1):
                load.start()

        slot = lax.rem(k, 2)
        gate_pre, up_pre = g_s[slot], u_s[slot]
        weight = expert_gates(gates[layer, origin], z * local_experts, local_experts, width)
        sigmoid = jax.nn.sigmoid(gate_pre)
        silu = gate_pre * sigmoid
        hid_s[origin] = (silu * up_pre * weight).astype(BF16)
        grad_hidden = dot_nt(rows_in, wd_s[...]) * weight
        dg_s[origin] = (grad_hidden * up_pre * sigmoid * (1.0 + gate_pre * (1.0 - sigmoid))).astype(BF16)
        du_s[origin] = (grad_hidden * silu).astype(BF16)
        return dot(dg_s[origin], wg_s[...]) + dot(du_s[origin], wu_s[...])

    finish = exchange(z, t, nz, nt, rows, dy_ref[...], spaces, ready, work, moves)
    full, total, whole = spaces[0], spaces[6], spaces[7]
    saves = [
        pltpu.make_async_copy(full, dy_out, o_sem.at[0]),
        pltpu.make_async_copy(hid_s, hid_out, o_sem.at[1]),
        pltpu.make_async_copy(dg_s, dg_out, o_sem.at[2]),
        pltpu.make_async_copy(du_s, du_out, o_sem.at[3]),
    ]
    for save in saves:
        save.start()
    unit, factor = unit_rows(h1_ref[...])
    g_moe = gains[layer, :, model_width : 2 * model_width]
    back, term = norm_back(total[...], g_moe, unit, factor)
    dh1 = dy_ref[...].astype(F32) + back
    dh1_ref[...] = dh1
    term_ref[...] = term
    whole[rows_at(t * rows, rows)] = dh1.astype(BF16)
    wait = spread_rows(t, nt, rows, whole, spaces[16], spaces[17])
    finish()
    wait()
    dat_ref[...] = whole[...]
    for save in saves:
        save.wait()
    for move in moves:
        move.finish()


def attend_back_kernel(layer, source, nz, nt, heads, bind, ins, outs, scratch):
    s, z, t = lax.axis_index("section"), lax.axis_index("expert"), lax.axis_index("tensor")
    (x_ref, tabs, gains, dat_ref, dh1_ref, term_moe, q_ref, k_ref, v_ref, qr_ref, kr_ref) = ins[:11]
    wq, wk, wv, wo = ins[11:15]
    dx_ref, dqkv_ref, terms_ref = outs[:3]
    wq_s, wk_s, wv_s, wo_s, part, outgoing, came, s_sem, r_sem, w_sem, gs_sem, gr_sem = scratch[:12]
    if layer == 0:
        whole, terms_near, terms_in, t_sem, near_send, near_recv = scratch[12:18]
        rest, terms_other, moves_in = scratch[18:], ins[15], ins[16:]
        terms_out, moves_out = outs[3], outs[4:]
    else:
        rest, moves_in, moves_out = scratch[12:], ins[15:], outs[3:]
    moves = bind(moves_in, moves_out, rest)
    loads = [
        pltpu.make_async_copy(src, dst, w_sem.at[i])
        for i, (src, dst) in enumerate(((wo, wo_s), (wq, wq_s), (wk, wk_s), (wv, wv_s)))
    ]
    for load in loads:
        load.start()
    greet(all_peers(s, z, t, nz, nt))
    late = ()
    if layer == 0:
        late = moves[-3:]
        moves = moves[:-3]
        late[0].src, late[1].src, late[2].src = dqkv_ref, whole, terms_ref
    for move in moves:
        move.start()

    block = x_ref.shape[1]
    rows = block // nt
    size = tabs.shape[-1]
    g_attn, _, g_query, g_key = split_gains(gains[layer], x_ref.shape[2], size)
    scale = 1.0 / math.sqrt(size)
    cos, sin, bias = tabs[layer, 0], tabs[layer, 1], tabs[layer, 2]
    cos_all, sin_all = tiled(cos, heads), tiled(sin, heads)
    qr, kr, v = qr_ref[...], kr_ref[...], v_ref[...]
    scores = dot_nt(qr, kr) * scale + tiled(bias, heads)
    peak = jnp.max(scores, axis=-1, keepdims=True)
    weight = jnp.exp(scores - peak)
    probs = weight * (1.0 / jnp.sum(weight, axis=-1, keepdims=True))
    loads[0].wait()
    do = heads_to_rows(dot_nt(dat_ref[...], wo_s[...]).astype(BF16), heads, size)
    dv = dot_tn(probs.astype(BF16), do).astype(BF16)
    dp = dot_nt(do, v)
    ds = (probs * (dp - jnp.sum(probs * dp, axis=-1, keepdims=True))).astype(BF16)
    dqr = dot(ds, kr) * scale
    dkr = dot_tn(ds, qr) * scale
    dqn = dqr * cos_all - half_turn(dqr) * sin_all
    dkn = dkr * cos - half_turn(dkr) * sin
    q_unit, q_factor = unit_rows(heads_to_rows(q_ref[...], heads, size))
    k_unit, k_factor = unit_rows(k_ref[...])
    dq, term_query = norm_back(dqn, g_query, q_unit, q_factor)
    dk, term_key = norm_back(dkn, g_key, k_unit, k_factor)
    dq = rows_to_heads(dq.astype(BF16), heads, block)
    dk = dk.astype(BF16)
    dqkv_ref[:, : heads * size] = dq
    dqkv_ref[:, heads * size : (heads + 1) * size] = dk
    dqkv_ref[:, (heads + 1) * size :] = dv
    if layer == 0:
        late[0].start()
    for load in loads[1:]:
        load.wait()
    part[...] = dot_nt(dq, wq_s[...]) + dot_nt(dk, wk_s[...]) + dot_nt(dv, wv_s[...])
    total = reduce_rows(t, nt, rows, part, outgoing, came, s_sem, r_sem)
    mine = rows_at(t * rows, rows)
    unit, factor = unit_rows(x_ref[source, mine].astype(F32))
    back, term_attn = norm_back(total, g_attn, unit, factor)
    dx = (dh1_ref[...] + back).astype(BF16)
    terms_ref[...] = jnp.zeros_like(terms_ref)
    write_terms(terms_ref, 0, term_moe[...])
    write_terms(terms_ref, 8, term_attn)
    terms_ref[16:17, :size] = term_query
    terms_ref[16:17, size : 2 * size] = term_key
    if layer == 1:
        dx_ref[...] = dx
    else:
        late[2].start()
        whole[mine] = dx
        wait = spread_rows(t, nt, rows, whole, gs_sem, gr_sem)
        wait()
        late[1].start()
        late[2].arrive()

        def total_of(ref):
            out = ref[0, 0]
            for section in range(2):
                for origin in range(nz):
                    if section or origin:
                        out = out + ref[section, origin]
            return out

        @pl.when(s == 0)
        def _():
            copy = pltpu.make_async_copy(late[2].out, terms_in, t_sem.at[0])
            copy.start()
            copy.wait()

        @pl.when(s != 0)
        def _():
            copy = pltpu.make_async_copy(terms_other, terms_in, t_sem.at[0])
            copy.start()
            copy.wait()

        terms_near[0] = total_of(terms_in)

        def near(j):
            return remote(
                terms_near.at[0],
                terms_near.at[j],
                near_send.at[j],
                near_recv.at[j],
                tensor=partner(t, jnp.int32(j), nt),
            )

        for j in range(1, nt):
            near(j).start()
        sums = terms_near[0]
        for j in range(1, nt):
            near(j).wait_recv()
            sums = sums + terms_near[j]
        for j in range(1, nt):
            near(j).wait_send()
        terms_out[...] = sums
        late[0].finish()
        late[1].finish()
        late[2].leave()
        dx_ref[...] = dx
    for move in moves:
        move.finish()


def expert_grads_kernel(nz, step, ins, outs, scratch):
    s = lax.axis_index("section")
    own, near = (ins[0:5], ins[5:10]), (ins[10:15], ins[15:20])
    left, right, stage, in_sem, out_sem = scratch

    def loads(layer):
        out = []
        for i in range(5):
            target = left.at[i] if i < 3 else right.at[i - 3]
            out.append(
                (
                    pltpu.make_async_copy(own[layer][i], target.at[pl.ds(0, nz)], in_sem.at[i, 0]),
                    pltpu.make_async_copy(near[layer][i], target.at[pl.ds(nz, nz)], in_sem.at[i, 1]),
                )
            )
        return out

    order = (3, 0, 1, 4, 2)
    for layer in range(2):

        @pl.when(s == layer)
        def _():
            copies = loads(layer)
            for i in order:
                for copy in copies[i]:
                    copy.start()

    waits = loads(0)
    width = right.shape[-1]
    tokens = 2 * nz * right.shape[2]
    cols = left.shape[-1]
    done = set()

    def need(i):
        if i not in done:
            for copy in waits[i]:
                copy.wait()
            done.add(i)

    turn = 0
    for i, r in ((0, 0), (1, 0), (2, 1)):
        need(3 + r)
        need(i)
        for c in range(0, cols, step):
            slot = turn % 2
            if turn >= 2:
                pltpu.make_async_copy(stage.at[slot], outs[0].at[pl.ds(0, step)], out_sem.at[slot]).wait()
            lhs = left[i, :, :, c : c + step].reshape(tokens, step)
            stage[slot] = dot_tn(lhs, right[r].reshape(tokens, width))
            pltpu.make_async_copy(stage.at[slot], outs[i].at[pl.ds(c, step)], out_sem.at[slot]).start()
            turn += 1
    for slot in range(2):
        pltpu.make_async_copy(stage.at[slot], outs[0].at[pl.ds(0, step)], out_sem.at[slot]).wait()


def attend_grads_kernel(q_cols, size, ins, outs, scratch):
    s = lax.axis_index("section")
    spaces, sems = scratch[:4], scratch[4]

    def loads(layer):
        refs = ins[4 * layer : 4 * layer + 4]
        return [pltpu.make_async_copy(r, d, sems.at[i]) for i, (r, d) in enumerate(zip(refs, spaces))]

    for layer in range(2):

        @pl.when(s == layer)
        def _():
            for load in loads(layer):
                load.start()

    waits = loads(0)
    a_s, d_s, o_s, t_s = spaces

    def flat(ref):
        return ref[...].reshape(-1, ref.shape[-1])

    waits[0].wait()
    waits[1].wait()
    grad = dot_tn(flat(a_s), flat(d_s))
    outs[0][...] = grad[:, :q_cols]
    outs[1][...] = grad[:, q_cols : q_cols + size]
    outs[2][...] = grad[:, q_cols + size :]
    waits[2].wait()
    waits[3].wait()
    outs[3][...] = dot_tn(flat(o_s), flat(t_s))


def shape_of(shape, dtype):
    return jax.ShapeDtypeStruct(tuple(shape), dtype)


def like(value, lead=()):
    return shape_of(tuple(lead) + tuple(value.shape), value.dtype)


def call(body, name, number, ins, outs, scratch):
    def kernel(*refs):
        body(refs[: len(ins)], refs[len(ins) : len(ins) + len(outs)], refs[len(ins) + len(outs) :])

    return pl.pallas_call(
        kernel,
        out_shape=tuple(o for o, _ in outs),
        in_specs=[spec for _, spec in ins],
        out_specs=tuple(spec for _, spec in outs),
        scratch_shapes=list(scratch),
        compiler_params=pltpu.CompilerParams(
            collective_id=number, has_side_effects=number is not None, vmem_limit_bytes=VMEM_LIMIT
        ),
        name=name,
    )(*[value for value, _ in ins])


def vm(*values):
    return [(value, VM) for value in values]


def any_place(*values):
    return [(value, ANY) for value in values]


def block_tables(lengths, block, size):
    ends = jnp.cumsum(lengths)
    starts = ends - lengths
    places = jnp.arange(block, dtype=jnp.int32)
    segment = jnp.sum((places[:, None] >= ends[None, :]).astype(jnp.int32), axis=1)
    numbers = jnp.arange(lengths.shape[0], dtype=jnp.int32)
    offset = jnp.sum(jnp.where(segment[:, None] == numbers[None, :], starts[None, :], 0), axis=1)
    half = jnp.arange(size // 2, dtype=F32)
    inverse = jnp.exp(half * (-2.0 * math.log(THETA) / size))
    angle = (places - offset).astype(F32)[:, None] * inverse[None, :]
    cos, sin = jnp.cos(angle), jnp.sin(angle)
    allowed = (places[None, :] <= places[:, None]) & (segment[:, None] == segment[None, :])
    bias = jnp.where(allowed, 0.0, -1e30).astype(F32)
    return jnp.stack(
        [
            jnp.concatenate([cos, cos], axis=-1),
            jnp.concatenate([-sin, sin], axis=-1),
            bias,
        ]
    )


def on_device(
    boundary, seq_lengths, expert_ids, route_weights, attn_gain, moe_gain, query_gain, key_norm_gain,
    w_query, key_weight, value_weight, w_output, w_gate, w_up, w_down,
):
    nz, nt = lax.axis_size("expert"), lax.axis_size("tensor")
    micro, block, width = boundary.shape[1:]
    size = query_gain.shape[1]
    heads = w_query.shape[2] // size
    local_experts = w_gate.shape[1]
    hidden = local_experts * w_gate.shape[2]
    experts = local_experts * nz
    rows = block // nt
    q_cols = heads * size
    assert micro == 2 and key_weight.shape[2] == size and experts <= LANES
    dma = pltpu.SemaphoreType.DMA

    tabs = jax.vmap(lambda lengths: block_tables(lengths, block, size))(seq_lengths[0, :, 0])
    lanes = jnp.arange(LANES, dtype=jnp.int32)
    gates = jnp.sum(
        jnp.where(expert_ids[0][..., None] == lanes, route_weights[0][..., None], 0.0), axis=2
    )
    wg, wu, wd = (w[0].reshape(hidden, width) for w in (w_gate, w_up, w_down))
    wq, wk, wv, wo = w_query[0], key_weight[0], value_weight[0], w_output[0]
    gains = jnp.concatenate([attn_gain, moe_gain, query_gain, key_norm_gain], axis=1)

    spaces = [
        pltpu.VMEM((width, q_cols), BF16),
        pltpu.VMEM((width, size), BF16),
        pltpu.VMEM((width, size), BF16),
        pltpu.VMEM((q_cols, width), BF16),
        pltpu.VMEM((block, width), F32),
        pltpu.VMEM((block, width), BF16),
        pltpu.VMEM((nt, rows, width), BF16),
        dma((nt,)),
        dma((nt,)),
    ]
    gathered = [
        shape_of((width, q_cols), BF16),
        shape_of((width, size), BF16),
        shape_of((width, size), BF16),
        shape_of((q_cols, width), BF16),
    ]
    attend_outs = vm(
        shape_of((rows, width), F32),
        shape_of((rows, width), BF16),
        shape_of((block, width), BF16),
        shape_of((block, q_cols), F32),
        shape_of((block, size), F32),
        shape_of((block, size), BF16),
        shape_of((heads * block, size), BF16),
        shape_of((block, size), BF16),
        shape_of((block, q_cols), BF16),
    )
    own_part = pltpu.VMEM((nz, rows, width), F32)
    expert_scratch = [pltpu.VMEM((hidden, width), BF16)] * 3

    relay = Relay(0, (0, 0, 0, 1), nz)
    started = call(
        functools.partial(start_attend_kernel, nz, nt, heads, relay),
        "start_attend_0",
        0,
        any_place(boundary[0], tabs, gates, gains, wq, wk, wv, wo, wg, wu, wd),
        any_place(
            shape_of((2, block, width), BF16),
            shape_of((2, 3, block, size), F32),
            shape_of((2, nz, block, LANES), F32),
            like(gains, (2,)),
            *gathered,
            *[shape_of((hidden, width), BF16)] * 3,
        )
        + attend_outs,
        [
            pltpu.VMEM((block, width), BF16),
            pltpu.VMEM((3, block, size), F32),
            pltpu.VMEM(gains.shape, F32),
            dma((4,)), dma((3,)), dma((4,)), dma((6,)), dma((6,)), dma((2, nz)), dma((2, nz)),
        ]
        + relay.scratch(4)
        + spaces,
    )
    edges, tabs_all, gates_all, gains_all = started[:4]
    weights_0 = started[4:8]
    expert_weights = (wg, wu, wd) + tuple(started[8:11])
    h1_0, b_0, a_0, q_0, k_0, v_0, qr_0, kr_0, o_0 = started[11:]

    def run_experts(layer, b, h1, move_ins, move_outs, move_scratch, bind):
        return call(
            functools.partial(experts_kernel, layer, nz, nt, local_experts, bind),
            f"experts_{layer}",
            1 + layer,
            vm(b, h1, gates_all) + any_place(*expert_weights, *move_ins),
            vm(shape_of((block, width), BF16))
            + any_place(
                shape_of((nz, block, width), BF16),
                shape_of((nz, block, hidden), F32),
                shape_of((nz, block, hidden), F32),
                *move_outs,
            ),
            expert_scratch
            + [pltpu.VMEM((nz, block, hidden), F32)] * 2
            + [dma((3,)), dma((3,)), own_part]
            + exchange_scratch(nz, nt, rows, block, width)
            + move_scratch,
        )

    def experts_back(layer, dy, h1, gate_pre, up_pre, move_ins, move_outs, move_scratch, bind):
        return call(
            functools.partial(experts_back_kernel, layer, nz, nt, local_experts, bind),
            f"experts_back_{layer}",
            3 + layer,
            vm(dy, h1, gains_all, gates_all)
            + any_place(gate_pre, up_pre, *expert_weights, *move_ins),
            vm(
                shape_of((block, width), BF16),
                shape_of((rows, width), F32),
                shape_of((1, width), F32),
            )
            + any_place(
                shape_of((nz, block, width), BF16),
                shape_of((nz, block, hidden), BF16),
                shape_of((nz, block, hidden), BF16),
                shape_of((nz, block, hidden), BF16),
                *move_outs,
            ),
            expert_scratch
            + [pltpu.VMEM((2, block, hidden), F32)] * 2
            + [pltpu.VMEM((nz, block, hidden), BF16)] * 3
            + [dma((3,)), dma((2,)), dma((2,)), dma((4,)), own_part]
            + exchange_scratch(nz, nt, rows, block, width)
            + move_scratch,
        )

    def binder(kinds):
        def bind(ins, outs, scratch):
            return [
                kind.bind(ins[i] if i < len(ins) else None, outs[i], scratch[3 * i : 3 * i + 3])
                for i, kind in enumerate(kinds)
            ]

        return bind

    def shapes_of(kinds, values):
        out = []
        for kind, value in zip(kinds, values):
            if isinstance(kind, Near):
                out.append(like(value, (2,) if kind.both else ()))
            elif kind.sliced:
                out.append(shape_of((2, nz, block, width // nz), value.dtype))
            else:
                out.append(like(value, (2, nz)))
        return out

    def scratch_of(kinds):
        return [sem for kind in kinds for sem in kind.scratch()]

    qkv = Relay(1, (0, 0, 0), nz)
    ran = run_experts(
        0, b_0, h1_0, (wq, wk, wv), gathered[:3], qkv.scratch(3),
        lambda ins, outs, scratch: [qkv.bind(ins, outs, scratch)],
    )
    x_1, ball_0, gp_0, up_0 = ran[:4]
    qkv_1 = ran[4:]

    relay_1 = Relay(1, (1,), nz)
    attended = call(
        functools.partial(attend_kernel, 1, nz, nt, heads, relay_1),
        "attend_1",
        5,
        vm(x_1, tabs_all, gains_all) + any_place(*qkv_1, wo),
        any_place(gathered[3]) + attend_outs,
        [dma((4,))] + relay_1.scratch(1) + spaces,
    )
    weights_1 = tuple(qkv_1) + (attended[0],)
    h1_1, b_1, a_1, q_1, k_1, v_1, qr_1, kr_1, o_1 = attended[1:]

    kinds = (Gather(0, nz), Gather(0, nz, True), Near(0))
    values = (o_0, a_0, ball_0)
    ran = run_experts(
        1, b_1, h1_1, values, shapes_of(kinds, values), scratch_of(kinds), binder(kinds)
    )
    y_1, ball_1, gp_1, up_1 = ran[:4]
    oall_0, aall_0, bnear_0 = ran[4:]

    dy_1 = lax.dynamic_slice_in_dim(edges[1], lax.axis_index("tensor") * rows, rows, 0)
    kinds = (Gather(1, nz), Gather(1, nz, True), Near(1), Near(1, True))
    values = (o_1, a_1, ball_1, y_1)
    ran = experts_back(
        1, dy_1, h1_1, gp_1, up_1, values, shapes_of(kinds, values), scratch_of(kinds), binder(kinds)
    )
    dat_1, dh1_1, tm_1, dyall_1, hid_1, dg_1, du_1 = ran[:7]
    oall_1, aall_1, bnear_1, ends_1 = ran[7:]

    def attend_back(layer, x, source, dat, dh1, term_moe, kept, weights, kinds, values, late):
        outs = vm(
            shape_of((rows, width), BF16),
            shape_of((block, q_cols + 2 * size), BF16),
            shape_of((TERM_ROWS, TERM_COLS), F32),
        )
        scratch = spaces + [dma((4,)), dma((nt,)), dma((nt,))]
        ins = vm(x, tabs_all, gains_all, dat, dh1, term_moe, *kept) + any_place(*weights)
        shapes = [o for o, _ in outs]
        late_shapes = []
        if late is not None:
            outs += vm(shape_of((TERM_ROWS, TERM_COLS), F32))
            scratch += [
                pltpu.VMEM((block, width), BF16),
                pltpu.VMEM((nt, TERM_ROWS, TERM_COLS), F32),
                pltpu.VMEM((2, nz, TERM_ROWS, TERM_COLS), F32),
                dma((1,)),
                dma((nt,)),
                dma((nt,)),
            ]
            ins += any_place(late)
            last = (Gather(0, nz), Near(0, True), Gather(0, nz))
            late_shapes = shapes_of(last, (shapes[1], shape_of((block, width), BF16), shapes[2]))
            kinds = kinds + last
        return call(
            functools.partial(attend_back_kernel, layer, source, nz, nt, heads, binder(kinds)),
            f"attend_back_{layer}",
            6 + layer,
            ins + any_place(*values),
            outs + any_place(*shapes_of(kinds[: len(values)], values), *late_shapes),
            scratch + scratch_of(kinds),
        )

    kinds = (Gather(1, nz, True), Near(1), Near(1), Near(1), Near(1))
    values = (dat_1, dg_1, du_1, hid_1, dyall_1)
    ran = attend_back(
        1, x_1[None], 0, dat_1, dh1_1, tm_1, (q_1, k_1, v_1, qr_1, kr_1), weights_1, kinds, values, None
    )
    dx_1, dqkv_1, terms_1 = ran[:3]
    datall_1, near_1 = ran[3], ran[4:8]

    kinds = (Gather(1, nz), Gather(1, nz))
    values = (dqkv_1, terms_1)
    ran = experts_back(
        0, dx_1, h1_0, gp_0, up_0, values, shapes_of(kinds, values), scratch_of(kinds), binder(kinds)
    )
    dat_0, dh1_0, tm_0, dyall_0, hid_0, dg_0, du_0 = ran[:7]
    dqkvall_1, termsall_1 = ran[7:]

    kinds = (Gather(0, nz, True), Near(0), Near(0), Near(0), Near(0))
    values = (dat_0, dg_0, du_0, hid_0, dyall_0)
    ran = attend_back(
        0, edges, 0, dat_0, dh1_0, tm_0, (q_0, k_0, v_0, qr_0, kr_0), weights_0, kinds, values, termsall_1
    )
    terms, datall_0, near_0 = ran[3], ran[4], ran[5:9]
    dqkvall_0, ends_0 = ran[9:11]

    step = 256
    flat = shape_of((hidden, width), F32)
    grad_gate, grad_up, grad_down = call(
        functools.partial(expert_grads_kernel, nz, step),
        "expert_grads",
        None,
        any_place(
            dg_0, du_0, hid_0, ball_0, dyall_0,
            dg_1, du_1, hid_1, ball_1, dyall_1,
            *near_0[:3], bnear_0, near_0[3],
            *near_1[:3], bnear_1, near_1[3],
        ),
        any_place(flat, flat, flat),
        [
            pltpu.VMEM((3, 2 * nz, block, hidden), BF16),
            pltpu.VMEM((2, 2 * nz, block, width), BF16),
            pltpu.VMEM((2, step, width), F32),
            dma((5, 2)),
            dma((2,)),
        ],
    )
    operands = (aall_0, dqkvall_0, oall_0, datall_0, aall_1, dqkvall_1, oall_1, datall_1)
    grad_query, grad_key, grad_value, grad_output = call(
        functools.partial(attend_grads_kernel, q_cols, size),
        "attend_grads",
        None,
        any_place(*operands),
        vm(
            shape_of(wq.shape, F32),
            shape_of(wk.shape, F32),
            shape_of(wv.shape, F32),
            shape_of(wo.shape, F32),
        ),
        [pltpu.VMEM(o.shape, o.dtype) for o in operands[:4]] + [dma((4,))],
    )
    ends = jnp.where(lax.axis_index("section") == 0, ends_0, ends_1)
    return (
        ends[None],
        terms[8:16].reshape(1, width),
        terms[:8].reshape(1, width),
        terms[16:17, :size],
        terms[16:17, size : 2 * size],
        grad_query[None],
        grad_key[None],
        grad_value[None],
        grad_output[None],
        grad_gate.reshape(w_gate.shape),
        grad_up.reshape(w_gate.shape),
        grad_down.reshape(w_gate.shape),
    )


def solution(mesh):
    return jax.shard_map(
        on_device,
        mesh=mesh,
        in_specs=(
            P("section", None, "expert", None),
            P("section", None, "expert", None),
            P("section", None, "expert", None),
            P("section", None, "expert", None),
            P("section", None),
            P("section", None),
            P("section", None),
            P("section", None),
            P("section", "expert", "tensor"),
            P("section", "expert", "tensor"),
            P("section", "expert", "tensor"),
            P("section", "tensor", "expert"),
            P("section", "expert", "tensor", None),
            P("section", "expert", "tensor", None),
            P("section", "expert", "tensor", None),
        ),
        out_specs=(
            P("section", None, "expert", None),
            P("section", None),
            P("section", None),
            P("section", None),
            P("section", None),
            P("section", "expert", "tensor"),
            P("section", "expert", "tensor"),
            P("section", "expert", "tensor"),
            P("section", "tensor", "expert"),
            P("section", "expert", "tensor", None),
            P("section", "expert", "tensor", None),
            P("section", "expert", "tensor", None),
        ),
        check_vma=False,
    )
```

time: 820 us -> 586 us (0.71)
  Pallas kernels: 763 us -> 569 us
  matrix products: 30.2 us -> 0 us
    pallas_call x10, Pallas kernels: 763 us -> 569 us  [call(): pl.pallas_call(kernel, out_shape=tuple((o for o, _ in outs)), in_specs=[s...]
    dot_general x7 -> x0, matrix products: 30.2 us -> none  [weight_grad(): lax.dot_general(flat(left), flat(right), (((0,), (0,)), ((), ())), prefer...]
where the time goes in v2:
time: 586 us; the launch traced here: 582 us
  Pallas kernels  569 us (97%)
  other arithmetic  7.12 us (1%)
    pallas_call x10, Pallas kernels, call(): pl.pallas_call(kernel, out_shape=tuple((o for o, _ in outs)), in_specs=[s...  569 us

profile of v2, /device:TPU:0, one launch (start us, length us, event | category | flops | bytes accessed | tf_op | source)
XLA Modules:
  0.0 582.0 jit_solution(11710294406805325111)
XLA Ops:
  0.7 0.9 reduce_window_sum.11
  1.5 0.1 convert_reduce_fusion
  1.6 0.7 sub.20
  2.3 0.1 select_reduce_fusion.1
  2.4 1.4 pad_maximum_fusion.refs_3_
  3.8 0.1 and_select_fusion
  3.9 0.8 copy.31
  4.7 0.8 copy.32
  5.5 1.4 select_reduce_fusion.refs_2_
  6.9 0.5 multiply_cosine_fusion
  7.5 0.1 maximum_bitcast_fusion.1
  7.6 0.8 maximum_bitcast_fusion.refs_1_
  8.4 112.3 %start_attend_0.1 = (bf16[2,128,2048]{2,1,0:T(8,128)(2,1)}, f32[2,3,128,128]{3,2,1,0:T(8,128)}, f32[2,4,128,128]{3,2,1,0:T(8,128)}, f32[2,1,4352]{2,1,0:T(1,128)...) custom-call(bf16[2,128,2048]{2,1,0:T(8,128)(2,1)} %bitcast.59, ...), custom_call_target="tpu_custom_call" | custom-call | tf_op jit(solution)/shard_map/start_attend_0/pallas_call | solution.py:1149
  120.7 1.1 slice.15
  121.7 0.7 dynamic-slice_bitcast_fusion.refs_0_
  122.4 92.9 %experts_0.1 = (bf16[128,2048]{1,0:T(8,128)(2,1)}, bf16[4,128,2048]{2,1,0:T(8,128)(2,1)}, f32[4,128,768]{2,1,0:T(8,128)}, f32[4,128,768]{2,1,0:T(8,128)}, bf16[2...) custom-call(bf16[32,2048]{1,0:T(8,128)(2,1)} %get-tuple-element.102.refs_0_, ...), custom_call_target="tpu_custom_call" | custom-call | tf_op jit(solution)/shard_map/experts_0/pallas_call | solution.py:1149
  215.3 56.0 %attend_1.1 = (bf16[1024,2048]{1,0:T(8,128)(2,1)}, f32[32,2048]{1,0:T(8,128)}, bf16[32,2048]{1,0:T(8,128)(2,1)}, bf16[128,2048]{1,0:T(8,128)(2,1)}, f32[128,1024...) custom-call(bf16[128,2048]{1,0:T(8,128)(2,1)} %get-tuple-element.108, ...), custom_call_target="tpu_custom_call" | custom-call | tf_op jit(solution)/shard_map/attend_1/pallas_call | solution.py:1149
  271.4 68.6 %experts_1.1 = (bf16[128,2048]{1,0:T(8,128)(2,1)}, bf16[4,128,2048]{2,1,0:T(8,128)(2,1)}, f32[4,128,768]{2,1,0:T(8,128)}, f32[4,128,768]{2,1,0:T(8,128)}, bf16[2...) custom-call(bf16[32,2048]{1,0:T(8,128)(2,1)} %get-tuple-element.113.refs_0_, ...), custom_call_target="tpu_custom_call" | custom-call | tf_op jit(solution)/shard_map/experts_1/pallas_call | solution.py:1149
  339.9 70.8 %experts_back_1.1 = (bf16[128,2048]{1,0:T(8,128)(2,1)}, f32[32,2048]{1,0:T(8,128)}, f32[1,2048]{1,0:T(1,128)}, bf16[4,128,2048]{2,1,0:T(8,128)(2,1)}, bf16[4,128...) custom-call(bf16[32,2048]{1,0:T(8,128)(2,1)} %dynamic-slice_bitcast_, ...), custom_call_target="tpu_custom_call" | custom-call | tf_op jit(solution)/shard_map/experts_back_1/pallas_call | solution.py:1149
  410.8 20.7 %attend_back_1.1 = (bf16[32,2048]{1,0:T(8,128)(2,1)}, bf16[128,1280]{1,0:T(8,128)(2,1)}, f32[24,256]{1,0:T(8,128)}, bf16[2,4,128,512]{3,2,1,0:T(8,128)(2,1)}, bf...) custom-call(bf16[1,128,2048]{2,1,0:T(8,128)(2,1)} %bitcast.58, ...), custom_call_target="tpu_custom_call" | custom-call | tf_op jit(solution)/shard_map/attend_back_1/pallas_call | solution.py:1149
  431.5 68.6 %experts_back_0.1 = (bf16[128,2048]{1,0:T(8,128)(2,1)}, f32[32,2048]{1,0:T(8,128)}, f32[1,2048]{1,0:T(1,128)}, bf16[4,128,2048]{2,1,0:T(8,128)(2,1)}, bf16[4,128...) custom-call(bf16[32,2048]{1,0:T(8,128)(2,1)} %get-tuple-element.136., ...), custom_call_target="tpu_custom_call" | custom-call | tf_op jit(solution)/shard_map/experts_back_0/pallas_call | solution.py:1149
  500.0 55.9 %attend_back_0.1 = (bf16[32,2048]{1,0:T(8,128)(2,1)}, bf16[128,1280]{1,0:T(8,128)(2,1)}, f32[24,256]{1,0:T(8,128)}, f32[24,256]{1,0:T(8,128)}, bf16[2,4,128,512]...) custom-call(bf16[2,128,2048]{2,1,0:T(8,128)(2,1)} %get-tuple-element, ...), custom_call_target="tpu_custom_call" | custom-call | tf_op jit(solution)/shard_map/attend_back_0/pallas_call | solution.py:1149
  556.0 16.0 %expert_grads.1 = (f32[768,2048]{1,0:T(8,128)}, f32[768,2048]{1,0:T(8,128)}, f32[768,2048]{1,0:T(8,128)}) custom-call(bf16[4,128,768]{2,1,0:T(8,128)(2,1)} %get-tuple-element.154.refs_17_.refs_0_, bf16[4,128,768]{2,1,0:T(8,128)(2,1)} %get-tuple-element.155.refs_18_.refs_1_, bf16[4,128,768]{2,1,0:T(8,128)(2,1)} %get-tuple-element.156.refs_19_.refs_2_, ...), custom_call_target="tpu_custom_call" | custom-call | tf_op jit(solution)/shard_map/expert_grads/pallas_call | solution.py:1149
  571.9 0.0 copy-start
  572.0 0.0 copy-start.1
  572.0 6.9 %attend_grads.1 = (f32[512,1024]{1,0:T(8,128)}, f32[512,128]{1,0:T(8,128)}, f32[512,128]{1,0:T(8,128)}, f32[1024,512]{1,0:T(8,128)}) custom-call(bf16[2,4,128,512]{3,2,1,0:T(8,128)(2,1)} %get-tuple-element.161.refs_0_, bf16[2,4,128,1280]{3,2,1,0:T(8,128)(2,1)} %get-tuple-element.162.refs_1_, bf16[2,4,128,1024]{3,2,1,0:T(8,128)(2,1)} %get-tuple-element.163.refs_2_, ...), custom_call_target="tpu_custom_call" | custom-call | tf_op jit(solution)/shard_map/attend_grads/pallas_call | solution.py:1149
  578.9 0.0 copy-start.2
  578.9 0.0 copy-done
  578.9 1.1 select_bitcast_fusion
  580.0 0.5 fusion.1
  580.5 0.6 copy.34
  581.1 0.6 copy.33
  (6 shorter events, 0.0 us)
Async XLA Ops:
  571.9 7.0 %copy-start = (bf16[2,128,2048]{2,1,0:T(8,128)(2,1)S(1)}, bf16[2,128,2048]{2,1,0:T(8,128)(2,1)}, u32[]{:S(2)}) copy-start(bf16[2,128,2048]{2,1,0:T(8,128)(2,1)} %get-tuple-element.159) | copy-start | bytes 3145732
  572.0 7.0 %copy-start.1 = (bf16[2,128,2048]{2,1,0:T(8,128)(2,1)S(1)}, bf16[2,128,2048]{2,1,0:T(8,128)(2,1)}, u32[]{:S(2)}) copy-start(bf16[2,128,2048]{2,1,0:T(8,128)(2,1)} %get-tuple-element.158) | copy-start | bytes 3145732
  578.9 1.1 copy-start.2

commit v3 on v2

--- a/solution.py
+++ b/solution.py
@@ -20,6 +20,7 @@
 
 ANY = pl.BlockSpec(memory_space=pl.ANY)
 VM = pl.BlockSpec(memory_space=pltpu.VMEM)
+SM = pl.BlockSpec(memory_space=pltpu.SMEM)
 
 
 def partner(index, k, count):
@@ -99,151 +100,208 @@
         terms_ref[row + i : row + i + 1, :] = vector[:, i * TERM_COLS : (i + 1) * TERM_COLS]
 
 
-def exchange_sems(nz, nt):
+def exchange_scratch(nz, nt, rows, block, width):
     dma = pltpu.SemaphoreType.DMA
-    return [dma((nz,)), dma((nz,)), dma((nz, nt)), dma((nz, nt))] * 2 + [dma((nt,)), dma((nt,))]
-
-
-def exchange_scratch(nz, nt, rows, block, width):
+    half = width // 2
     return [
         pltpu.VMEM((nz, block, width), BF16),
         pltpu.VMEM((nz, block, width), BF16),
         pltpu.VMEM((block, width), F32),
-        pltpu.VMEM((nz, nt, rows, width), BF16),
+        pltpu.VMEM((nz, 2 * rows, half), BF16),
+        pltpu.VMEM((nz, 2, rows, half), BF16),
+        pltpu.VMEM((nz, 2, rows, half), BF16),
+        pltpu.VMEM((nz, 2, rows, half), BF16),
         pltpu.VMEM((nz, rows, width), BF16),
         pltpu.VMEM((nz, rows, width), BF16),
+        pltpu.VMEM((nz, rows, width), F32),
         pltpu.VMEM((rows, width), F32),
         pltpu.VMEM((block, width), BF16),
-    ] + exchange_sems(nz, nt)
+        dma((4, nz)),
+        dma((4, nz, 2)),
+        dma((6, nz, 2)),
+        dma((2, nt)),
+    ]
+
+
+EXCHANGE_SCRATCH = 16
 
 
 def exchange(z, t, nz, nt, rows, own_rows, scratch, ready, work, moves):
-    (full, outgoing, part, came_near, passed, came_far, total, _) = scratch[:8]
-    (gz_send, gz_recv, gt_send, gt_recv, rz_send, rz_recv, rt_send, rt_recv) = scratch[8:16]
+    (full, outgoing, part, from_y, from_x, pairs, came_pairs) = scratch[:7]
+    (passed, came_far, own_part, total) = scratch[7:11]
+    far_sem, row_sem, part_sem = scratch[12:15]
+    assert nt == 4
     i32 = jnp.int32
-    mine = rows_at(t * rows, rows)
-
-    def far_copy(k):
+    width = full.shape[-1]
+    half = width // 2
+    first, second = pl.ds(0, half), pl.ds(half, half)
+    near_x, near_y, across = (partner(t, i32(j), nt) for j in (1, 2, 3))
+
+    def window(index):
+        return rows_at(index * rows, rows)
+
+    mine = window(t)
+    x_rows, y_rows, across_rows = window(near_x), window(near_y), window(across)
+    my_pair = rows_at(lax.div(t, 2) * (2 * rows), 2 * rows)
+    y_pair = rows_at(lax.div(near_y, 2) * (2 * rows), 2 * rows)
+    in_pair = lax.rem(t, 2)
+    pair_mine, pair_x = window(in_pair), window(1 - in_pair)
+
+    def far_copy(k, source):
+        spot = full.at[source, mine]
+        return remote(spot, spot, far_sem.at[0, k], far_sem.at[1, k], expert=partner(z, i32(k), nz))
+
+    def row_copy(k, source, j, window_of):
+        spot = full.at[source, window_of]
         return remote(
-            full.at[z, mine],
-            full.at[z, mine],
-            gz_send.at[k],
-            gz_recv.at[k],
-            expert=partner(z, i32(k), nz),
+            spot, spot, row_sem.at[0, k, j], row_sem.at[1, k, j], tensor=(near_x, near_y)[j]
         )
 
-    def near_copy(k, source, j):
+    def on_copy(k, source, j, window_of):
+        spot = full.at[source, window_of, (second, first)[j]]
         return remote(
-            full.at[source, mine],
-            full.at[source, mine],
-            gt_send.at[k, j],
-            gt_recv.at[k, j],
-            tensor=partner(t, i32(j), nt),
+            spot, spot, row_sem.at[2, k, j], row_sem.at[3, k, j], tensor=(near_x, near_y)[j]
         )
 
-    def near_arrival(k, source, j):
-        theirs = rows_at(partner(t, i32(j), nt) * rows, rows)
+    def send_rows(k, source):
+        for j in range(2):
+            row_copy(k, source, j, mine).start()
+
+    def pass_rows(k, source):
+        row_copy(k, source, 0, x_rows).wait_recv()
+        on_copy(k, source, 1, x_rows).start()
+        row_copy(k, source, 1, y_rows).wait_recv()
+        on_copy(k, source, 0, y_rows).start()
+
+    def wait_rows(k, source):
+        for j in range(2):
+            on_copy(k, source, j, across_rows).wait_recv()
+
+    def part_copy(k, i):
+        src = ((y_pair, first), (across_rows, second), (x_rows, second))[i]
+        dst = (from_y.at[k], from_x.at[k, 1], from_x.at[k, 0])[i]
+        group, slot = ((0, 0), (2, 1), (2, 0))[i]
         return remote(
-            full.at[source, theirs],
-            full.at[source, theirs],
-            gt_send.at[k, j],
-            gt_recv.at[k, j],
-            tensor=partner(t, i32(j), nt),
+            outgoing.at[k, src[0], src[1]],
+            dst,
+            part_sem.at[group, k, slot],
+            part_sem.at[group + 1, k, slot],
+            tensor=near_x if i else near_y,
         )
 
-    def far_arrival(k):
-        source = partner(z, i32(k), nz)
+    def pair_copy(k, j):
         return remote(
-            full.at[source, mine],
-            full.at[source, mine],
-            gz_send.at[k],
-            gz_recv.at[k],
-            expert=source,
-        )
-
-    def part_copy(k, j):
-        peer = partner(t, i32(j), nt)
-        return remote(
-            outgoing.at[k, rows_at(peer * rows, rows)],
-            came_near.at[k, j],
-            rt_send.at[k, j],
-            rt_recv.at[k, j],
-            tensor=peer,
+            pairs.at[k, j],
+            came_pairs.at[k, j],
+            part_sem.at[4, k, j],
+            part_sem.at[5, k, j],
+            tensor=(near_x, near_y)[j],
         )
 
     def sum_copy(k):
         return remote(
             passed.at[k],
             came_far.at[k],
-            rz_send.at[k],
-            rz_recv.at[k],
+            far_sem.at[2, k],
+            far_sem.at[3, k],
             expert=partner(z, k, nz),
         )
 
+    def produce(k, source):
+        wait_rows(k, source)
+        part[...] = work(k, source, full[source])
+        outgoing[k] = part[...].astype(BF16)
+        for i in range(3):
+            part_copy(k, i).start()
+        own_part[k] = part[mine]
+
+    def pair_up(k):
+        part_copy(k, 0).wait_recv()
+        kept = outgoing[k, x_rows, first].astype(F32)
+        pairs[k, 0] = (kept + from_y[k, pair_x].astype(F32)).astype(BF16)
+        pair_copy(k, 0).start()
+        part_copy(k, 1).wait_recv()
+        kept = outgoing[k, y_rows, second].astype(F32)
+        pairs[k, 1] = (kept + from_x[k, 1].astype(F32)).astype(BF16)
+        pair_copy(k, 1).start()
+
+    def collect(k):
+        part_copy(k, 2).wait_recv()
+        pair_copy(k, 0).wait_recv()
+        pair_copy(k, 1).wait_recv()
+        own = own_part[k]
+        left = own[:, :half] + from_y[k, pair_mine].astype(F32) + came_pairs[k, 0].astype(F32)
+        right = own[:, half:] + from_x[k, 0].astype(F32) + came_pairs[k, 1].astype(F32)
+        return left, right
+
+    def collect_own():
+        left, right = collect(i32(0))
+        total[:, :half] = left
+        total[:, half:] = right
+
+    def collect_far(k):
+        left, right = collect(k)
+        passed[k, :, first] = left.astype(BF16)
+        passed[k, :, second] = right.astype(BF16)
+        sum_copy(k).start()
+
     full[z, mine] = own_rows
     for k in range(1, nz):
-        far_copy(k).start()
-    for j in range(1, nt):
-        near_copy(0, z, j).start()
+        far_copy(k, z).start()
+    send_rows(0, z)
+    ready()
+    for k in range(1, nz):
+        source = partner(z, i32(k), nz)
+        far_copy(k, source).wait_recv()
+        send_rows(k, source)
+        if k == 1:
+            pass_rows(0, z)
     for move in moves:
         move.start()
-
-    ready()
-
-    def produce(k, source):
-        for j in range(1, nt):
-            near_arrival(k, source, j).wait_recv()
-        part[...] = work(k, source, full[source])
-        outgoing[k] = part[...].astype(BF16)
-        for j in range(1, nt):
-            part_copy(k, j).start()
-        return part[mine]
-
-    def collect(k):
-        out = passed_own[k]
-        for j in range(1, nt):
-            part_copy(k, j).wait_recv()
-            out = out + came_near[k, j].astype(F32)
-        return out
-
-    passed_own = scratch[18]
-    passed_own[0] = produce(i32(0), z)
-    for k in range(1, nz):
-        far_arrival(k).wait_recv()
-        for j in range(1, nt):
-            near_copy(k, partner(z, i32(k), nz), j).start()
+    pass_rows(1, partner(z, i32(1), nz))
 
     def step(k, carry):
-        passed_own[k] = produce(k, partner(z, k, nz))
+        @pl.when(k + 1 < nz)
+        def _():
+            pass_rows(k + 1, partner(z, k + 1, nz))
+
+        turn = lax.rem(k, nz)
+        produce(turn, partner(z, turn, nz))
 
         @pl.when(k >= 2)
         def _():
-            passed[k - 1] = collect(k - 1).astype(BF16)
-            sum_copy(k - 1).start()
+            pair_up(k - 1)
+
+        @pl.when(k >= 3)
+        def _():
+            collect_far(k - 2)
 
         return carry
 
-    lax.fori_loop(1, nz, step, 0)
+    lax.fori_loop(1, nz + 1, step, 0)
     for move in moves:
         move.poll(1)
-    passed[nz - 1] = collect(nz - 1).astype(BF16)
-    sum_copy(i32(nz - 1)).start()
+    collect_far(i32(nz - 1))
+    pair_up(i32(0))
     for move in moves:
         move.poll(2)
-    total[...] = collect(0)
+    collect_own()
     for k in range(1, nz):
         sum_copy(i32(k)).wait_recv()
         total[...] += came_far[k].astype(F32)
 
     def finish():
         for k in range(1, nz):
-            far_copy(k).wait_send()
+            far_copy(k, z).wait_send()
             sum_copy(i32(k)).wait_send()
         for k in range(nz):
             source = partner(z, i32(k), nz)
-            for j in range(1, nt):
-                near_copy(k, source, j).wait_send()
-                part_copy(k, j).wait_send()
+            for j in range(2):
+                row_copy(k, source, j, mine).wait_send()
+                on_copy(k, source, j, (y_rows, x_rows)[j]).wait_send()
+                pair_copy(k, j).wait_send()
+            for i in range(3):
+                part_copy(k, i).wait_send()
 
     return finish
 
@@ -628,14 +686,45 @@
     b_ref[...] = (unit_rows(h1)[0] * g_moe).astype(BF16)
 
 
+def fill_tables(tabs, lengths, m):
+    block, size = tabs.shape[2:]
+    row = lax.broadcasted_iota(jnp.int32, (block, size), 0)
+    lane = lax.broadcasted_iota(jnp.int32, (block, size), 1)
+    begin, segment, segment_of_lane = (jnp.zeros((block, size), jnp.int32) for _ in range(3))
+    end = jnp.int32(0)
+    for n in range(lengths.shape[1]):
+        end = end + lengths[m, n]
+        begin = jnp.where(row >= end, end, begin)
+        segment = segment + jnp.where(row >= end, 1, 0)
+        segment_of_lane = segment_of_lane + jnp.where(lane >= end, 1, 0)
+    half = size // 2
+    position = jnp.where(lane >= half, lane - half, lane).astype(F32)
+    inverse = jnp.exp(position * (-2.0 * math.log(THETA) / size))
+    angle = (row - begin).astype(F32) * inverse
+    sin = jnp.sin(angle)
+    tabs[m, 0] = jnp.cos(angle)
+    tabs[m, 1] = jnp.where(lane >= half, sin, -sin)
+    tabs[m, 2] = jnp.where((lane <= row) & (segment == segment_of_lane), 0.0, -1e30)
+
+
+def fill_gates(gates, ids, route_weights, m):
+    expert_of, weight_of = ids[m], route_weights[m]
+    lane = lax.broadcasted_iota(jnp.int32, gates.shape[1:], 1)
+    out = jnp.zeros(gates.shape[1:], F32)
+    for c in range(expert_of.shape[1]):
+        out = out + jnp.where(lane == expert_of[:, c : c + 1], weight_of[:, c : c + 1], 0.0)
+    gates[m] = out
+
+
 def start_attend_kernel(nz, nt, heads, relay, ins, outs, scratch):
     s, z, t = lax.axis_index("section"), lax.axis_index("expert"), lax.axis_index("tensor")
-    boundary, tabs, gates, gains, wq, wk, wv, wo, wg, wu, wd = ins
+    lengths, ids, route_weights, boundary, gains, wq, wk, wv, wo, wg, wu, wd = ins
     edges, tabs_out, gates_out, gains_out = outs[:4]
     gathered, (sg, su, sd), results = outs[4:8], outs[8:11], outs[11:]
-    x_s, tabs_s, gains_s, w_sem, in_sem, own_sem, sib_send, sib_recv, gate_send, gate_recv = scratch[:10]
-    relay.bind((wq, wk, wv, wo), gathered, scratch[10:17])
-    attn_scratch = scratch[17:]
+    x_s, tabs_s, gains_s, tabs, gates = scratch[:5]
+    w_sem, in_sem, own_sem, sib_send, sib_recv, gate_send, gate_recv = scratch[5:12]
+    relay.bind((wq, wk, wv, wo), gathered, scratch[12:19])
+    attn_scratch = scratch[19:]
     other = 1 - s
     i32 = jnp.int32
 
@@ -645,8 +734,8 @@
         pltpu.make_async_copy(gains, gains_out.at[s], own_sem.at[2]),
         pltpu.make_async_copy(gates.at[s], gates_out.at[s, z], own_sem.at[3]),
     ]
-    for copy in own:
-        copy.start()
+    own[0].start()
+    own[2].start()
     greet(all_peers(s, z, t, nz, nt))
 
     def sibling(i, src, dst):
@@ -660,7 +749,7 @@
         (wu, su, su),
         (wd, sd, sd),
     ]
-    for i in range(3):
+    for i in (0, 2):
         sibling(i, *pairs[i][:2]).start()
     for a in range(3):
         relay.begin(a)
@@ -686,6 +775,13 @@
             expert=zz,
         )
 
+    for m in range(2):
+        fill_tables(tabs, lengths, m)
+    sibling(1, *pairs[1][:2]).start()
+    own[1].start()
+    for m in range(2):
+        fill_gates(gates, ids, route_weights, m)
+    own[3].start()
     turns = [(d, k) for d in range(2) for k in range(nz) if d or k]
     for d, k in turns:
         gate_copy(d, k).start()
@@ -748,37 +844,31 @@
         relay.end(a)
 
 
-def attend_kernel(layer, nz, nt, heads, relay, ins, outs, scratch):
+def attend_kernel(layer, nz, nt, heads, bind, ins, outs, scratch):
     s, z, t = lax.axis_index("section"), lax.axis_index("expert"), lax.axis_index("tensor")
-    x_ref, tabs, gains, wq, wk, wv, wo = ins
-    w_sem = scratch[0]
-    relay.bind((wo,), outs[:1], scratch[1:8])
-    attn_scratch = scratch[8:]
+    x_ref, tabs, gains, wq, wk, wv, wo = ins[:7]
+    w_sem, attn_scratch, rest = scratch[0], scratch[1:10], scratch[10:]
+    moves = bind(ins[7:], outs[9:], rest)
     loads = [
         pltpu.make_async_copy(src, dst, w_sem.at[i])
-        for i, (src, dst) in enumerate(zip((wq, wk, wv, outs[0]), attn_scratch))
+        for i, (src, dst) in enumerate(zip((wq, wk, wv, wo), attn_scratch))
     ]
-    for load in loads[:3]:
+    for load in loads:
         load.start()
     greet(all_peers(s, z, t, nz, nt))
-    relay.begin(0)
+    for move in moves:
+        move.start()
 
     def wait_qkv():
         for load in loads[:3]:
             load.wait()
 
-    def wait_out():
-        for k in range(1, nz):
-            relay.step(0, k)
-        relay.settle(0)
-        loads[3].start()
-        loads[3].wait()
-
     tables = (tabs[layer, 0], tabs[layer, 1], tabs[layer, 2])
     attend_body(
-        t, nt, heads, x_ref, tables, gains[layer], outs[1:], attn_scratch, wait_qkv, wait_out
+        t, nt, heads, x_ref, tables, gains[layer], outs[:9], attn_scratch, wait_qkv, loads[3].wait
     )
-    relay.end(0)
+    for move in moves:
+        move.finish()
 
 
 def load_experts(layer, s, own, sibling, scratch, sems):
@@ -802,8 +892,8 @@
     s, z, t = lax.axis_index("section"), lax.axis_index("expert"), lax.axis_index("tensor")
     b_ref, h1_ref, gates, wg, wu, wd, sg, su, sd = ins[:9]
     y_ref, b_out, g_out, u_out = outs[:4]
-    wg_s, wu_s, wd_s, g_s, u_s, w_sem, o_sem, own_part = scratch[:8]
-    spaces, rest = list(scratch[8:26]) + [own_part], scratch[26:]
+    wg_s, wu_s, wd_s, g_s, u_s, w_sem, o_sem = scratch[:7]
+    spaces, rest = scratch[7 : 7 + EXCHANGE_SCRATCH], scratch[7 + EXCHANGE_SCRATCH :]
     moves = bind(ins[9:], outs[4:], rest)
     rows = b_ref.shape[0]
     loads = load_experts(layer, s, (wg, wu, wd), (sg, su, sd), (wg_s, wu_s, wd_s), w_sem)
@@ -824,7 +914,7 @@
         return dot(hidden, wd_s[...])
 
     finish = exchange(z, t, nz, nt, rows, b_ref[...], spaces, ready, work, moves)
-    full, total, whole = spaces[0], spaces[6], spaces[7]
+    full, total, whole, spread_sem = spaces[0], spaces[10], spaces[11], spaces[15]
     saves = [
         pltpu.make_async_copy(full, b_out, o_sem.at[0]),
         pltpu.make_async_copy(g_s, g_out, o_sem.at[1]),
@@ -833,7 +923,7 @@
     for save in saves:
         save.start()
     whole[rows_at(t * rows, rows)] = (h1_ref[...] + total[...]).astype(BF16)
-    wait = spread_rows(t, nt, rows, whole, spaces[16], spaces[17])
+    wait = spread_rows(t, nt, rows, whole, spread_sem.at[0], spread_sem.at[1])
     finish()
     wait()
     y_ref[...] = whole[...]
@@ -847,14 +937,14 @@
     s, z, t = lax.axis_index("section"), lax.axis_index("expert"), lax.axis_index("tensor")
     dy_ref, h1_ref, gains, gates, g_in, u_in, wg, wu, wd, sg, su, sd = ins[:12]
     dat_ref, dh1_ref, term_ref, dy_out, hid_out, dg_out, du_out = outs[:7]
-    wg_s, wu_s, wd_s, g_s, u_s, hid_s, dg_s, du_s, w_sem, g_sem, u_sem, o_sem, own_part = scratch[:13]
-    spaces, rest = list(scratch[13:31]) + [own_part], scratch[31:]
+    wg_s, wu_s, wd_s, g_s, u_s, hid_s, dg_s, du_s, w_sem, g_sem, u_sem, o_sem = scratch[:12]
+    spaces, rest = scratch[12 : 12 + EXCHANGE_SCRATCH], scratch[12 + EXCHANGE_SCRATCH :]
     moves = bind(ins[12:], outs[7:], rest)
     rows, model_width = dy_ref.shape
     loads = load_experts(layer, s, (wd, wg, wu), (sd, sg, su), (wd_s, wg_s, wu_s), w_sem)
 
     def kept(k):
-        origin, slot = partner(z, k, nz), lax.rem(k, 2)
+        origin, slot = partner(z, lax.rem(k + 1, nz), nz), lax.rem(k, 2)
         return (
             pltpu.make_async_copy(g_in.at[origin], g_s.at[slot], g_sem.at[slot]),
             pltpu.make_async_copy(u_in.at[origin], u_s.at[slot], u_sem.at[slot]),
@@ -870,15 +960,16 @@
             load.wait()
 
     def work(k, origin, rows_in):
-        for load in kept(k):
+        turn = lax.rem(k + nz - 1, nz)
+        for load in kept(turn):
             load.wait()
 
-        @pl.when(k + 1 < nz)
-        def _():
-            for load in kept(k + 1):
+        @pl.when(turn + 1 < nz)
+        def _():
+            for load in kept(turn + 1):
                 load.start()
 
-        slot = lax.rem(k, 2)
+        slot = lax.rem(turn, 2)
         gate_pre, up_pre = g_s[slot], u_s[slot]
         weight = expert_gates(gates[layer, origin], z * local_experts, local_experts, width)
         sigmoid = jax.nn.sigmoid(gate_pre)
@@ -890,7 +981,7 @@
         return dot(dg_s[origin], wg_s[...]) + dot(du_s[origin], wu_s[...])
 
     finish = exchange(z, t, nz, nt, rows, dy_ref[...], spaces, ready, work, moves)
-    full, total, whole = spaces[0], spaces[6], spaces[7]
+    full, total, whole, spread_sem = spaces[0], spaces[10], spaces[11], spaces[15]
     saves = [
         pltpu.make_async_copy(full, dy_out, o_sem.at[0]),
         pltpu.make_async_copy(hid_s, hid_out, o_sem.at[1]),
@@ -906,7 +997,7 @@
     dh1_ref[...] = dh1
     term_ref[...] = term
     whole[rows_at(t * rows, rows)] = dh1.astype(BF16)
-    wait = spread_rows(t, nt, rows, whole, spaces[16], spaces[17])
+    wait = spread_rows(t, nt, rows, whole, spread_sem.at[0], spread_sem.at[1])
     finish()
     wait()
     dat_ref[...] = whole[...]
@@ -1102,36 +1193,45 @@
         pltpu.make_async_copy(stage.at[slot], outs[0].at[pl.ds(0, step)], out_sem.at[slot]).wait()
 
 
-def attend_grads_kernel(q_cols, size, ins, outs, scratch):
-    s = lax.axis_index("section")
-    spaces, sems = scratch[:4], scratch[4]
-
-    def loads(layer):
-        refs = ins[4 * layer : 4 * layer + 4]
+def attend_grads_kernel(nz, q_cols, size, ins, outs, scratch):
+    s, z = lax.axis_index("section"), lax.axis_index("expert")
+    spaces, sems, d_sem = scratch[:4], scratch[4], scratch[5]
+    a_s, o_s, t_s, d_s = spaces
+    early, blocks, late = ins[:3], ins[3 : 3 + nz], ins[3 + nz :]
+
+    def loads(refs):
         return [pltpu.make_async_copy(r, d, sems.at[i]) for i, (r, d) in enumerate(zip(refs, spaces))]
 
-    for layer in range(2):
+    def parts(layer):
+        out = []
+        for k in range(nz):
+            spot = partner(z, jnp.int32(k), nz)
+            src = blocks[k] if layer == 0 else late[3].at[:, spot]
+            out.append(pltpu.make_async_copy(src, d_s.at[:, spot], d_sem.at[k]))
+        return out
+
+    for layer, refs in enumerate((early, late[:3])):
 
         @pl.when(s == layer)
         def _():
-            for load in loads(layer):
+            for load in loads(refs) + parts(layer):
                 load.start()
 
-    waits = loads(0)
-    a_s, d_s, o_s, t_s = spaces
+    waits = loads(early)
 
     def flat(ref):
         return ref[...].reshape(-1, ref.shape[-1])
 
+    waits[1].wait()
+    waits[2].wait()
+    outs[3][...] = dot_tn(flat(o_s), flat(t_s))
     waits[0].wait()
-    waits[1].wait()
+    for load in parts(0):
+        load.wait()
     grad = dot_tn(flat(a_s), flat(d_s))
     outs[0][...] = grad[:, :q_cols]
     outs[1][...] = grad[:, q_cols : q_cols + size]
     outs[2][...] = grad[:, q_cols + size :]
-    waits[2].wait()
-    waits[3].wait()
-    outs[3][...] = dot_tn(flat(o_s), flat(t_s))
 
 
 def shape_of(shape, dtype):
@@ -1165,28 +1265,6 @@
 
 def any_place(*values):
     return [(value, ANY) for value in values]
-
-
-def block_tables(lengths, block, size):
-    ends = jnp.cumsum(lengths)
-    starts = ends - lengths
-    places = jnp.arange(block, dtype=jnp.int32)
-    segment = jnp.sum((places[:, None] >= ends[None, :]).astype(jnp.int32), axis=1)
-    numbers = jnp.arange(lengths.shape[0], dtype=jnp.int32)
-    offset = jnp.sum(jnp.where(segment[:, None] == numbers[None, :], starts[None, :], 0), axis=1)
-    half = jnp.arange(size // 2, dtype=F32)
-    inverse = jnp.exp(half * (-2.0 * math.log(THETA) / size))
-    angle = (places - offset).astype(F32)[:, None] * inverse[None, :]
-    cos, sin = jnp.cos(angle), jnp.sin(angle)
-    allowed = (places[None, :] <= places[:, None]) & (segment[:, None] == segment[None, :])
-    bias = jnp.where(allowed, 0.0, -1e30).astype(F32)
-    return jnp.stack(
-        [
-            jnp.concatenate([cos, cos], axis=-1),
-            jnp.concatenate([-sin, sin], axis=-1),
-            bias,
-        ]
-    )
 
 
 def on_device(
@@ -1202,14 +1280,9 @@
     experts = local_experts * nz
     rows = block // nt
     q_cols = heads * size
-    assert micro == 2 and key_weight.shape[2] == size and experts <= LANES
+    assert micro == 2 and key_weight.shape[2] == size == block and experts <= LANES
     dma = pltpu.SemaphoreType.DMA
 
-    tabs = jax.vmap(lambda lengths: block_tables(lengths, block, size))(seq_lengths[0, :, 0])
-    lanes = jnp.arange(LANES, dtype=jnp.int32)
-    gates = jnp.sum(
-        jnp.where(expert_ids[0][..., None] == lanes, route_weights[0][..., None], 0.0), axis=2
-    )
     wg, wu, wd = (w[0].reshape(hidden, width) for w in (w_gate, w_up, w_down))
     wq, wk, wv, wo = w_query[0], key_weight[0], value_weight[0], w_output[0]
     gains = jnp.concatenate([attn_gain, moe_gain, query_gain, key_norm_gain], axis=1)
@@ -1242,15 +1315,39 @@
         shape_of((block, size), BF16),
         shape_of((block, q_cols), BF16),
     )
-    own_part = pltpu.VMEM((nz, rows, width), F32)
     expert_scratch = [pltpu.VMEM((hidden, width), BF16)] * 3
+
+    def binder(kinds):
+        def bind(ins, outs, scratch):
+            return [
+                kind.bind(ins[i] if i < len(ins) else None, outs[i], scratch[3 * i : 3 * i + 3])
+                for i, kind in enumerate(kinds)
+            ]
+
+        return bind
+
+    def shapes_of(kinds, values):
+        out = []
+        for kind, value in zip(kinds, values):
+            if isinstance(kind, Near):
+                out.append(like(value, (2,) if kind.both else ()))
+            elif kind.sliced:
+                out.append(shape_of((2, nz, block, width // nz), value.dtype))
+            else:
+                out.append(like(value, (2, nz)))
+        return out
+
+    def scratch_of(kinds):
+        return [sem for kind in kinds for sem in kind.scratch()]
 
     relay = Relay(0, (0, 0, 0, 1), nz)
     started = call(
         functools.partial(start_attend_kernel, nz, nt, heads, relay),
         "start_attend_0",
         0,
-        any_place(boundary[0], tabs, gates, gains, wq, wk, wv, wo, wg, wu, wd),
+        [(seq_lengths[0, :, 0], SM)]
+        + vm(expert_ids[0], route_weights[0])
+        + any_place(boundary[0], gains, wq, wk, wv, wo, wg, wu, wd),
         any_place(
             shape_of((2, block, width), BF16),
             shape_of((2, 3, block, size), F32),
@@ -1264,6 +1361,8 @@
             pltpu.VMEM((block, width), BF16),
             pltpu.VMEM((3, block, size), F32),
             pltpu.VMEM(gains.shape, F32),
+            pltpu.VMEM((2, 3, block, size), F32),
+            pltpu.VMEM((2, block, LANES), F32),
             dma((4,)), dma((3,)), dma((4,)), dma((6,)), dma((6,)), dma((2, nz)), dma((2, nz)),
         ]
         + relay.scratch(4)
@@ -1289,7 +1388,7 @@
             ),
             expert_scratch
             + [pltpu.VMEM((nz, block, hidden), F32)] * 2
-            + [dma((3,)), dma((3,)), own_part]
+            + [dma((3,)), dma((3,))]
             + exchange_scratch(nz, nt, rows, block, width)
             + move_scratch,
         )
@@ -1316,70 +1415,48 @@
             expert_scratch
             + [pltpu.VMEM((2, block, hidden), F32)] * 2
             + [pltpu.VMEM((nz, block, hidden), BF16)] * 3
-            + [dma((3,)), dma((2,)), dma((2,)), dma((4,)), own_part]
+            + [dma((3,)), dma((2,)), dma((2,)), dma((4,))]
             + exchange_scratch(nz, nt, rows, block, width)
             + move_scratch,
         )
 
-    def binder(kinds):
-        def bind(ins, outs, scratch):
-            return [
-                kind.bind(ins[i] if i < len(ins) else None, outs[i], scratch[3 * i : 3 * i + 3])
-                for i, kind in enumerate(kinds)
-            ]
-
-        return bind
-
-    def shapes_of(kinds, values):
-        out = []
-        for kind, value in zip(kinds, values):
-            if isinstance(kind, Near):
-                out.append(like(value, (2,) if kind.both else ()))
-            elif kind.sliced:
-                out.append(shape_of((2, nz, block, width // nz), value.dtype))
-            else:
-                out.append(like(value, (2, nz)))
-        return out
-
-    def scratch_of(kinds):
-        return [sem for kind in kinds for sem in kind.scratch()]
-
-    qkv = Relay(1, (0, 0, 0), nz)
+    relay_1 = Relay(1, (0, 0, 0, 1), nz)
     ran = run_experts(
-        0, b_0, h1_0, (wq, wk, wv), gathered[:3], qkv.scratch(3),
-        lambda ins, outs, scratch: [qkv.bind(ins, outs, scratch)],
+        0, b_0, h1_0, (wq, wk, wv, wo), gathered, relay_1.scratch(4),
+        lambda ins, outs, scratch: [relay_1.bind(ins, outs, scratch)],
     )
     x_1, ball_0, gp_0, up_0 = ran[:4]
-    qkv_1 = ran[4:]
-
-    relay_1 = Relay(1, (1,), nz)
+    weights_1 = tuple(ran[4:])
+
+    kinds = (Gather(0, nz, True),)
+    values = (a_0,)
     attended = call(
-        functools.partial(attend_kernel, 1, nz, nt, heads, relay_1),
+        functools.partial(attend_kernel, 1, nz, nt, heads, binder(kinds)),
         "attend_1",
         5,
-        vm(x_1, tabs_all, gains_all) + any_place(*qkv_1, wo),
-        any_place(gathered[3]) + attend_outs,
-        [dma((4,))] + relay_1.scratch(1) + spaces,
+        vm(x_1, tabs_all, gains_all) + any_place(*weights_1, *values),
+        attend_outs + any_place(*shapes_of(kinds, values)),
+        [dma((4,))] + spaces + scratch_of(kinds),
     )
-    weights_1 = tuple(qkv_1) + (attended[0],)
-    h1_1, b_1, a_1, q_1, k_1, v_1, qr_1, kr_1, o_1 = attended[1:]
-
-    kinds = (Gather(0, nz), Gather(0, nz, True), Near(0))
-    values = (o_0, a_0, ball_0)
+    h1_1, b_1, a_1, q_1, k_1, v_1, qr_1, kr_1, o_1 = attended[:9]
+    aall_0 = attended[9]
+
+    kinds = (Gather(0, nz), Near(0))
+    values = (o_0, ball_0)
     ran = run_experts(
         1, b_1, h1_1, values, shapes_of(kinds, values), scratch_of(kinds), binder(kinds)
     )
     y_1, ball_1, gp_1, up_1 = ran[:4]
-    oall_0, aall_0, bnear_0 = ran[4:]
+    oall_0, bnear_0 = ran[4:]
 
     dy_1 = lax.dynamic_slice_in_dim(edges[1], lax.axis_index("tensor") * rows, rows, 0)
-    kinds = (Gather(1, nz), Gather(1, nz, True), Near(1), Near(1, True))
-    values = (o_1, a_1, ball_1, y_1)
+    kinds = (Gather(1, nz), Near(1), Near(1, True))
+    values = (o_1, ball_1, y_1)
     ran = experts_back(
         1, dy_1, h1_1, gp_1, up_1, values, shapes_of(kinds, values), scratch_of(kinds), binder(kinds)
     )
     dat_1, dh1_1, tm_1, dyall_1, hid_1, dg_1, du_1 = ran[:7]
-    oall_1, aall_1, bnear_1, ends_1 = ran[7:]
+    oall_1, bnear_1, ends_1 = ran[7:]
 
     def attend_back(layer, x, source, dat, dh1, term_moe, kept, weights, kinds, values, late):
         outs = vm(
@@ -1402,7 +1479,7 @@
                 dma((nt,)),
             ]
             ins += any_place(late)
-            last = (Gather(0, nz), Near(0, True), Gather(0, nz))
+            last = (Near(0, True), Near(0, True), Gather(0, nz))
             late_shapes = shapes_of(last, (shapes[1], shape_of((block, width), BF16), shapes[2]))
             kinds = kinds + last
         return call(
@@ -1414,13 +1491,13 @@
             scratch + scratch_of(kinds),
         )
 
-    kinds = (Gather(1, nz, True), Near(1), Near(1), Near(1), Near(1))
-    values = (dat_1, dg_1, du_1, hid_1, dyall_1)
+    kinds = (Gather(1, nz, True), Near(1), Near(1), Near(1), Near(1), Gather(1, nz, True))
+    values = (dat_1, dg_1, du_1, hid_1, dyall_1, a_1)
     ran = attend_back(
         1, x_1[None], 0, dat_1, dh1_1, tm_1, (q_1, k_1, v_1, qr_1, kr_1), weights_1, kinds, values, None
     )
     dx_1, dqkv_1, terms_1 = ran[:3]
-    datall_1, near_1 = ran[3], ran[4:8]
+    datall_1, near_1, aall_1 = ran[3], ran[4:8], ran[8]
 
     kinds = (Gather(1, nz), Gather(1, nz))
     values = (dqkv_1, terms_1)
@@ -1436,7 +1513,11 @@
         0, edges, 0, dat_0, dh1_0, tm_0, (q_0, k_0, v_0, qr_0, kr_0), weights_0, kinds, values, termsall_1
     )
     terms, datall_0, near_0 = ran[3], ran[4], ran[5:9]
-    dqkvall_0, ends_0 = ran[9:11]
+    dqkv_both, ends_0 = ran[9:11]
+    dqkv_0 = [dqkv_both]
+    for k in range(1, nz):
+        pairs = [(place, place ^ k) for place in range(nz)]
+        dqkv_0.append(lax.ppermute(dqkv_both, ("section", "expert"), pairs))
 
     step = 256
     flat = shape_of((hidden, width), F32)
@@ -1459,9 +1540,9 @@
             dma((2,)),
         ],
     )
-    operands = (aall_0, dqkvall_0, oall_0, datall_0, aall_1, dqkvall_1, oall_1, datall_1)
+    operands = (aall_0, oall_0, datall_0, *dqkv_0, aall_1, oall_1, datall_1, dqkvall_1)
     grad_query, grad_key, grad_value, grad_output = call(
-        functools.partial(attend_grads_kernel, q_cols, size),
+        functools.partial(attend_grads_kernel, nz, q_cols, size),
         "attend_grads",
         None,
         any_place(*operands),
@@ -1471,7 +1552,7 @@
             shape_of(wv.shape, F32),
             shape_of(wo.shape, F32),
         ),
-        [pltpu.VMEM(o.shape, o.dtype) for o in operands[:4]] + [dma((4,))],
+        [pltpu.VMEM(o.shape, o.dtype) for o in operands[-4:]] + [dma((3,)), dma((nz,))],
     )
     ends = jnp.where(lax.axis_index("section") == 0, ends_0, ends_1)
     return (

time: 586 us -> 541 us (0.923)
  Pallas kernels: 569 us -> 507 us
  starting transfers between devices: 0 us -> 10.4 us
    pallas_call x10, Pallas kernels: 569 us -> 507 us  [call(): pl.pallas_call(kernel, out_shape=tuple((o for o, _ in outs)), in_specs=[s...]
    ppermute x0 -> x3, starting transfers between devices: none -> 10.4 us  [on_device(): dqkv_0.append(lax.ppermute(dqkv_both, ('section', 'expert'), pairs))]
  transfers between devices with their start and end apart: 0 -> 3, of which waited for: 0 -> 1; matrix products, arithmetic and copies ran while one was open for 0% -> 1% of each run, Pallas kernels for 0% -> 3%
where the time goes in v3:
time: 541 us; the launch traced here: 534 us
  Pallas kernels  507 us (94%)
  starting transfers between devices  10.4 us (2%)
  local copies, waits for them, and re-layouts  8.91 us (2%)
    pallas_call x10, Pallas kernels, call(): pl.pallas_call(kernel, out_shape=tuple((o for o, _ in outs)), in_specs=[s...  507 us
  transfers between devices with their start and end apart: 3, of which 1 were waited for; matrix products, arithmetic and copies ran while one was open for 1% of the time, Pallas kernels for 3%

profile of v3, /device:TPU:0, one launch (start us, length us, event | category | flops | bytes accessed | tf_op | source)
XLA Modules:
  0.0 533.7 jit_solution(18079490838680364917)
XLA Ops:
  0.6 1.5 copy.27
  2.1 1.5 copy.28
  3.6 1.4 pad_maximum_fusion.refs_4_
  5.0 108.3 %start_attend_0.1 = (bf16[2,128,2048]{2,1,0:T(8,128)(2,1)}, f32[2,3,128,128]{3,2,1,0:T(8,128)}, f32[2,4,128,128]{3,2,1,0:T(8,128)}, f32[2,1,4352]{2,1,0:T(1,128)...) custom-call(s32[2,4]{1,0:T(2,128)} %bitcast.60, ...), custom_call_target="tpu_custom_call" | custom-call | tf_op jit(solution)/shard_map/start_attend_0/pallas_call | solution.py:1249
  113.3 1.1 slice.15
  114.4 0.7 dynamic-slice_bitcast_fusion.refs_0_
  115.0 108.8 %experts_0.1 = (bf16[128,2048]{1,0:T(8,128)(2,1)}, bf16[4,128,2048]{2,1,0:T(8,128)(2,1)}, f32[4,128,768]{2,1,0:T(8,128)}, f32[4,128,768]{2,1,0:T(8,128)}, bf16[2...) custom-call(bf16[32,2048]{1,0:T(8,128)(2,1)} %get-tuple-element.102.re, ...), custom_call_target="tpu_custom_call" | custom-call | tf_op jit(solution)/shard_map/experts_0/pallas_call | solution.py:1249
  223.8 16.4 %attend_1.1 = (f32[32,2048]{1,0:T(8,128)}, bf16[32,2048]{1,0:T(8,128)(2,1)}, bf16[128,2048]{1,0:T(8,128)(2,1)}, f32[128,1024]{1,0:T(8,128)}, f32[128,128]{1,0:T(...) custom-call(bf16[128,2048]{1,0:T(8,128)(2,1)} %get-tuple-element.108, ...), custom_call_target="tpu_custom_call" | custom-call | tf_op jit(solution)/shard_map/attend_1/pallas_call | solution.py:1249
  240.3 59.2 %experts_1.1 = (bf16[128,2048]{1,0:T(8,128)(2,1)}, bf16[4,128,2048]{2,1,0:T(8,128)(2,1)}, f32[4,128,768]{2,1,0:T(8,128)}, f32[4,128,768]{2,1,0:T(8,128)}, bf16[2...) custom-call(bf16[32,2048]{1,0:T(8,128)(2,1)} %get-tuple-element.115.refs_0_, ...), custom_call_target="tpu_custom_call" | custom-call | tf_op jit(solution)/shard_map/experts_1/pallas_call | solution.py:1249
  299.5 60.8 %experts_back_1.1 = (bf16[128,2048]{1,0:T(8,128)(2,1)}, f32[32,2048]{1,0:T(8,128)}, f32[1,2048]{1,0:T(1,128)}, bf16[4,128,2048]{2,1,0:T(8,128)(2,1)}, bf16[4,128...) custom-call(bf16[32,2048]{1,0:T(8,128)(2,1)} %dynamic-slice_bitcast_, ...), custom_call_target="tpu_custom_call" | custom-call | tf_op jit(solution)/shard_map/experts_back_1/pallas_call | solution.py:1249
  360.3 24.0 %attend_back_1.1 = (bf16[32,2048]{1,0:T(8,128)(2,1)}, bf16[128,1280]{1,0:T(8,128)(2,1)}, f32[24,256]{1,0:T(8,128)}, bf16[2,4,128,512]{3,2,1,0:T(8,128)(2,1)}, bf...) custom-call(bf16[1,128,2048]{2,1,0:T(8,128)(2,1)} %bitcast.50, ...), custom_call_target="tpu_custom_call" | custom-call | tf_op jit(solution)/shard_map/attend_back_1/pallas_call | solution.py:1249
  384.3 72.5 %experts_back_0.1 = (bf16[128,2048]{1,0:T(8,128)(2,1)}, f32[32,2048]{1,0:T(8,128)}, f32[1,2048]{1,0:T(1,128)}, bf16[4,128,2048]{2,1,0:T(8,128)(2,1)}, bf16[4,128...) custom-call(bf16[32,2048]{1,0:T(8,128)(2,1)} %get-tuple-element.136., ...), custom_call_target="tpu_custom_call" | custom-call | tf_op jit(solution)/shard_map/experts_back_0/pallas_call | solution.py:1249
  456.9 34.3 %attend_back_0.1 = (bf16[32,2048]{1,0:T(8,128)(2,1)}, bf16[128,1280]{1,0:T(8,128)(2,1)}, f32[24,256]{1,0:T(8,128)}, f32[24,256]{1,0:T(8,128)}, bf16[2,4,128,512]...) custom-call(bf16[2,128,2048]{2,1,0:T(8,128)(2,1)} %get-tuple-element, ...), custom_call_target="tpu_custom_call" | custom-call | tf_op jit(solution)/shard_map/attend_back_0/pallas_call | solution.py:1249
  491.1 3.4 collective-permute-start.2
  494.5 2.5 collective-permute-start.1
  497.0 4.5 collective-permute-start
  501.5 0.7 slice_bitcast_fusion
  502.2 0.6 copy.30
  502.9 0.6 copy.29
  503.5 0.0 copy-start
  503.5 15.9 %expert_grads.1 = (f32[768,2048]{1,0:T(8,128)}, f32[768,2048]{1,0:T(8,128)}, f32[768,2048]{1,0:T(8,128)}) custom-call(bf16[4,128,768]{2,1,0:T(8,128)(2,1)} %get-tuple-element.154.refs_17_.refs_0_, bf16[4,128,768]{2,1,0:T(8,128)(2,1)} %get-tuple-element.155.refs_18_.refs_1_, bf16[4,128,768]{2,1,0:T(8,128)(2,1)} %get-tuple-element.156.refs_19_.refs_2_, ...), custom_call_target="tpu_custom_call" | custom-call | tf_op jit(solution)/shard_map/expert_grads/pallas_call | solution.py:1249
  519.3 1.2 fusion
  520.5 0.0 copy-done
  520.5 0.0 copy-done.1
  520.5 1.1 select_bitcast_fusion
  521.6 0.0 collective-permute-done.2.refs_6_
  521.6 3.3 collective-permute-done.1.refs_5_
  524.9 0.0 collective-permute-done.refs_4_
  524.9 0.0 copy-done.2
  524.9 0.8 copy-done.3
  525.7 0.2 copy-done.4
  525.9 7.3 %attend_grads.1 = (f32[512,1024]{1,0:T(8,128)}, f32[512,128]{1,0:T(8,128)}, f32[512,128]{1,0:T(8,128)}, f32[1024,512]{1,0:T(8,128)}) custom-call(bf16[2,4,128,512]{3,2,1,0:T(8,128)(2,1)} %get-tuple-element.161.refs_0_, bf16[2,4,128,1024]{3,2,1,0:T(8,128)(2,1)} %get-tuple-element.162.refs_1_, bf16[2,4,128,512]{3,2,1,0:T(8,128)(2,1)} %get-tuple-element.163.refs_2_, ...), custom_call_target="tpu_custom_call" | custom-call | tf_op jit(solution)/shard_map/attend_grads/pallas_call | solution.py:1249
  (4 shorter events, 0.0 us)
Async XLA Ops:
  491.1 30.5 %collective-permute-start.2 = (bf16[2,128,1280]{2,1,0:T(8,128)(2,1)}, bf16[2,128,1280]{2,1,0:T(8,128)(2,1)S(1)}, u32[]{:S(2)}, u32[]{:S(2)}) collective-permute-start(bf16[2,128,1280]{2,1,0:T(8,128)(2,1)} %get-tuple-element.164.refs_3_), channel_id=1, source_target_pairs={{0,12},{4,8},{8,4},{12,0},{1,13},{5,9},{9,5},{13,1},{2,14},{6,10},... | collective-permute-start | bytes 1966088 | tf_op jit(solution)/shard_map/ppermute | solution.py:1520
  494.5 30.4 %collective-permute-start.1 = (bf16[2,128,1280]{2,1,0:T(8,128)(2,1)}, bf16[2,128,1280]{2,1,0:T(8,128)(2,1)S(1)}, u32[]{:S(2)}, u32[]{:S(2)}) collective-permute-start(bf16[2,128,1280]{2,1,0:T(8,128)(2,1)} %get-tuple-element.164.refs_3_), channel_id=1, source_target_pairs={{0,8},{4,12},{8,0},{12,4},{1,9},{5,13},{9,1},{13,5},{2,10},{6,14},... | collective-permute-start | bytes 1966088 | tf_op jit(solution)/shard_map/ppermute | solution.py:1520
  497.0 27.9 %collective-permute-start = (bf16[2,128,1280]{2,1,0:T(8,128)(2,1)}, bf16[2,128,1280]{2,1,0:T(8,128)(2,1)S(1)}, u32[]{:S(2)}, u32[]{:S(2)}) collective-permute-start(bf16[2,128,1280]{2,1,0:T(8,128)(2,1)} %get-tuple-element.164.refs_3_), channel_id=1, source_target_pairs={{0,4},{4,0},{8,12},{12,8},{1,5},{5,1},{9,13},{13,9},{2,6},{6,2},{1... | collective-permute-start | bytes 1966088 | tf_op jit(solution)/shard_map/ppermute | solution.py:1520
  503.5 17.1 %copy-start = (bf16[2,128,2048]{2,1,0:T(8,128)(2,1)S(1)}, bf16[2,128,2048]{2,1,0:T(8,128)(2,1)}, u32[]{:S(2)}) copy-start(bf16[2,128,2048]{2,1,0:T(8,128)(2,1)} %get-tuple-element.159) | copy-start | bytes 3145732
  503.5 17.1 %copy-start.1 = (bf16[2,128,2048]{2,1,0:T(8,128)(2,1)S(1)}, bf16[2,128,2048]{2,1,0:T(8,128)(2,1)}, u32[]{:S(2)}) copy-start(bf16[2,128,2048]{2,1,0:T(8,128)(2,1)} %get-tuple-element.158) | copy-start | bytes 3145732
  521.6 3.3 copy-start.2
  524.9 0.8 copy-start.3
  524.9 1.0 copy-start.4

commit v4 on v3

--- a/solution.py
+++ b/solution.py
@@ -16,7 +16,7 @@
 MESH = pl.DeviceIdType.MESH
 F32 = jnp.float32
 BF16 = jnp.bfloat16
-VMEM_LIMIT = 60 * 1024 * 1024
+VMEM_LIMIT = 62 * 1024 * 1024
 
 ANY = pl.BlockSpec(memory_space=pl.ANY)
 VM = pl.BlockSpec(memory_space=pltpu.VMEM)
@@ -100,210 +100,278 @@
         terms_ref[row + i : row + i + 1, :] = vector[:, i * TERM_COLS : (i + 1) * TERM_COLS]
 
 
-def exchange_scratch(nz, nt, rows, block, width):
-    dma = pltpu.SemaphoreType.DMA
-    half = width // 2
-    return [
-        pltpu.VMEM((nz, block, width), BF16),
-        pltpu.VMEM((nz, block, width), BF16),
-        pltpu.VMEM((block, width), F32),
-        pltpu.VMEM((nz, 2 * rows, half), BF16),
-        pltpu.VMEM((nz, 2, rows, half), BF16),
-        pltpu.VMEM((nz, 2, rows, half), BF16),
-        pltpu.VMEM((nz, 2, rows, half), BF16),
-        pltpu.VMEM((nz, rows, width), BF16),
-        pltpu.VMEM((nz, rows, width), BF16),
-        pltpu.VMEM((nz, rows, width), F32),
-        pltpu.VMEM((rows, width), F32),
-        pltpu.VMEM((block, width), BF16),
-        dma((4, nz)),
-        dma((4, nz, 2)),
-        dma((6, nz, 2)),
-        dma((2, nt)),
-    ]
-
-
-EXCHANGE_SCRATCH = 16
-
-
-def exchange(z, t, nz, nt, rows, own_rows, scratch, ready, work, moves):
-    (full, outgoing, part, from_y, from_x, pairs, came_pairs) = scratch[:7]
-    (passed, came_far, own_part, total) = scratch[7:11]
-    far_sem, row_sem, part_sem = scratch[12:15]
-    assert nt == 4
-    i32 = jnp.int32
-    width = full.shape[-1]
-    half = width // 2
-    first, second = pl.ds(0, half), pl.ds(half, half)
-    near_x, near_y, across = (partner(t, i32(j), nt) for j in (1, 2, 3))
-
-    def window(index):
-        return rows_at(index * rows, rows)
-
-    mine = window(t)
-    x_rows, y_rows, across_rows = window(near_x), window(near_y), window(across)
-    my_pair = rows_at(lax.div(t, 2) * (2 * rows), 2 * rows)
-    y_pair = rows_at(lax.div(near_y, 2) * (2 * rows), 2 * rows)
-    in_pair = lax.rem(t, 2)
-    pair_mine, pair_x = window(in_pair), window(1 - in_pair)
-
-    def far_copy(k, source):
-        spot = full.at[source, mine]
-        return remote(spot, spot, far_sem.at[0, k], far_sem.at[1, k], expert=partner(z, i32(k), nz))
-
-    def row_copy(k, source, j, window_of):
-        spot = full.at[source, window_of]
+class Square:
+    def __init__(self, nz, nt, rows, width):
+        assert nt == 4
+        self.z, self.t = lax.axis_index("expert"), lax.axis_index("tensor")
+        self.nz, self.rows = nz, rows
+        half = width // 2
+        self.half, self.first, self.second = half, pl.ds(0, half), pl.ds(half, half)
+        near_x, near_y, across = (partner(self.t, jnp.int32(j), nt) for j in (1, 2, 3))
+        self.near = (near_x, near_y)
+        self.mine, self.x_rows, self.y_rows, self.across_rows = (
+            self.window(i) for i in (self.t, near_x, near_y, across)
+        )
+        self.y_pair = rows_at(lax.div(near_y, 2) * (2 * rows), 2 * rows)
+        in_pair = lax.rem(self.t, 2)
+        self.pair_mine, self.pair_x = self.window(in_pair), self.window(1 - in_pair)
+
+    def window(self, index):
+        return rows_at(index * self.rows, self.rows)
+
+
+class RowGather:
+    @staticmethod
+    def scratch(nz):
+        return [pltpu.SemaphoreType.DMA((2, nz)), pltpu.SemaphoreType.DMA((4, nz, 2))]
+
+    def __init__(self, square, full, sems):
+        self.sq, self.full = square, full
+        self.far_sem, self.row_sem = sems
+
+    def far_copy(self, k, source, src=None):
+        sq = self.sq
+        spot = self.full.at[source, sq.mine]
         return remote(
-            spot, spot, row_sem.at[0, k, j], row_sem.at[1, k, j], tensor=(near_x, near_y)[j]
-        )
-
-    def on_copy(k, source, j, window_of):
-        spot = full.at[source, window_of, (second, first)[j]]
+            spot if src is None else src,
+            spot,
+            self.far_sem.at[0, k],
+            self.far_sem.at[1, k],
+            expert=partner(sq.z, jnp.int32(k), sq.nz),
+        )
+
+    def row_copy(self, k, source, j, window, src=None):
+        spot = self.full.at[source, window]
         return remote(
-            spot, spot, row_sem.at[2, k, j], row_sem.at[3, k, j], tensor=(near_x, near_y)[j]
-        )
-
-    def send_rows(k, source):
+            spot if src is None else src,
+            spot,
+            self.row_sem.at[0, k, j],
+            self.row_sem.at[1, k, j],
+            tensor=self.sq.near[j],
+        )
+
+    def on_copy(self, k, source, j, window):
+        spot = self.full.at[source, window, (self.sq.second, self.sq.first)[j]]
+        return remote(
+            spot, spot, self.row_sem.at[2, k, j], self.row_sem.at[3, k, j], tensor=self.sq.near[j]
+        )
+
+    def send(self, k, source, src=None):
         for j in range(2):
-            row_copy(k, source, j, mine).start()
-
-    def pass_rows(k, source):
-        row_copy(k, source, 0, x_rows).wait_recv()
-        on_copy(k, source, 1, x_rows).start()
-        row_copy(k, source, 1, y_rows).wait_recv()
-        on_copy(k, source, 0, y_rows).start()
-
-    def wait_rows(k, source):
+            self.row_copy(k, source, j, self.sq.mine, src).start()
+
+    def hand_on(self, k, source):
+        self.row_copy(k, source, 0, self.sq.x_rows).wait_recv()
+        self.on_copy(k, source, 1, self.sq.x_rows).start()
+        self.row_copy(k, source, 1, self.sq.y_rows).wait_recv()
+        self.on_copy(k, source, 0, self.sq.y_rows).start()
+
+    def arrive(self, k, source):
         for j in range(2):
-            on_copy(k, source, j, across_rows).wait_recv()
-
-    def part_copy(k, i):
-        src = ((y_pair, first), (across_rows, second), (x_rows, second))[i]
-        dst = (from_y.at[k], from_x.at[k, 1], from_x.at[k, 0])[i]
+            self.on_copy(k, source, j, self.sq.across_rows).wait_recv()
+
+    def leave(self, k, source):
+        for j in range(2):
+            self.row_copy(k, source, j, self.sq.mine).wait_send()
+            self.on_copy(k, source, j, (self.sq.y_rows, self.sq.x_rows)[j]).wait_send()
+
+
+class RowSum:
+    @staticmethod
+    def scratch(nz, rows, block, width):
+        half = width // 2
+        dma = pltpu.SemaphoreType.DMA
+        return [
+            pltpu.VMEM((nz, block, width), BF16),
+            pltpu.VMEM((nz, 2 * rows, half), BF16),
+            pltpu.VMEM((nz, 2, rows, half), BF16),
+            pltpu.VMEM((nz, 2, rows, half), BF16),
+            pltpu.VMEM((nz, 2, rows, half), BF16),
+            pltpu.VMEM((nz, rows, width), BF16),
+            pltpu.VMEM((nz, rows, width), BF16),
+            pltpu.VMEM((rows, width), F32),
+            dma((2, nz)),
+            dma((6, nz, 2)),
+        ]
+
+    count = 10
+
+    def __init__(self, square, scratch, own=None):
+        self.sq, self.own = square, own
+        (self.outgoing, self.from_y, self.from_x, self.pairs, self.came_pairs) = scratch[:5]
+        (self.passed, self.came_far, self.total, self.far_sem, self.part_sem) = scratch[5:]
+
+    def part_copy(self, k, i):
+        sq = self.sq
+        window, cols = ((sq.y_pair, sq.first), (sq.across_rows, sq.second), (sq.x_rows, sq.second))[i]
+        dst = (self.from_y.at[k], self.from_x.at[k, 1], self.from_x.at[k, 0])[i]
         group, slot = ((0, 0), (2, 1), (2, 0))[i]
         return remote(
-            outgoing.at[k, src[0], src[1]],
+            self.outgoing.at[k, window, cols],
             dst,
-            part_sem.at[group, k, slot],
-            part_sem.at[group + 1, k, slot],
-            tensor=near_x if i else near_y,
-        )
-
-    def pair_copy(k, j):
+            self.part_sem.at[group, k, slot],
+            self.part_sem.at[group + 1, k, slot],
+            tensor=sq.near[0] if i else sq.near[1],
+        )
+
+    def pair_copy(self, k, j):
         return remote(
-            pairs.at[k, j],
-            came_pairs.at[k, j],
-            part_sem.at[4, k, j],
-            part_sem.at[5, k, j],
-            tensor=(near_x, near_y)[j],
-        )
-
-    def sum_copy(k):
+            self.pairs.at[k, j],
+            self.came_pairs.at[k, j],
+            self.part_sem.at[4, k, j],
+            self.part_sem.at[5, k, j],
+            tensor=self.sq.near[j],
+        )
+
+    def sum_copy(self, k):
         return remote(
-            passed.at[k],
-            came_far.at[k],
-            far_sem.at[2, k],
-            far_sem.at[3, k],
-            expert=partner(z, k, nz),
-        )
+            self.passed.at[k],
+            self.came_far.at[k],
+            self.far_sem.at[0, k],
+            self.far_sem.at[1, k],
+            expert=partner(self.sq.z, k, self.sq.nz),
+        )
+
+    def send(self, k):
+        for i in range(3):
+            self.part_copy(k, i).start()
+
+    def pair_up(self, k):
+        sq = self.sq
+        self.part_copy(k, 0).wait_recv()
+        kept = self.outgoing[k, sq.x_rows, sq.first].astype(F32)
+        self.pairs[k, 0] = (kept + self.from_y[k, sq.pair_x].astype(F32)).astype(BF16)
+        self.pair_copy(k, 0).start()
+        self.part_copy(k, 1).wait_recv()
+        kept = self.outgoing[k, sq.y_rows, sq.second].astype(F32)
+        self.pairs[k, 1] = (kept + self.from_x[k, 1].astype(F32)).astype(BF16)
+        self.pair_copy(k, 1).start()
+
+    def collect(self, k):
+        sq = self.sq
+        self.part_copy(k, 2).wait_recv()
+        self.pair_copy(k, 0).wait_recv()
+        self.pair_copy(k, 1).wait_recv()
+        own = self.outgoing[k, sq.mine].astype(F32) if self.own is None else self.own[k]
+        left = own[:, : sq.half] + self.from_y[k, sq.pair_mine].astype(F32)
+        right = own[:, sq.half :] + self.from_x[k, 0].astype(F32)
+        return (
+            left + self.came_pairs[k, 0].astype(F32),
+            right + self.came_pairs[k, 1].astype(F32),
+        )
+
+    def collect_own(self):
+        left, right = self.collect(jnp.int32(0))
+        self.total[:, : self.sq.half] = left
+        self.total[:, self.sq.half :] = right
+
+    def collect_far(self, k):
+        left, right = self.collect(k)
+        self.passed[k, :, self.sq.first] = left.astype(BF16)
+        self.passed[k, :, self.sq.second] = right.astype(BF16)
+        self.sum_copy(k).start()
+
+    def add_far(self):
+        for k in range(1, self.sq.nz):
+            self.sum_copy(jnp.int32(k)).wait_recv()
+            self.total[...] += self.came_far[k].astype(F32)
+
+    def leave(self, far=True):
+        for k in range(self.sq.nz):
+            if k and far:
+                self.sum_copy(jnp.int32(k)).wait_send()
+            for j in range(2):
+                self.pair_copy(k, j).wait_send()
+            for i in range(3):
+                self.part_copy(k, i).wait_send()
+
+
+def exchange_scratch(nz, nt, rows, block, width):
+    return (
+        [
+            pltpu.VMEM((nz, block, width), BF16),
+            ("part", pltpu.VMEM((block, width), F32)),
+            ("own", pltpu.VMEM((nz, rows, width), F32)),
+            pltpu.VMEM((block, width), BF16),
+            pltpu.SemaphoreType.DMA((2, nt)),
+        ]
+        + RowGather.scratch(nz)
+        + RowSum.scratch(nz, rows, block, width)
+    )
+
+
+EXCHANGE_SCRATCH = 7 + RowSum.count
+
+
+def exchange(nz, nt, own_rows, scratch, ready, work, at):
+    full, part, own_part = scratch[:3]
+    sq = Square(nz, nt, own_rows.shape[0], full.shape[-1])
+    z = sq.z
+    gather = RowGather(sq, full, scratch[5:7])
+    sums = RowSum(sq, scratch[7 : 7 + RowSum.count], own_part)
+    i32 = jnp.int32
 
     def produce(k, source):
-        wait_rows(k, source)
+        gather.arrive(k, source)
         part[...] = work(k, source, full[source])
-        outgoing[k] = part[...].astype(BF16)
-        for i in range(3):
-            part_copy(k, i).start()
-        own_part[k] = part[mine]
-
-    def pair_up(k):
-        part_copy(k, 0).wait_recv()
-        kept = outgoing[k, x_rows, first].astype(F32)
-        pairs[k, 0] = (kept + from_y[k, pair_x].astype(F32)).astype(BF16)
-        pair_copy(k, 0).start()
-        part_copy(k, 1).wait_recv()
-        kept = outgoing[k, y_rows, second].astype(F32)
-        pairs[k, 1] = (kept + from_x[k, 1].astype(F32)).astype(BF16)
-        pair_copy(k, 1).start()
-
-    def collect(k):
-        part_copy(k, 2).wait_recv()
-        pair_copy(k, 0).wait_recv()
-        pair_copy(k, 1).wait_recv()
-        own = own_part[k]
-        left = own[:, :half] + from_y[k, pair_mine].astype(F32) + came_pairs[k, 0].astype(F32)
-        right = own[:, half:] + from_x[k, 0].astype(F32) + came_pairs[k, 1].astype(F32)
-        return left, right
-
-    def collect_own():
-        left, right = collect(i32(0))
-        total[:, :half] = left
-        total[:, half:] = right
-
-    def collect_far(k):
-        left, right = collect(k)
-        passed[k, :, first] = left.astype(BF16)
-        passed[k, :, second] = right.astype(BF16)
-        sum_copy(k).start()
-
-    full[z, mine] = own_rows
+        sums.outgoing[k] = part[...].astype(BF16)
+        sums.send(k)
+        own_part[k] = part[sq.mine]
+
+    full[z, sq.mine] = own_rows
     for k in range(1, nz):
-        far_copy(k, z).start()
-    send_rows(0, z)
+        gather.far_copy(k, z).start()
+    gather.send(0, z)
+    at("begin")
     ready()
     for k in range(1, nz):
         source = partner(z, i32(k), nz)
-        far_copy(k, source).wait_recv()
-        send_rows(k, source)
+        gather.far_copy(k, source).wait_recv()
+        gather.send(k, source)
         if k == 1:
-            pass_rows(0, z)
-    for move in moves:
-        move.start()
-    pass_rows(1, partner(z, i32(1), nz))
+            gather.hand_on(0, z)
+    at("arrived")
+    gather.hand_on(1, partner(z, i32(1), nz))
 
     def step(k, carry):
         @pl.when(k + 1 < nz)
         def _():
-            pass_rows(k + 1, partner(z, k + 1, nz))
+            gather.hand_on(k + 1, partner(z, k + 1, nz))
 
         turn = lax.rem(k, nz)
         produce(turn, partner(z, turn, nz))
 
         @pl.when(k >= 2)
         def _():
-            pair_up(k - 1)
+            sums.pair_up(k - 1)
 
         @pl.when(k >= 3)
         def _():
-            collect_far(k - 2)
+            sums.collect_far(k - 2)
+
+        @pl.when(k == 2)
+        def _():
+            at("second")
 
         return carry
 
     lax.fori_loop(1, nz + 1, step, 0)
-    for move in moves:
-        move.poll(1)
-    collect_far(i32(nz - 1))
-    pair_up(i32(0))
-    for move in moves:
-        move.poll(2)
-    collect_own()
-    for k in range(1, nz):
-        sum_copy(i32(k)).wait_recv()
-        total[...] += came_far[k].astype(F32)
+    at("looped")
+    sums.collect_far(i32(nz - 1))
+    sums.pair_up(i32(0))
+    sums.collect_own()
+    at("collected")
+    sums.add_far()
 
     def finish():
-        for k in range(1, nz):
-            far_copy(k, z).wait_send()
-            sum_copy(i32(k)).wait_send()
         for k in range(nz):
             source = partner(z, i32(k), nz)
-            for j in range(2):
-                row_copy(k, source, j, mine).wait_send()
-                on_copy(k, source, j, (y_rows, x_rows)[j]).wait_send()
-                pair_copy(k, j).wait_send()
-            for i in range(3):
-                part_copy(k, i).wait_send()
-
-    return finish
+            if k:
+                gather.far_copy(k, z).wait_send()
+            gather.leave(k, source)
+        sums.leave()
+
+    return sums.total, finish
 
 
 def spread_rows(t, nt, rows, block_ref, send_sem, recv_sem):
@@ -373,14 +441,14 @@
     def __init__(self, layer, spots, nz):
         self.layer, self.spots, self.nz = layer, spots, nz
 
-    def scratch(self, count):
+    def scratch(self, count=4):
         dma = pltpu.SemaphoreType.DMA
         return [dma((count,))] + [dma((count, self.nz))] * 6
 
     def bind(self, shards, outs, sems):
         self.s, self.z = lax.axis_index("section"), lax.axis_index("expert")
         self.shards, self.outs, self.sems = shards, outs, sems
-        self.source = self.s == self.layer
+        self.source = self.hands = self.s == self.layer
         self.count = len(shards)
         return self
 
@@ -423,6 +491,9 @@
         @pl.when(self.source)
         def _():
             self.home(a).start()
+
+        @pl.when(self.hands)
+        def _():
             self.hand(a, self.z, True).start()
 
     def begin(self, a):
@@ -441,7 +512,9 @@
             def _():
                 self.hop(a, z - k, k + 1, True).start()
 
-            self.hand(a, z - k).start()
+            @pl.when(self.hands)
+            def _():
+                self.hand(a, z - k).start()
 
         @pl.when(self.source & (z + k < nz))
         def _():
@@ -451,7 +524,9 @@
             def _():
                 self.hop(a, z + k, k + 1, False).start()
 
-            self.hand(a, z + k).start()
+            @pl.when(self.hands)
+            def _():
+                self.hand(a, z + k).start()
 
     def settle(self, a):
         @pl.when(self.source)
@@ -466,10 +541,13 @@
     def end(self, a):
         z, nz = self.z, self.nz
 
-        @pl.when(self.source)
+        @pl.when(self.hands)
         def _():
             for owner in range(nz):
                 self.hand(a, owner).wait_send()
+
+        @pl.when(self.source)
+        def _():
             for step in range(1, nz):
 
                 @pl.when((z >= step - 1) & (z + 1 < nz))
@@ -485,7 +563,7 @@
             self.begin(a)
 
     def poll(self, turn):
-        if turn < self.nz - 1:
+        if turn < min(3, self.nz - 1):
             for a in range(self.count):
                 self.step(a, turn)
 
@@ -498,25 +576,139 @@
             self.end(a)
 
 
+class Line(Relay):
+    def __init__(self, layer, nz):
+        super().__init__(layer, None, nz)
+
+    def scratch(self):
+        return super().scratch(1)
+
+    def bind(self, ins, outs, sems):
+        super().bind(ins, outs, sems)
+        self.source, self.hands = self.s >= 0, self.s != self.layer
+        return self
+
+    def place(self, a, owner, section=None):
+        return self.outs[a].at[self.s if section is None else section, owner]
+
+    def settle(self, a):
+        self.home(a).wait()
+
+        @pl.when(self.s == self.layer)
+        def _():
+            for owner in range(self.nz):
+                spot = self.place(a, owner, 1 - self.layer)
+                remote(
+                    spot, spot, self.sems[5].at[a, owner], self.sems[6].at[a, owner], section=1 - self.s
+                ).wait_recv()
+
+
+class Slice:
+    def __init__(self, layer, nz, nt):
+        self.layer, self.nz, self.nt = layer, nz, nt
+
+    def scratch(self):
+        dma = pltpu.SemaphoreType.DMA
+        return [dma((2,)), dma((self.nz,)), dma((2, self.nz)), dma((2, self.nt))]
+
+    def bind(self, ins, outs, sems):
+        self.s, self.z, self.t = (lax.axis_index(a) for a in ("section", "expert", "tensor"))
+        self.src, (self.out, self.rows_out), self.sems = ins[0], outs, sems
+        rows, self.cols = self.rows_out.shape[2:]
+        self.rows = rows
+        self.mine = rows_at(self.t * rows, rows)
+        self.receives = self.s == self.layer
+        return self
+
+    def far(self, k, local, section=None, origin=None):
+        zz = partner(self.z, jnp.int32(k), self.nz)
+        src = self.src.at[self.mine, rows_at(zz * self.cols, self.cols)]
+        section = self.s if section is None else section
+        spot = self.rows_out.at[section, self.z if origin is None else origin]
+        if local:
+            return pltpu.make_async_copy(src, spot, self.sems[0].at[0])
+        return remote(
+            src,
+            spot,
+            self.sems[1].at[k],
+            self.sems[2].at[section, k],
+            section=jnp.int32(self.layer),
+            expert=zz,
+        )
+
+    def near(self, j, window):
+        return remote(
+            self.rows_out,
+            self.out.at[:, :, window],
+            self.sems[3].at[0, j],
+            self.sems[3].at[1, j],
+            tensor=partner(self.t, jnp.int32(j), self.nt),
+        )
+
+    def home(self):
+        return pltpu.make_async_copy(self.rows_out, self.out.at[:, :, self.mine], self.sems[0].at[1])
+
+    def start(self):
+        for k in range(1, self.nz):
+            self.far(k, False).start()
+
+        @pl.when(self.receives)
+        def _():
+            self.far(0, True).start()
+
+        @pl.when(jnp.logical_not(self.receives))
+        def _():
+            self.far(0, False).start()
+
+    def poll(self, turn):
+        if turn != 1:
+            return
+
+        @pl.when(self.receives)
+        def _():
+            self.far(0, True).wait()
+            for section in range(2):
+                for k in range(self.nz):
+                    if k or section != self.layer:
+                        zz = partner(self.z, jnp.int32(k), self.nz)
+                        self.far(k, False, section, zz).wait_recv()
+            self.home().start()
+            for j in range(1, self.nt):
+                self.near(j, self.mine).start()
+
+    def finish(self):
+        for k in range(1, self.nz):
+            self.far(k, False).wait_send()
+
+        @pl.when(jnp.logical_not(self.receives))
+        def _():
+            self.far(0, False).wait_send()
+
+        @pl.when(self.receives)
+        def _():
+            self.home().wait()
+            for j in range(1, self.nt):
+                theirs = partner(self.t, jnp.int32(j), self.nt) * self.rows
+                self.near(j, rows_at(theirs, self.rows)).wait_recv()
+                self.near(j, self.mine).wait_send()
+
+
 class Gather:
-    def __init__(self, layer, nz, sliced=False):
-        self.layer, self.nz, self.sliced = layer, nz, sliced
+    def __init__(self, layer, nz):
+        self.layer, self.nz = layer, nz
 
     def scratch(self):
         dma = pltpu.SemaphoreType.DMA
         return [dma((1,)), dma((self.nz,)), dma((2, self.nz))]
 
-    def bind(self, src, out, sems):
+    def bind(self, ins, outs, sems):
         self.s, self.z = lax.axis_index("section"), lax.axis_index("expert")
-        self.src, self.out, self.sems = src, out, sems
+        self.src, self.out, self.sems = (ins or (None,))[0], outs[0], sems
         return self
 
     def copy(self, k, local, section=None, origin=None):
         zz = partner(self.z, jnp.int32(k), self.nz)
         src = self.src
-        if self.sliced:
-            cols = self.out.shape[-1]
-            src = src.at[:, rows_at(zz * cols, cols)]
         section = self.s if section is None else section
         spot = self.out.at[section, self.z if origin is None else origin]
         if local:
@@ -576,8 +768,9 @@
         dma = pltpu.SemaphoreType.DMA
         return [dma((1,)), dma((1,)), dma((1,))]
 
-    def bind(self, src, out, sems):
-        self.s, self.src, self.out, self.sems = lax.axis_index("section"), src, out, sems
+    def bind(self, ins, outs, sems):
+        self.s, self.sems = lax.axis_index("section"), sems
+        self.src, self.out = (ins or (None,))[0], outs[0]
         return self
 
     def local(self):
@@ -622,6 +815,207 @@
         @pl.when(self.s != self.layer)
         def _():
             self.copy().wait_send()
+
+
+class RowsFar:
+    def __init__(self, slot, nz, nt):
+        self.slot, self.nz, self.nt = slot, nz, nt
+
+    def scratch(self):
+        return [pltpu.SemaphoreType.DMA((1,)), pltpu.SemaphoreType.DMA((2, self.nz))]
+
+    def bind(self, ins, outs, sems):
+        self.z, self.t = lax.axis_index("expert"), lax.axis_index("tensor")
+        self.src, self.out, self.sems = ins[0], outs[0], sems
+        return self
+
+    def copy(self, k, origin):
+        rows = self.out.shape[1]
+        src = self.src.at[self.slot, rows_at(self.t * rows, rows)]
+        if k == 0:
+            return pltpu.make_async_copy(src, self.out.at[origin], self.sems[0].at[0])
+        return remote(
+            src,
+            self.out.at[origin],
+            self.sems[1].at[0, k],
+            self.sems[1].at[1, k],
+            expert=partner(self.z, jnp.int32(k), self.nz),
+        )
+
+    def start(self):
+        for k in range(self.nz):
+            self.copy(k, self.z).start()
+
+    def poll(self, turn):
+        pass
+
+    def finish(self):
+        self.copy(0, self.z).wait()
+        for k in range(1, self.nz):
+            self.copy(k, self.z).wait_send()
+            self.copy(k, partner(self.z, jnp.int32(k), self.nz)).wait_recv()
+
+
+class Spread:
+    def __init__(self, nz, nt):
+        self.nz, self.nt = nz, nt
+
+    def scratch(self):
+        return [pltpu.SemaphoreType.DMA((1,))] + RowGather.scratch(self.nz)
+
+    def bind(self, ins, outs, sems):
+        self.src, self.out, self.sems = ins[0], outs[0], sems
+        self.sq = Square(self.nz, self.nt, *self.src.shape[1:])
+        self.gather = RowGather(self.sq, self.out, sems[1:])
+        return self
+
+    def local(self):
+        return pltpu.make_async_copy(self.src, self.out.at[:, self.sq.mine], self.sems[0].at[0])
+
+    def start(self):
+        self.local().start()
+        for k in range(self.nz):
+            self.gather.send(k, k, self.src.at[k])
+
+    def poll(self, turn):
+        if turn == 1:
+            for k in range(self.nz):
+                self.gather.hand_on(k, k)
+
+    def finish(self):
+        self.local().wait()
+        for k in range(self.nz):
+            self.gather.arrive(k, k)
+            self.gather.leave(k, k)
+
+
+class SumNear:
+    def __init__(self, nz, nt, rows, block, width):
+        self.nz, self.nt = nz, nt
+        self.shape = rows, block, width
+
+    def scratch(self):
+        return [pltpu.SemaphoreType.DMA((2,))] + RowSum.scratch(self.nz, *self.shape)
+
+    def bind(self, ins, outs, scratch):
+        self.src, self.out, self.sems = ins[0], outs[0], scratch[0]
+        self.sq = Square(self.nz, self.nt, self.shape[0], self.shape[2])
+        self.sums = RowSum(self.sq, scratch[1:])
+        return self
+
+    def start(self):
+        load = pltpu.make_async_copy(self.src, self.sums.outgoing, self.sems.at[0])
+        load.start()
+        load.wait()
+        for k in range(self.nz):
+            self.sums.send(k)
+
+    def poll(self, turn):
+        if turn == 1:
+            for k in range(self.nz):
+                self.sums.pair_up(jnp.int32(k))
+        if turn == 2:
+            for k in range(self.nz):
+                left, right = self.sums.collect(jnp.int32(k))
+                self.sums.passed[k, :, self.sq.first] = left.astype(BF16)
+                self.sums.passed[k, :, self.sq.second] = right.astype(BF16)
+            self.save().start()
+
+    def save(self):
+        return pltpu.make_async_copy(self.sums.passed, self.out, self.sems.at[1])
+
+    def finish(self):
+        self.save().wait()
+        self.sums.leave(False)
+
+
+class SumFar:
+    def __init__(self, nz, rows, width):
+        self.nz, self.shape = nz, (rows, width)
+
+    def scratch(self):
+        dma = pltpu.SemaphoreType.DMA
+        return [
+            pltpu.VMEM((self.nz,) + self.shape, BF16),
+            pltpu.VMEM(self.shape, BF16),
+            dma((2,)),
+            dma((2, self.nz)),
+        ]
+
+    def bind(self, ins, outs, scratch):
+        self.z = lax.axis_index("expert")
+        self.src, self.rows_ref = ins
+        self.out = outs[0]
+        self.came, self.result, self.sems, self.far_sem = scratch
+        return self
+
+    def copy(self, k):
+        if k == 0:
+            return pltpu.make_async_copy(self.src.at[0], self.came.at[0], self.sems.at[0])
+        return remote(
+            self.src.at[k],
+            self.came.at[k],
+            self.far_sem.at[0, k],
+            self.far_sem.at[1, k],
+            expert=partner(self.z, jnp.int32(k), self.nz),
+        )
+
+    def save(self):
+        return pltpu.make_async_copy(self.result, self.out, self.sems.at[1])
+
+    def start(self):
+        for k in range(self.nz):
+            self.copy(k).start()
+
+    def poll(self, turn):
+        if turn == 2:
+            self.copy(0).wait()
+            total = self.rows_ref[...] + self.came[0].astype(F32)
+            for k in range(1, self.nz):
+                self.copy(k).wait_recv()
+                total = total + self.came[k].astype(F32)
+            self.result[...] = total.astype(BF16)
+            self.save().start()
+
+    def finish(self):
+        self.save().wait()
+        for k in range(1, self.nz):
+            self.copy(k).wait_send()
+
+
+class SpreadNear:
+    def __init__(self, layer, nt, block, width):
+        self.nt, self.shape, self.near = nt, (block, width), Near(layer, True)
+
+    def scratch(self):
+        dma = pltpu.SemaphoreType.DMA
+        return [pltpu.VMEM(self.shape, BF16), dma((1,)), dma((2, self.nt))] + self.near.scratch()
+
+    def bind(self, ins, outs, scratch):
+        self.t = lax.axis_index("tensor")
+        self.src = ins[0]
+        self.whole, self.load_sem, self.spread_sem = scratch[:3]
+        self.near.bind([self.whole], outs, scratch[3:])
+        self.rows = self.src.shape[0]
+        return self
+
+    def start(self):
+        load = pltpu.make_async_copy(
+            self.src, self.whole.at[rows_at(self.t * self.rows, self.rows)], self.load_sem.at[0]
+        )
+        load.start()
+        load.wait()
+        self.wait = spread_rows(
+            self.t, self.nt, self.rows, self.whole, self.spread_sem.at[0], self.spread_sem.at[1]
+        )
+
+    def poll(self, turn):
+        if turn == 1:
+            self.wait()
+            self.near.start()
+
+    def finish(self):
+        self.near.finish()
 
 
 def heads_to_rows(value, heads, size):
@@ -716,7 +1110,7 @@
     gates[m] = out
 
 
-def start_attend_kernel(nz, nt, heads, relay, ins, outs, scratch):
+def start_attend_kernel(nz, nt, heads, relay, hello, at, ins, outs, scratch):
     s, z, t = lax.axis_index("section"), lax.axis_index("expert"), lax.axis_index("tensor")
     lengths, ids, route_weights, boundary, gains, wq, wk, wv, wo, wg, wu, wd = ins
     edges, tabs_out, gates_out, gains_out = outs[:4]
@@ -736,7 +1130,7 @@
     ]
     own[0].start()
     own[2].start()
-    greet(all_peers(s, z, t, nz, nt))
+    hello(all_peers(s, z, t, nz, nt))
 
     def sibling(i, src, dst):
         return remote(src, dst, sib_send.at[i], sib_recv.at[i], section=other)
@@ -755,14 +1149,6 @@
         relay.begin(a)
     relay.begin_home(3)
 
-    @pl.when(z == 0)
-    def _():
-        relay.begin_side(3, True)
-
-    @pl.when(z == nz - 1)
-    def _():
-        relay.begin_side(3, False)
-
     def gate_copy(d, k, arrival=False):
         zz = partner(z, i32(k), nz)
         section = s if d == 0 else other
@@ -810,11 +1196,11 @@
             for a in range(3):
                 relay.step(a, k)
 
-            @pl.when((z == k) & (z < nz - 1))
+            @pl.when((z == k) | ((z == 0) & (k == 1)))
             def _():
                 relay.begin_side(3, True)
 
-            @pl.when((z == nz - 1 - k) & (z > 0))
+            @pl.when((z == nz - 1 - k) | ((z == nz - 1) & (k == 1)))
             def _():
                 relay.begin_side(3, False)
 
@@ -827,6 +1213,7 @@
     def wait_out():
         for k in range(1, nz):
             relay.step(3, k)
+        at("shards")
         relay.settle(3)
         bring(3).start()
         bring(3).wait()
@@ -842,33 +1229,43 @@
         gate_copy(d, k, True).wait_recv()
     for a in range(4):
         relay.end(a)
-
-
-def attend_kernel(layer, nz, nt, heads, bind, ins, outs, scratch):
+    at("end")
+
+
+def attend_kernel(layer, nz, nt, heads, hello, at, ins, outs, scratch):
     s, z, t = lax.axis_index("section"), lax.axis_index("expert"), lax.axis_index("tensor")
-    x_ref, tabs, gains, wq, wk, wv, wo = ins[:7]
-    w_sem, attn_scratch, rest = scratch[0], scratch[1:10], scratch[10:]
-    moves = bind(ins[7:], outs[9:], rest)
+    x_ref, tabs, gains, wq, wk, wv, wo = ins
+    w_sem, tabs_s, gains_s, attn_scratch = scratch[0], scratch[1], scratch[2], scratch[3:]
     loads = [
         pltpu.make_async_copy(src, dst, w_sem.at[i])
         for i, (src, dst) in enumerate(zip((wq, wk, wv, wo), attn_scratch))
     ]
-    for load in loads:
+    small = [
+        pltpu.make_async_copy(tabs.at[layer], tabs_s, w_sem.at[4]),
+        pltpu.make_async_copy(gains.at[layer], gains_s, w_sem.at[5]),
+    ]
+    for load in small:
         load.start()
-    greet(all_peers(s, z, t, nz, nt))
-    for move in moves:
-        move.start()
+    hello(all_peers(s, z, t, nz, nt))
+    at("begin")
+    for load in small:
+        load.wait()
 
     def wait_qkv():
+        at("qkv")
+        for load in loads[:3]:
+            load.start()
         for load in loads[:3]:
             load.wait()
 
-    tables = (tabs[layer, 0], tabs[layer, 1], tabs[layer, 2])
-    attend_body(
-        t, nt, heads, x_ref, tables, gains[layer], outs[:9], attn_scratch, wait_qkv, loads[3].wait
-    )
-    for move in moves:
-        move.finish()
+    def wait_out():
+        at("out")
+        loads[3].start()
+        loads[3].wait()
+
+    tables = (tabs_s[0], tabs_s[1], tabs_s[2])
+    attend_body(t, nt, heads, x_ref, tables, gains_s[...], outs, attn_scratch, wait_qkv, wait_out)
+    at("end")
 
 
 def load_experts(layer, s, own, sibling, scratch, sems):
@@ -888,16 +1285,17 @@
     return copies(own)
 
 
-def experts_kernel(layer, nz, nt, local_experts, bind, ins, outs, scratch):
+def experts_kernel(layer, nz, nt, local_experts, hello, at, ins, outs, scratch):
     s, z, t = lax.axis_index("section"), lax.axis_index("expert"), lax.axis_index("tensor")
-    b_ref, h1_ref, gates, wg, wu, wd, sg, su, sd = ins[:9]
-    y_ref, b_out, g_out, u_out = outs[:4]
-    wg_s, wu_s, wd_s, g_s, u_s, w_sem, o_sem = scratch[:7]
-    spaces, rest = scratch[7 : 7 + EXCHANGE_SCRATCH], scratch[7 + EXCHANGE_SCRATCH :]
-    moves = bind(ins[9:], outs[4:], rest)
+    b_ref, h1_ref, gates, wg, wu, wd, sg, su, sd = ins
+    y_ref, b_out, g_out, u_out = outs
+    wg_s, wu_s, wd_s, g_s, u_s, gates_s, w_sem, o_sem = scratch[:8]
+    spaces = scratch[8:]
     rows = b_ref.shape[0]
     loads = load_experts(layer, s, (wg, wu, wd), (sg, su, sd), (wg_s, wu_s, wd_s), w_sem)
-    greet(all_peers(s, z, t, nz, nt))
+    loads.append(pltpu.make_async_copy(gates.at[layer], gates_s, w_sem.at[3]))
+    loads[3].start()
+    hello(all_peers(s, z, t, nz, nt))
     width = wg.shape[0] // local_experts
 
     def ready():
@@ -909,12 +1307,12 @@
         up_pre = dot_nt(rows_in, wu_s[...])
         g_s[origin] = gate_pre
         u_s[origin] = up_pre
-        weight = expert_gates(gates[layer, origin], z * local_experts, local_experts, width)
+        weight = expert_gates(gates_s[origin], z * local_experts, local_experts, width)
         hidden = (gate_pre * jax.nn.sigmoid(gate_pre) * up_pre * weight).astype(BF16)
         return dot(hidden, wd_s[...])
 
-    finish = exchange(z, t, nz, nt, rows, b_ref[...], spaces, ready, work, moves)
-    full, total, whole, spread_sem = spaces[0], spaces[10], spaces[11], spaces[15]
+    total, finish = exchange(nz, nt, b_ref[...], spaces, ready, work, at)
+    full, whole, spread_sem = spaces[0], spaces[3], spaces[4]
     saves = [
         pltpu.make_async_copy(full, b_out, o_sem.at[0]),
         pltpu.make_async_copy(g_s, g_out, o_sem.at[1]),
@@ -924,24 +1322,26 @@
         save.start()
     whole[rows_at(t * rows, rows)] = (h1_ref[...] + total[...]).astype(BF16)
     wait = spread_rows(t, nt, rows, whole, spread_sem.at[0], spread_sem.at[1])
+    at("spread")
     finish()
     wait()
     y_ref[...] = whole[...]
     for save in saves:
         save.wait()
-    for move in moves:
-        move.finish()
-
-
-def experts_back_kernel(layer, nz, nt, local_experts, bind, ins, outs, scratch):
+    at("end")
+
+
+def experts_back_kernel(layer, nz, nt, local_experts, hello, at, ins, outs, scratch):
     s, z, t = lax.axis_index("section"), lax.axis_index("expert"), lax.axis_index("tensor")
-    dy_ref, h1_ref, gains, gates, g_in, u_in, wg, wu, wd, sg, su, sd = ins[:12]
-    dat_ref, dh1_ref, term_ref, dy_out, hid_out, dg_out, du_out = outs[:7]
+    dy_ref, h1_ref, gains, gates, g_in, u_in, wg, wu, wd, sg, su, sd = ins
+    dat_ref, dh1_ref, term_ref, dy_out, hid_out, dg_out, du_out = outs
     wg_s, wu_s, wd_s, g_s, u_s, hid_s, dg_s, du_s, w_sem, g_sem, u_sem, o_sem = scratch[:12]
-    spaces, rest = scratch[12 : 12 + EXCHANGE_SCRATCH], scratch[12 + EXCHANGE_SCRATCH :]
-    moves = bind(ins[12:], outs[7:], rest)
+    gates_s, scratch = scratch[12], scratch[:12] + scratch[13:]
+    spaces = scratch[12:]
     rows, model_width = dy_ref.shape
     loads = load_experts(layer, s, (wd, wg, wu), (sd, sg, su), (wd_s, wg_s, wu_s), w_sem)
+    loads.append(pltpu.make_async_copy(gates.at[layer], gates_s, w_sem.at[3]))
+    loads[3].start()
 
     def kept(k):
         origin, slot = partner(z, lax.rem(k + 1, nz), nz), lax.rem(k, 2)
@@ -952,7 +1352,7 @@
 
     for load in kept(jnp.int32(0)):
         load.start()
-    greet(all_peers(s, z, t, nz, nt))
+    hello(all_peers(s, z, t, nz, nt))
     width = wg.shape[0] // local_experts
 
     def ready():
@@ -971,7 +1371,7 @@
 
         slot = lax.rem(turn, 2)
         gate_pre, up_pre = g_s[slot], u_s[slot]
-        weight = expert_gates(gates[layer, origin], z * local_experts, local_experts, width)
+        weight = expert_gates(gates_s[origin], z * local_experts, local_experts, width)
         sigmoid = jax.nn.sigmoid(gate_pre)
         silu = gate_pre * sigmoid
         hid_s[origin] = (silu * up_pre * weight).astype(BF16)
@@ -980,8 +1380,8 @@
         du_s[origin] = (grad_hidden * silu).astype(BF16)
         return dot(dg_s[origin], wg_s[...]) + dot(du_s[origin], wu_s[...])
 
-    finish = exchange(z, t, nz, nt, rows, dy_ref[...], spaces, ready, work, moves)
-    full, total, whole, spread_sem = spaces[0], spaces[10], spaces[11], spaces[15]
+    total, finish = exchange(nz, nt, dy_ref[...], spaces, ready, work, at)
+    full, whole, spread_sem = spaces[0], spaces[3], spaces[4]
     saves = [
         pltpu.make_async_copy(full, dy_out, o_sem.at[0]),
         pltpu.make_async_copy(hid_s, hid_out, o_sem.at[1]),
@@ -998,47 +1398,129 @@
     term_ref[...] = term
     whole[rows_at(t * rows, rows)] = dh1.astype(BF16)
     wait = spread_rows(t, nt, rows, whole, spread_sem.at[0], spread_sem.at[1])
+    at("spread")
     finish()
     wait()
     dat_ref[...] = whole[...]
     for save in saves:
         save.wait()
-    for move in moves:
-        move.finish()
-
-
-def attend_back_kernel(layer, source, nz, nt, heads, bind, ins, outs, scratch):
+    at("end")
+
+
+def experts_both_kernel(layer, nz, nt, local_experts, hello, at, ins, outs, scratch):
+    s, z, t = lax.axis_index("section"), lax.axis_index("expert"), lax.axis_index("tensor")
+    b_ref, h1_ref, dy_ref, gains, gates, dy_all, wg, wu, wd, sg, su, sd = ins
+    dat_ref, dh1_ref, term_ref, b_out, y_out, hid_out, dg_out, du_out = outs
+    wg_s, wu_s, wd_s, dy_s, y_s, hid_s, dg_s, du_s, w_sem, dy_sem, y_sem, o_sem = scratch[:12]
+    gates_s, scratch = scratch[12], scratch[:12] + scratch[13:]
+    spaces = scratch[12:]
+    rows, model_width = b_ref.shape
+    loads = load_experts(layer, s, (wg, wu, wd), (sg, su, sd), (wg_s, wu_s, wd_s), w_sem)
+    loads.append(pltpu.make_async_copy(gates.at[layer], gates_s, w_sem.at[3]))
+    loads[3].start()
+
+    def cotangent(turn):
+        origin, slot = partner(z, lax.rem(turn + 1, nz), nz), lax.rem(turn, 2)
+        return pltpu.make_async_copy(dy_all.at[origin], dy_s.at[slot], dy_sem.at[slot])
+
+    def store(turn):
+        k, slot = lax.rem(turn + 1, nz), lax.rem(turn, 2)
+        return pltpu.make_async_copy(y_s.at[slot], y_out.at[k], y_sem.at[slot])
+
+    cotangent(jnp.int32(0)).start()
+    hello(all_peers(s, z, t, nz, nt))
+    width = wg.shape[0] // local_experts
+
+    def ready():
+        for load in loads:
+            load.wait()
+
+    def work(k, origin, rows_in):
+        turn = lax.rem(k + nz - 1, nz)
+        slot = lax.rem(turn, 2)
+        cotangent(turn).wait()
+
+        @pl.when(turn + 1 < nz)
+        def _():
+            cotangent(turn + 1).start()
+
+        @pl.when(turn >= 2)
+        def _():
+            store(turn - 2).wait()
+
+        gate_pre = dot_nt(rows_in, wg_s[...])
+        up_pre = dot_nt(rows_in, wu_s[...])
+        weight = expert_gates(gates_s[origin], z * local_experts, local_experts, width)
+        sigmoid = jax.nn.sigmoid(gate_pre)
+        silu = gate_pre * sigmoid
+        hid_s[origin] = (silu * up_pre * weight).astype(BF16)
+        grad_hidden = dot_nt(dy_s[slot], wd_s[...]) * weight
+        dg_s[origin] = (grad_hidden * up_pre * sigmoid * (1.0 + gate_pre * (1.0 - sigmoid))).astype(BF16)
+        du_s[origin] = (grad_hidden * silu).astype(BF16)
+        y_s[slot] = dot(hid_s[origin], wd_s[...]).astype(BF16)
+        store(turn).start()
+        return dot(dg_s[origin], wg_s[...]) + dot(du_s[origin], wu_s[...])
+
+    total, finish = exchange(nz, nt, b_ref[...], spaces, ready, work, at)
+    full, whole, spread_sem = spaces[0], spaces[3], spaces[4]
+    saves = [
+        pltpu.make_async_copy(full, b_out, o_sem.at[0]),
+        pltpu.make_async_copy(hid_s, hid_out, o_sem.at[1]),
+        pltpu.make_async_copy(dg_s, dg_out, o_sem.at[2]),
+        pltpu.make_async_copy(du_s, du_out, o_sem.at[3]),
+    ]
+    for save in saves:
+        save.start()
+    unit, factor = unit_rows(h1_ref[...])
+    g_moe = gains[layer, :, model_width : 2 * model_width]
+    back, term = norm_back(total[...], g_moe, unit, factor)
+    dh1 = dy_ref[...].astype(F32) + back
+    dh1_ref[...] = dh1
+    term_ref[...] = term
+    whole[rows_at(t * rows, rows)] = dh1.astype(BF16)
+    wait = spread_rows(t, nt, rows, whole, spread_sem.at[0], spread_sem.at[1])
+    at("spread")
+    finish()
+    wait()
+    dat_ref[...] = whole[...]
+    for save in saves:
+        save.wait()
+    store(jnp.int32(nz - 2)).wait()
+    store(jnp.int32(nz - 1)).wait()
+    at("end")
+
+
+def attend_back_kernel(layer, source, nz, nt, heads, hello, at, ins, outs, scratch):
     s, z, t = lax.axis_index("section"), lax.axis_index("expert"), lax.axis_index("tensor")
     (x_ref, tabs, gains, dat_ref, dh1_ref, term_moe, q_ref, k_ref, v_ref, qr_ref, kr_ref) = ins[:11]
     wq, wk, wv, wo = ins[11:15]
     dx_ref, dqkv_ref, terms_ref = outs[:3]
     wq_s, wk_s, wv_s, wo_s, part, outgoing, came, s_sem, r_sem, w_sem, gs_sem, gr_sem = scratch[:12]
+    x_s, scratch = scratch[12], scratch[13:]
     if layer == 0:
-        whole, terms_near, terms_in, t_sem, near_send, near_recv = scratch[12:18]
-        rest, terms_other, moves_in = scratch[18:], ins[15], ins[16:]
-        terms_out, moves_out = outs[3], outs[4:]
-    else:
-        rest, moves_in, moves_out = scratch[12:], ins[15:], outs[3:]
-    moves = bind(moves_in, moves_out, rest)
+        whole, terms_near, terms_in, t_sem, near_send, near_recv = scratch
+        terms_other, terms_out = ins[15], outs[3]
+    block, model_width = dat_ref.shape
+    rows = block // nt
+    mine = rows_at(t * rows, rows)
+    x_copy = pltpu.make_async_copy(
+        x_ref.at[mine] if source is None else x_ref.at[source, mine], x_s, w_sem.at[4]
+    )
+    x_copy.start()
     loads = [
         pltpu.make_async_copy(src, dst, w_sem.at[i])
         for i, (src, dst) in enumerate(((wo, wo_s), (wq, wq_s), (wk, wk_s), (wv, wv_s)))
     ]
     for load in loads:
         load.start()
-    greet(all_peers(s, z, t, nz, nt))
-    late = ()
+    hello(all_peers(s, z, t, nz, nt))
     if layer == 0:
-        late = moves[-3:]
-        moves = moves[:-3]
+        late = [at.moves[name] for name in ("dqkv_0", "dx_0", "terms_0")]
         late[0].src, late[1].src, late[2].src = dqkv_ref, whole, terms_ref
-    for move in moves:
-        move.start()
-
-    block = x_ref.shape[1]
-    rows = block // nt
+    at("begin")
+
     size = tabs.shape[-1]
-    g_attn, _, g_query, g_key = split_gains(gains[layer], x_ref.shape[2], size)
+    g_attn, _, g_query, g_key = split_gains(gains[layer], model_width, size)
     scale = 1.0 / math.sqrt(size)
     cos, sin, bias = tabs[layer, 0], tabs[layer, 1], tabs[layer, 2]
     cos_all, sin_all = tiled(cos, heads), tiled(sin, heads)
@@ -1067,12 +1549,14 @@
     dqkv_ref[:, (heads + 1) * size :] = dv
     if layer == 0:
         late[0].start()
+    at("dqkv")
     for load in loads[1:]:
         load.wait()
     part[...] = dot_nt(dq, wq_s[...]) + dot_nt(dk, wk_s[...]) + dot_nt(dv, wv_s[...])
     total = reduce_rows(t, nt, rows, part, outgoing, came, s_sem, r_sem)
-    mine = rows_at(t * rows, rows)
-    unit, factor = unit_rows(x_ref[source, mine].astype(F32))
+    at("reduced")
+    x_copy.wait()
+    unit, factor = unit_rows(x_s[...].astype(F32))
     back, term_attn = norm_back(total, g_attn, unit, factor)
     dx = (dh1_ref[...] + back).astype(BF16)
     terms_ref[...] = jnp.zeros_like(terms_ref)
@@ -1080,6 +1564,7 @@
     write_terms(terms_ref, 8, term_attn)
     terms_ref[16:17, :size] = term_query
     terms_ref[16:17, size : 2 * size] = term_key
+    at("terms")
     if layer == 1:
         dx_ref[...] = dx
     else:
@@ -1134,8 +1619,7 @@
         late[1].finish()
         late[2].leave()
         dx_ref[...] = dx
-    for move in moves:
-        move.finish()
+    at("end")
 
 
 def expert_grads_kernel(nz, step, ins, outs, scratch):
@@ -1193,45 +1677,36 @@
         pltpu.make_async_copy(stage.at[slot], outs[0].at[pl.ds(0, step)], out_sem.at[slot]).wait()
 
 
-def attend_grads_kernel(nz, q_cols, size, ins, outs, scratch):
-    s, z = lax.axis_index("section"), lax.axis_index("expert")
-    spaces, sems, d_sem = scratch[:4], scratch[4], scratch[5]
+def attend_grads_kernel(q_cols, size, ins, outs, scratch):
+    s = lax.axis_index("section")
+    spaces, sems = scratch[:4], scratch[4]
     a_s, o_s, t_s, d_s = spaces
-    early, blocks, late = ins[:3], ins[3 : 3 + nz], ins[3 + nz :]
-
-    def loads(refs):
+
+    def loads(layer):
+        refs = ins[4 * layer : 4 * layer + 4]
         return [pltpu.make_async_copy(r, d, sems.at[i]) for i, (r, d) in enumerate(zip(refs, spaces))]
 
-    def parts(layer):
-        out = []
-        for k in range(nz):
-            spot = partner(z, jnp.int32(k), nz)
-            src = blocks[k] if layer == 0 else late[3].at[:, spot]
-            out.append(pltpu.make_async_copy(src, d_s.at[:, spot], d_sem.at[k]))
-        return out
-
-    for layer, refs in enumerate((early, late[:3])):
+    for layer in range(2):
 
         @pl.when(s == layer)
         def _():
-            for load in loads(refs) + parts(layer):
+            for load in loads(layer):
                 load.start()
 
-    waits = loads(early)
+    waits = loads(0)
 
     def flat(ref):
         return ref[...].reshape(-1, ref.shape[-1])
 
-    waits[1].wait()
-    waits[2].wait()
-    outs[3][...] = dot_tn(flat(o_s), flat(t_s))
     waits[0].wait()
-    for load in parts(0):
-        load.wait()
+    waits[3].wait()
     grad = dot_tn(flat(a_s), flat(d_s))
     outs[0][...] = grad[:, :q_cols]
     outs[1][...] = grad[:, q_cols : q_cols + size]
     outs[2][...] = grad[:, q_cols + size :]
+    waits[1].wait()
+    waits[2].wait()
+    outs[3][...] = dot_tn(flat(o_s), flat(t_s))
 
 
 def shape_of(shape, dtype):
@@ -1248,7 +1723,7 @@
 
     return pl.pallas_call(
         kernel,
-        out_shape=tuple(o for o, _ in outs),
+        out_shape=tuple(shape_of(o.shape, o.dtype) for o, _ in outs),
         in_specs=[spec for _, spec in ins],
         out_specs=tuple(spec for _, spec in outs),
         scratch_shapes=list(scratch),
@@ -1257,6 +1732,113 @@
         ),
         name=name,
     )(*[value for value, _ in ins])
+
+
+class Slot:
+    def __init__(self, shape):
+        self.shape, self.dtype, self.value = tuple(shape.shape), shape.dtype, None
+
+
+class At:
+    def __init__(self, stage, plan, moves):
+        self.stage, self.plan, self.moves = stage, plan, moves
+
+    def __call__(self, point):
+        for name, act in self.plan.get((self.stage, point), ()):
+            act(self.moves[name])
+
+
+USUAL = {
+    "second": None,
+    "looped": 1, "out": 1, "dqkv": 1,
+    "collected": 2, "reduced": 2,
+    "spread": 3, "terms": 3,
+}
+
+
+class Group:
+    def __init__(self, name, number, fused):
+        self.name, self.number, self.fused = name, number, fused
+        self.stages, self.moves, self.plan = [], {}, {}
+
+    def stage(self, name, body, ins, outs, scratch):
+        slots = [Slot(shape) for shape, _ in outs]
+        self.stages.append((name, body, ins, list(zip(slots, [spec for _, spec in outs])), scratch))
+        return slots
+
+    def move(self, name, stage, move, ins, outs, plan, start="begin", manual=False):
+        slots = [Slot(shape) for shape in outs]
+        self.moves[name] = (stage, move, ins, [(slot, ANY) for slot in slots])
+        if not self.fused:
+            plan = []
+            if not manual:
+                plan = [(stage, start, lambda m: m.start()), (stage, "end", lambda m: m.finish())]
+                for point, turn in USUAL.items():
+                    if turn:
+                        plan.append((stage, point, lambda m, turn=turn: m.poll(turn)))
+        for at_stage, point, act in plan:
+            self.plan.setdefault((at_stage, point), []).append((name, act))
+        return slots
+
+    def run(self):
+        if self.fused:
+            self.launch(self.name, self.number, self.stages, list(self.moves))
+            return
+        for i, stage in enumerate(self.stages):
+            names = [name for name, entry in self.moves.items() if entry[0] == stage[0]]
+            self.launch(stage[0], self.number + i, [stage], names)
+
+    def launch(self, name, number, stages, names):
+        moves = [self.moves[n] for n in names]
+        outs = [pair for stage in stages for pair in stage[3]] + [p for m in moves for p in m[3]]
+        out_at = {id(slot): i for i, (slot, _) in enumerate(outs)}
+        ins, in_at, scratch, scratch_at = [], {}, [], {}
+
+        def place(pairs):
+            where = []
+            for value, spec in pairs:
+                if id(value) in out_at:
+                    where.append(("out", out_at[id(value)]))
+                    continue
+                key = (id(value), id(spec))
+                if key not in in_at:
+                    in_at[key] = len(ins)
+                    ins.append((value.value if isinstance(value, Slot) else value, spec))
+                where.append(("in", in_at[key]))
+            return where
+
+        def reserve(items):
+            where = []
+            for item in items:
+                key, space = item if isinstance(item, tuple) else (None, item)
+                if key is not None and key in scratch_at:
+                    where.append(scratch_at[key])
+                    continue
+                scratch.append(space)
+                where.append(len(scratch) - 1)
+                if key is not None:
+                    scratch_at[key] = len(scratch) - 1
+            return where
+
+        stage_at = [(place(st[2]), [out_at[id(o)] for o, _ in st[3]], reserve(st[4])) for st in stages]
+        move_at = [
+            (place(m[2]), [out_at[id(o)] for o, _ in m[3]], reserve(m[1].scratch())) for m in moves
+        ]
+
+        def body(in_refs, out_refs, scratch_refs):
+            def pick(places):
+                where, results, spaces = places
+                refs = [(out_refs if kind == "out" else in_refs)[i] for kind, i in where]
+                return refs, [out_refs[i] for i in results], [scratch_refs[i] for i in spaces]
+
+            bound = {n: m[1].bind(*pick(at)) for n, m, at in zip(names, moves, move_at)}
+            for i, stage in enumerate(stages):
+                hello = greet if i == 0 else lambda peers: None
+                stage[1](hello, At(stage[0], self.plan, bound), *pick(stage_at[i]))
+
+        results = call(body, name, number, ins, outs, scratch)
+        for (slot, _), value in zip(outs, results):
+            slot.value = value
 
 
 def vm(*values):
@@ -1287,17 +1869,19 @@
     wq, wk, wv, wo = w_query[0], key_weight[0], value_weight[0], w_output[0]
     gains = jnp.concatenate([attn_gain, moe_gain, query_gain, key_norm_gain], axis=1)
 
-    spaces = [
-        pltpu.VMEM((width, q_cols), BF16),
-        pltpu.VMEM((width, size), BF16),
-        pltpu.VMEM((width, size), BF16),
-        pltpu.VMEM((q_cols, width), BF16),
-        pltpu.VMEM((block, width), F32),
-        pltpu.VMEM((block, width), BF16),
-        pltpu.VMEM((nt, rows, width), BF16),
-        dma((nt,)),
-        dma((nt,)),
-    ]
+    def attend_spaces(own):
+        return [
+            ("wq", pltpu.VMEM((width, q_cols), BF16)),
+            ("wk", pltpu.VMEM((width, size), BF16)),
+            ("wv", pltpu.VMEM((width, size), BF16)),
+            ("wo", pltpu.VMEM((q_cols, width), BF16)),
+            ("part", pltpu.VMEM((block, width), F32)),
+            pltpu.VMEM((block, width), BF16),
+            pltpu.VMEM((nt, rows, width), BF16),
+            dma((nt,)),
+            dma((nt,)),
+        ]
+
     gathered = [
         shape_of((width, q_cols), BF16),
         shape_of((width, size), BF16),
@@ -1315,36 +1899,42 @@
         shape_of((block, size), BF16),
         shape_of((block, q_cols), BF16),
     )
-    expert_scratch = [pltpu.VMEM((hidden, width), BF16)] * 3
-
-    def binder(kinds):
-        def bind(ins, outs, scratch):
-            return [
-                kind.bind(ins[i] if i < len(ins) else None, outs[i], scratch[3 * i : 3 * i + 3])
-                for i, kind in enumerate(kinds)
-            ]
-
-        return bind
-
-    def shapes_of(kinds, values):
-        out = []
-        for kind, value in zip(kinds, values):
-            if isinstance(kind, Near):
-                out.append(like(value, (2,) if kind.both else ()))
-            elif kind.sliced:
-                out.append(shape_of((2, nz, block, width // nz), value.dtype))
-            else:
-                out.append(like(value, (2, nz)))
-        return out
-
-    def scratch_of(kinds):
-        return [sem for kind in kinds for sem in kind.scratch()]
-
+    expert_scratch = [("wg", pltpu.VMEM((hidden, width), BF16)), ("wu", pltpu.VMEM((hidden, width), BF16))]
+    expert_scratch += [("wd", pltpu.VMEM((hidden, width), BF16))]
+    hid_scratch = [(n, pltpu.VMEM((nz, block, hidden), BF16)) for n in ("hid", "dg", "du")]
+    all_tokens = shape_of((nz, block, width), BF16)
+    all_hidden = shape_of((nz, block, hidden), BF16)
+    cols = width // nz
+    sliced = [shape_of((2, nz, block, cols), BF16), shape_of((2, nz, rows, cols), BF16)]
+
+    def start(move):
+        move.start()
+
+    def finish(move):
+        move.finish()
+
+    def poll(turn):
+        return lambda move: move.poll(turn)
+
+    def steps(arrays, k):
+        return lambda move: [move.step(a, k) for a in arrays]
+
+    def begins(*arrays):
+        return lambda move: [move.begin(a) for a in arrays]
+
+    def settles(*arrays):
+        return lambda move: [move.settle(a) for a in arrays]
+
+    def ends_of(move):
+        for a in range(4):
+            move.end(a)
+
+    fused = nz <= 4
+    fore = Group("forward", 0, fused)
     relay = Relay(0, (0, 0, 0, 1), nz)
-    started = call(
+    started = fore.stage(
+        "attend_0",
         functools.partial(start_attend_kernel, nz, nt, heads, relay),
-        "start_attend_0",
-        0,
         [(seq_lengths[0, :, 0], SM)]
         + vm(expert_ids[0], route_weights[0])
         + any_place(boundary[0], gains, wq, wk, wv, wo, wg, wu, wd),
@@ -1363,112 +1953,101 @@
             pltpu.VMEM(gains.shape, F32),
             pltpu.VMEM((2, 3, block, size), F32),
             pltpu.VMEM((2, block, LANES), F32),
-            dma((4,)), dma((3,)), dma((4,)), dma((6,)), dma((6,)), dma((2, nz)), dma((2, nz)),
+            dma((4,)), dma((3,)), dma((5,)), dma((6,)), dma((6,)), dma((2, nz)), dma((2, nz)),
         ]
         + relay.scratch(4)
-        + spaces,
+        + attend_spaces(0),
     )
     edges, tabs_all, gates_all, gains_all = started[:4]
     weights_0 = started[4:8]
     expert_weights = (wg, wu, wd) + tuple(started[8:11])
     h1_0, b_0, a_0, q_0, k_0, v_0, qr_0, kr_0, o_0 = started[11:]
 
-    def run_experts(layer, b, h1, move_ins, move_outs, move_scratch, bind):
-        return call(
-            functools.partial(experts_kernel, layer, nz, nt, local_experts, bind),
-            f"experts_{layer}",
-            1 + layer,
-            vm(b, h1, gates_all) + any_place(*expert_weights, *move_ins),
-            vm(shape_of((block, width), BF16))
-            + any_place(
-                shape_of((nz, block, width), BF16),
-                shape_of((nz, block, hidden), F32),
-                shape_of((nz, block, hidden), F32),
-                *move_outs,
-            ),
-            expert_scratch
-            + [pltpu.VMEM((nz, block, hidden), F32)] * 2
-            + [dma((3,)), dma((3,))]
-            + exchange_scratch(nz, nt, rows, block, width)
-            + move_scratch,
-        )
-
-    def experts_back(layer, dy, h1, gate_pre, up_pre, move_ins, move_outs, move_scratch, bind):
-        return call(
-            functools.partial(experts_back_kernel, layer, nz, nt, local_experts, bind),
-            f"experts_back_{layer}",
-            3 + layer,
-            vm(dy, h1, gains_all, gates_all)
-            + any_place(gate_pre, up_pre, *expert_weights, *move_ins),
-            vm(
-                shape_of((block, width), BF16),
-                shape_of((rows, width), F32),
-                shape_of((1, width), F32),
-            )
-            + any_place(
-                shape_of((nz, block, width), BF16),
-                shape_of((nz, block, hidden), BF16),
-                shape_of((nz, block, hidden), BF16),
-                shape_of((nz, block, hidden), BF16),
-                *move_outs,
-            ),
-            expert_scratch
-            + [pltpu.VMEM((2, block, hidden), F32)] * 2
-            + [pltpu.VMEM((nz, block, hidden), BF16)] * 3
-            + [dma((3,)), dma((2,)), dma((2,)), dma((4,))]
-            + exchange_scratch(nz, nt, rows, block, width)
-            + move_scratch,
-        )
-
-    relay_1 = Relay(1, (0, 0, 0, 1), nz)
-    ran = run_experts(
-        0, b_0, h1_0, (wq, wk, wv, wo), gathered, relay_1.scratch(4),
-        lambda ins, outs, scratch: [relay_1.bind(ins, outs, scratch)],
-    )
-    x_1, ball_0, gp_0, up_0 = ran[:4]
-    weights_1 = tuple(ran[4:])
-
-    kinds = (Gather(0, nz, True),)
-    values = (a_0,)
-    attended = call(
-        functools.partial(attend_kernel, 1, nz, nt, heads, binder(kinds)),
+    x_1, ball_0, gp_0, up_0 = fore.stage(
+        "experts_0",
+        functools.partial(experts_kernel, 0, nz, nt, local_experts),
+        vm(b_0, h1_0) + any_place(gates_all, *expert_weights),
+        vm(shape_of((block, width), BF16))
+        + any_place(
+            all_tokens,
+            shape_of((nz, block, hidden), F32),
+            shape_of((nz, block, hidden), F32),
+        ),
+        expert_scratch
+        + [pltpu.VMEM((nz, block, hidden), F32)] * 2
+        + [pltpu.VMEM((nz, block, LANES), F32), dma((4,)), dma((3,))]
+        + exchange_scratch(nz, nt, rows, block, width),
+    )
+
+    weights_1 = fore.move(
+        "weights_1", "experts_0", Relay(1, (0, 0, 0, 1), nz), any_place(wq, wk, wv, wo), gathered,
+        [
+            ("attend_0", "shards", begins(0, 1, 2)),
+            ("experts_0", "begin", steps((0, 1, 2), 1)),
+            ("experts_0", "begin", begins(3)),
+            ("experts_0", "second", steps((0, 1, 2), 2)),
+            ("experts_0", "looped", steps((3,), 1)),
+            ("experts_0", "collected", steps((0, 1, 2), 3)),
+            ("experts_0", "spread", steps((3,), 2)),
+            ("attend_1", "qkv", settles(0, 1, 2)),
+            ("attend_1", "out", steps((3,), 3)),
+            ("attend_1", "out", settles(3)),
+            ("attend_1", "end", ends_of),
+        ],
+    )
+
+    (dy_rows,) = fore.move(
+        "dy_rows", "attend_0", RowsFar(1, nz, nt), any_place(edges), [shape_of((nz, rows, width), BF16)],
+        [("experts_0", "looped", start), ("attend_1", "begin", finish)],
+        "shards",
+    )
+    (dyall_1,) = fore.move(
+        "dy_all", "experts_0", Spread(nz, nt), any_place(dy_rows), [all_tokens],
+        [("attend_1", "begin", start), ("attend_1", "out", poll(1)), ("attend_1", "end", finish)],
+    )
+
+    h1_1, b_1, a_1, q_1, k_1, v_1, qr_1, kr_1, o_1 = fore.stage(
         "attend_1",
-        5,
-        vm(x_1, tabs_all, gains_all) + any_place(*weights_1, *values),
-        attend_outs + any_place(*shapes_of(kinds, values)),
-        [dma((4,))] + spaces + scratch_of(kinds),
-    )
-    h1_1, b_1, a_1, q_1, k_1, v_1, qr_1, kr_1, o_1 = attended[:9]
-    aall_0 = attended[9]
-
-    kinds = (Gather(0, nz), Near(0))
-    values = (o_0, ball_0)
-    ran = run_experts(
-        1, b_1, h1_1, values, shapes_of(kinds, values), scratch_of(kinds), binder(kinds)
-    )
-    y_1, ball_1, gp_1, up_1 = ran[:4]
-    oall_0, bnear_0 = ran[4:]
-
-    dy_1 = lax.dynamic_slice_in_dim(edges[1], lax.axis_index("tensor") * rows, rows, 0)
-    kinds = (Gather(1, nz), Near(1), Near(1, True))
-    values = (o_1, ball_1, y_1)
-    ran = experts_back(
-        1, dy_1, h1_1, gp_1, up_1, values, shapes_of(kinds, values), scratch_of(kinds), binder(kinds)
-    )
-    dat_1, dh1_1, tm_1, dyall_1, hid_1, dg_1, du_1 = ran[:7]
-    oall_1, bnear_1, ends_1 = ran[7:]
-
-    def attend_back(layer, x, source, dat, dh1, term_moe, kept, weights, kinds, values, late):
+        functools.partial(attend_kernel, 1, nz, nt, heads),
+        vm(x_1) + any_place(tabs_all, gains_all, *weights_1),
+        attend_outs,
+        [dma((6,)), pltpu.VMEM((3, block, size), F32), pltpu.VMEM(gains.shape, F32)] + attend_spaces(1),
+    )
+    aall_0, _ = fore.move(
+        "a_0", "attend_1", Slice(0, nz, nt), any_place(a_0), sliced,
+        [("attend_1", "begin", start), ("attend_1", "out", poll(1)), ("attend_1", "end", finish)],
+    )
+    fore.run()
+
+    back = Group("backward", 8, fused)
+    dy_1 = lax.dynamic_slice_in_dim(edges.value[1], lax.axis_index("tensor") * rows, rows, 0)
+    dat_1, dh1_1, tm_1, ball_1, yparts_1, hid_1, dg_1, du_1 = back.stage(
+        "both_1",
+        functools.partial(experts_both_kernel, 1, nz, nt, local_experts),
+        vm(b_1, h1_1, dy_1, gains_all) + any_place(gates_all, dyall_1, *expert_weights),
+        vm(
+            shape_of((block, width), BF16),
+            shape_of((rows, width), F32),
+            shape_of((1, width), F32),
+        )
+        + any_place(all_tokens, all_tokens, all_hidden, all_hidden, all_hidden),
+        expert_scratch
+        + [pltpu.VMEM((2, block, width), BF16)] * 2
+        + hid_scratch
+        + [dma((4,)), dma((2,)), dma((2,)), dma((4,)), ("gates", pltpu.VMEM((nz, block, LANES), F32))]
+        + exchange_scratch(nz, nt, rows, block, width),
+    )
+
+    def attend_back(layer, x, source, dat, dh1, term_moe, kept, weights, others=None):
         outs = vm(
             shape_of((rows, width), BF16),
             shape_of((block, q_cols + 2 * size), BF16),
             shape_of((TERM_ROWS, TERM_COLS), F32),
         )
-        scratch = spaces + [dma((4,)), dma((nt,)), dma((nt,))]
-        ins = vm(x, tabs_all, gains_all, dat, dh1, term_moe, *kept) + any_place(*weights)
-        shapes = [o for o, _ in outs]
-        late_shapes = []
-        if late is not None:
+        scratch = attend_spaces(layer) + [dma((5,)), dma((nt,)), dma((nt,))]
+        scratch += [pltpu.VMEM((rows, width), BF16)]
+        ins = any_place(x) + vm(tabs_all, gains_all, dat, dh1, term_moe, *kept) + any_place(*weights)
+        if others is not None:
             outs += vm(shape_of((TERM_ROWS, TERM_COLS), F32))
             scratch += [
                 pltpu.VMEM((block, width), BF16),
@@ -1478,46 +2057,112 @@
                 dma((nt,)),
                 dma((nt,)),
             ]
-            ins += any_place(late)
-            last = (Near(0, True), Near(0, True), Gather(0, nz))
-            late_shapes = shapes_of(last, (shapes[1], shape_of((block, width), BF16), shapes[2]))
-            kinds = kinds + last
-        return call(
-            functools.partial(attend_back_kernel, layer, source, nz, nt, heads, binder(kinds)),
+            ins += any_place(others)
+        return back.stage(
             f"attend_back_{layer}",
-            6 + layer,
-            ins + any_place(*values),
-            outs + any_place(*shapes_of(kinds[: len(values)], values), *late_shapes),
-            scratch + scratch_of(kinds),
-        )
-
-    kinds = (Gather(1, nz, True), Near(1), Near(1), Near(1), Near(1), Gather(1, nz, True))
-    values = (dat_1, dg_1, du_1, hid_1, dyall_1, a_1)
-    ran = attend_back(
-        1, x_1[None], 0, dat_1, dh1_1, tm_1, (q_1, k_1, v_1, qr_1, kr_1), weights_1, kinds, values, None
-    )
-    dx_1, dqkv_1, terms_1 = ran[:3]
-    datall_1, near_1, aall_1 = ran[3], ran[4:8], ran[8]
-
-    kinds = (Gather(1, nz), Gather(1, nz))
-    values = (dqkv_1, terms_1)
-    ran = experts_back(
-        0, dx_1, h1_0, gp_0, up_0, values, shapes_of(kinds, values), scratch_of(kinds), binder(kinds)
-    )
-    dat_0, dh1_0, tm_0, dyall_0, hid_0, dg_0, du_0 = ran[:7]
-    dqkvall_1, termsall_1 = ran[7:]
-
-    kinds = (Gather(0, nz, True), Near(0), Near(0), Near(0), Near(0))
-    values = (dat_0, dg_0, du_0, hid_0, dyall_0)
-    ran = attend_back(
-        0, edges, 0, dat_0, dh1_0, tm_0, (q_0, k_0, v_0, qr_0, kr_0), weights_0, kinds, values, termsall_1
-    )
-    terms, datall_0, near_0 = ran[3], ran[4], ran[5:9]
-    dqkv_both, ends_0 = ran[9:11]
-    dqkv_0 = [dqkv_both]
-    for k in range(1, nz):
-        pairs = [(place, place ^ k) for place in range(nz)]
-        dqkv_0.append(lax.ppermute(dqkv_both, ("section", "expert"), pairs))
+            functools.partial(attend_back_kernel, layer, source, nz, nt, heads),
+            ins,
+            outs,
+            scratch,
+        )
+
+    last = ("attend_back_0", "end", finish)
+    kept_1, kept_0 = (q_1, k_1, v_1, qr_1, kr_1), (q_0, k_0, v_0, qr_0, kr_0)
+    dx_1, dqkv_1, terms_1 = attend_back(1, x_1, None, dat_1, dh1_1, tm_1, kept_1, weights_1)
+    dat_0, dh1_0, tm_0, dyall_0, hid_0, dg_0, du_0 = back.stage(
+        "experts_back_0",
+        functools.partial(experts_back_kernel, 0, nz, nt, local_experts),
+        vm(dx_1, h1_0, gains_all) + any_place(gates_all, gp_0, up_0, *expert_weights),
+        vm(
+            shape_of((block, width), BF16),
+            shape_of((rows, width), F32),
+            shape_of((1, width), F32),
+        )
+        + any_place(all_tokens, all_hidden, all_hidden, all_hidden),
+        expert_scratch
+        + [pltpu.VMEM((2, block, hidden), F32)] * 2
+        + hid_scratch
+        + [dma((4,)), dma((2,)), dma((2,)), dma((4,)), ("gates", pltpu.VMEM((nz, block, LANES), F32))]
+        + exchange_scratch(nz, nt, rows, block, width),
+    )
+
+    def gather(name, stage, layer, value, begin, end=last):
+        return back.move(
+            name, stage, Gather(layer, nz), any_place(value), [like(value, (2, nz))],
+            [begin + (start,), end], begin[1],
+        )
+
+    def near(name, stage, layer, value):
+        return back.move(
+            name, stage, Near(layer), any_place(value), [like(value)], [(stage, "begin", start), last]
+        )
+
+    def columns(name, stage, layer, value, begin, middle):
+        return back.move(
+            name, stage, Slice(layer, nz, nt), any_place(value), sliced,
+            [begin + (start,), middle + (poll(1),), last], begin[1] if begin[0] == stage else "begin",
+        )
+
+    (bnear_0,) = near("b_0", "both_1", 0, ball_0)
+    (oall_0,) = gather("o_0", "both_1", 0, o_0, ("both_1", "arrived"))
+    aall_1, _ = columns(
+        "a_1", "both_1", 1, a_1, ("both_1", "looped"), ("attend_back_1", "dqkv")
+    )
+    (oall_1,) = gather("o_1", "attend_back_1", 1, o_1, ("attend_back_1", "begin"))
+    near_1 = [
+        near(f"near_1_{i}", "attend_back_1", 1, value)[0]
+        for i, value in enumerate((dg_1, du_1, hid_1, ball_1, dyall_1))
+    ]
+    datall_1, _ = columns(
+        "dat_1", "attend_back_1", 1, dat_1, ("attend_back_1", "begin"), ("attend_back_1", "reduced")
+    )
+    (ysums_1,) = back.move(
+        "y_near", "attend_back_1", SumNear(nz, nt, rows, block, width), any_place(yparts_1),
+        [shape_of((nz, rows, width), BF16)],
+        [
+            ("attend_back_1", "begin", start),
+            ("attend_back_1", "dqkv", poll(1)),
+            ("attend_back_1", "end", poll(2)),
+            ("attend_back_1", "end", finish),
+        ],
+    )
+    (dqkvall_1,) = gather("dqkv_1", "experts_back_0", 1, dqkv_1, ("experts_back_0", "arrived"))
+    (termsall_1,) = gather(
+        "terms_1", "experts_back_0", 1, terms_1, ("experts_back_0", "begin"),
+        ("attend_back_0", "begin", finish),
+    )
+    (yrows_1,) = back.move(
+        "y_far", "experts_back_0", SumFar(nz, rows, width), any_place(ysums_1) + vm(h1_1),
+        [shape_of((rows, width), BF16)],
+        [
+            ("experts_back_0", "arrived", start),
+            ("experts_back_0", "spread", poll(2)),
+            ("experts_back_0", "end", finish),
+        ],
+    )
+    _, dqkv_0, terms_0, terms = attend_back(
+        0, edges, 0, dat_0, dh1_0, tm_0, kept_0, weights_0, termsall_1
+    )
+    datall_0, _ = columns(
+        "dat_0", "attend_back_0", 0, dat_0, ("attend_back_0", "begin"), ("attend_back_0", "reduced")
+    )
+    near_0 = [bnear_0] + [
+        near(f"near_0_{i}", "attend_back_0", 0, value)[0]
+        for i, value in enumerate((dyall_0, dg_0, du_0, hid_0))
+    ]
+    (ends_1,) = back.move(
+        "y_spread", "attend_back_0", SpreadNear(1, nt, block, width), any_place(yrows_1),
+        [shape_of((2, block, width), BF16)],
+        [("attend_back_0", "begin", start), ("attend_back_0", "dqkv", poll(1)), last],
+    )
+    hand = [("dqkv_0", Gather(0, nz), like(dqkv_0, (2, nz)))]
+    hand += [("dx_0", Near(0, True), shape_of((2, block, width), BF16))]
+    hand += [("terms_0", Gather(0, nz), like(terms_0, (2, nz)))]
+    dqkvall_0, ends_0, _ = (
+        back.move(name, "attend_back_0", move, [], [shape], [], manual=True)[0]
+        for name, move, shape in hand
+    )
+    back.run()
 
     step = 256
     flat = shape_of((hidden, width), F32)
@@ -1526,10 +2171,15 @@
         "expert_grads",
         None,
         any_place(
-            dg_0, du_0, hid_0, ball_0, dyall_0,
-            dg_1, du_1, hid_1, ball_1, dyall_1,
-            *near_0[:3], bnear_0, near_0[3],
-            *near_1[:3], bnear_1, near_1[3],
+            *(
+                slot.value
+                for slot in (
+                    dg_0, du_0, hid_0, ball_0, dyall_0,
+                    dg_1, du_1, hid_1, ball_1, dyall_1,
+                    *near_0[2:], *near_0[:2],
+                    *near_1,
+                )
+            )
         ),
         any_place(flat, flat, flat),
         [
@@ -1540,9 +2190,11 @@
             dma((2,)),
         ],
     )
-    operands = (aall_0, oall_0, datall_0, *dqkv_0, aall_1, oall_1, datall_1, dqkvall_1)
+    operands = (aall_0, oall_0, datall_0, dqkvall_0, aall_1, oall_1, datall_1, dqkvall_1)
+    operands = tuple(slot.value for slot in operands)
+    terms = terms.value
     grad_query, grad_key, grad_value, grad_output = call(
-        functools.partial(attend_grads_kernel, nz, q_cols, size),
+        functools.partial(attend_grads_kernel, q_cols, size),
         "attend_grads",
         None,
         any_place(*operands),
@@ -1552,9 +2204,9 @@
             shape_of(wv.shape, F32),
             shape_of(wo.shape, F32),
         ),
-        [pltpu.VMEM(o.shape, o.dtype) for o in operands[-4:]] + [dma((3,)), dma((nz,))],
-    )
-    ends = jnp.where(lax.axis_index("section") == 0, ends_0, ends_1)
+        [pltpu.VMEM(o.shape, o.dtype) for o in operands[:4]] + [dma((4,))],
+    )
+    ends = jnp.where(lax.axis_index("section") == 0, ends_0.value, ends_1.value)
     return (
         ends[None],
         terms[8:16].reshape(1, width),

time: 541 us -> 507 us (0.937)
  Pallas kernels: 507 us -> 488 us
  starting transfers between devices: 10.4 us -> 0 us
    pallas_call x10 -> x4, Pallas kernels: 507 us -> 488 us  [call(): pl.pallas_call(kernel, out_shape=tuple((shape_of(o.shape, o.dtype) for o,...]
    ppermute x3 -> x0, starting transfers between devices: 10.4 us -> none  [on_device(): dqkv_0.append(lax.ppermute(dqkv_both, ('section', 'expert'), pairs))]
  transfers between devices with their start and end apart: 3 -> 0, of which waited for: 1 -> 0; matrix products, arithmetic and copies ran while one was open for 1% -> 0% of each run, Pallas kernels for 3% -> 0%
where the time goes in v4:
time: 507 us; the launch traced here: 499 us
  Pallas kernels  488 us (96%)
  local copies, waits for them, and re-layouts  6.46 us (1%)
    pallas_call x4, Pallas kernels, call(): pl.pallas_call(kernel, out_shape=tuple((shape_of(o.shape, o.dtype) for o,...  488 us

profile of v4, /device:TPU:0, one launch (start us, length us, event | category | flops | bytes accessed | tf_op | source)
XLA Modules:
  0.0 499.0 jit_solution(10080881961548552369)
XLA Ops:
  0.7 1.4 pad_maximum_fusion.refs_4_
  2.0 1.5 copy.27
  3.5 1.5 copy.28
  5.0 243.5 %forward.1 = (bf16[2,128,2048]{2,1,0:T(8,128)(2,1)}, f32[2,3,128,128]{3,2,1,0:T(8,128)}, f32[2,4,128,128]{3,2,1,0:T(8,128)}, f32[2,1,4352]{2,1,0:T(1,128)}, bf16...) custom-call(s32[2,4]{1,0:T(2,128)} %bitcast.45, ...), custom_call_target="tpu_custom_call" | custom-call | tf_op jit(solution)/shard_map/forward/pallas_call | solution.py:1724
  248.5 1.1 slice.15
  249.6 0.7 dynamic-slice_bitcast_fusion.refs_2_
  250.3 220.7 %backward.1 = (bf16[128,2048]{1,0:T(8,128)(2,1)}, f32[32,2048]{1,0:T(8,128)}, f32[1,2048]{1,0:T(1,128)}, bf16[4,128,2048]{2,1,0:T(8,128)(2,1)}, bf16[4,128,2048]...) custom-call(bf16[32,2048]{1,0:T(8,128)(2,1)} %get-tuple-element.84.r, ...), custom_call_target="tpu_custom_call" | custom-call | tf_op jit(solution)/shard_map/backward/pallas_call | solution.py:1724
  471.0 0.0 copy-start
  471.0 2.3 select_bitcast_fusion
  473.3 0.0 copy-done
  473.3 0.5 fusion
  473.8 0.6 copy.30
  474.4 0.6 copy.29
  475.0 7.7 %attend_grads.1 = (f32[512,1024]{1,0:T(8,128)}, f32[512,128]{1,0:T(8,128)}, f32[512,128]{1,0:T(8,128)}, f32[1024,512]{1,0:T(8,128)}) custom-call(bf16[2,4,128,512]{3,2,1,0:T(8,128)(2,1)} %get-tuple-element.123.refs_0_, bf16[2,4,128,1024]{3,2,1,0:T(8,128)(2,1)} %get-tuple-element.124.refs_1_, bf16[2,4,128,512]{3,2,1,0:T(8,128)(2,1)} %get-tuple-element.125.refs_2_, ...), custom_call_target="tpu_custom_call" | custom-call | tf_op jit(solution)/shard_map/attend_grads/pallas_call | solution.py:1724
  482.8 15.9 %expert_grads.1 = (f32[768,2048]{1,0:T(8,128)}, f32[768,2048]{1,0:T(8,128)}, f32[768,2048]{1,0:T(8,128)}) custom-call(bf16[4,128,768]{2,1,0:T(8,128)(2,1)} %get-tuple-element.135.refs_0_, bf16[4,128,768]{2,1,0:T(8,128)(2,1)} %get-tuple-element.136.refs_1_, bf16[4,128,768]{2,1,0:T(8,128)(2,1)} %get-tuple-element.137.refs_2_, ...), custom_call_target="tpu_custom_call" | custom-call | tf_op jit(solution)/shard_map/expert_grads/pallas_call | solution.py:1724
  (1 shorter events, 0.0 us)
Async XLA Ops:
  471.0 2.3 copy-start

commit v5 on v4

--- a/solution.py
+++ b/solution.py
@@ -14,6 +14,7 @@
 TERM_ROWS = 24
 TERM_COLS = 256
 MESH = pl.DeviceIdType.MESH
+SECTION, EXPERT, TENSOR = "section", "expert", "tensor"
 F32 = jnp.float32
 BF16 = jnp.bfloat16
 VMEM_LIMIT = 62 * 1024 * 1024
@@ -21,6 +22,20 @@
 ANY = pl.BlockSpec(memory_space=pl.ANY)
 VM = pl.BlockSpec(memory_space=pltpu.VMEM)
 SM = pl.BlockSpec(memory_space=pltpu.SMEM)
+
+(
+    BEGIN, END, SPREAD, ARRIVED, SECOND, LOOPED, COLLECTED, TABLES, QKV, SHARDS, SENT, OUT, REDUCED, DQKV, TERMS, TAIL,
+) = range(0, 16)
+(
+    ATTEND_0, EXPERTS_0, ATTEND_1, BOTH_1, ATTEND_BACK_1, EXPERTS_BACK_0, ATTEND_BACK_0,
+) = range(0, 7)
+(
+    MOVE_WEIGHTS_1, MOVE_DY_ROWS, MOVE_DY_ALL, MOVE_B_0, MOVE_O_0, MOVE_A_0, MOVE_A_1, MOVE_O_1, MOVE_DAT_1, MOVE_Y_NEAR, MOVE_DQKV_1, MOVE_TERMS_1, MOVE_Y_FAR, MOVE_DAT_0, MOVE_Y_SPREAD, MOVE_DQKV_0, MOVE_DX_0, MOVE_TERMS_0,
+) = range(0, 18)
+NEAR_0, NEAR_1 = 40, 50
+(
+    SHARED_PART, SHARED_OWN, SHARED_GATES, SHARED_WG, SHARED_WU, SHARED_WD, SHARED_WQ, SHARED_WK, SHARED_WV, SHARED_WO, SHARED_HID, SHARED_DG, SHARED_DU,
+) = range(0, 13)
 
 
 def partner(index, k, count):
@@ -56,7 +71,7 @@
 def layer_peers(z, t, nz, nt):
     i32 = jnp.int32
     peers = [{"expert": partner(z, i32(k), nz)} for k in range(1, nz)]
-    peers += [{"tensor": partner(t, i32(k), nt)} for k in range(1, nt)]
+    peers += [{TENSOR: partner(t, i32(k), nt)} for k in range(1, nt)]
     return peers
 
 
@@ -103,7 +118,7 @@
 class Square:
     def __init__(self, nz, nt, rows, width):
         assert nt == 4
-        self.z, self.t = lax.axis_index("expert"), lax.axis_index("tensor")
+        self.z, self.t = lax.axis_index(EXPERT), lax.axis_index(TENSOR)
         self.nz, self.rows = nz, rows
         half = width // 2
         self.half, self.first, self.second = half, pl.ds(0, half), pl.ds(half, half)
@@ -290,8 +305,8 @@
     return (
         [
             pltpu.VMEM((nz, block, width), BF16),
-            ("part", pltpu.VMEM((block, width), F32)),
-            ("own", pltpu.VMEM((nz, rows, width), F32)),
+            (SHARED_PART, pltpu.VMEM((block, width), F32)),
+            (SHARED_OWN, pltpu.VMEM((nz, rows, width), F32)),
             pltpu.VMEM((block, width), BF16),
             pltpu.SemaphoreType.DMA((2, nt)),
         ]
@@ -322,7 +337,7 @@
     for k in range(1, nz):
         gather.far_copy(k, z).start()
     gather.send(0, z)
-    at("begin")
+    at(BEGIN)
     ready()
     for k in range(1, nz):
         source = partner(z, i32(k), nz)
@@ -330,7 +345,7 @@
         gather.send(k, source)
         if k == 1:
             gather.hand_on(0, z)
-    at("arrived")
+    at(ARRIVED)
     gather.hand_on(1, partner(z, i32(1), nz))
 
     def step(k, carry):
@@ -351,16 +366,16 @@
 
         @pl.when(k == 2)
         def _():
-            at("second")
+            at(SECOND)
 
         return carry
 
     lax.fori_loop(1, nz + 1, step, 0)
-    at("looped")
+    at(LOOPED)
     sums.collect_far(i32(nz - 1))
     sums.pair_up(i32(0))
     sums.collect_own()
-    at("collected")
+    at(COLLECTED)
     sums.add_far()
 
     def finish():
@@ -403,7 +418,7 @@
     return wait
 
 
-def reduce_rows(t, nt, rows, part, outgoing, came, send_sem, recv_sem):
+def reduce_rows(t, nt, rows, part, outgoing, came, send_sem, recv_sem, at):
     i32 = jnp.int32
     outgoing[...] = part[...].astype(BF16)
 
@@ -419,6 +434,7 @@
 
     for j in range(1, nt):
         copy(j).start()
+    at(SENT)
     total = part[rows_at(t * rows, rows)]
     for j in range(1, nt):
         copy(j).wait_recv()
@@ -430,11 +446,11 @@
 
 def all_peers(s, z, t, nz, nt):
     i32 = jnp.int32
-    peers = [{"section": 1 - s}]
+    peers = [{SECTION: 1 - s}]
     for k in range(1, nz):
         zz = partner(z, i32(k), nz)
-        peers += [{"expert": zz}, {"section": 1 - s, "expert": zz}]
-    return peers + [{"tensor": partner(t, i32(j), nt)} for j in range(1, nt)]
+        peers += [{EXPERT: zz}, {SECTION: 1 - s, EXPERT: zz}]
+    return peers + [{TENSOR: partner(t, i32(j), nt)} for j in range(1, nt)]
 
 
 class Relay:
@@ -446,7 +462,7 @@
         return [dma((count,))] + [dma((count, self.nz))] * 6
 
     def bind(self, shards, outs, sems):
-        self.s, self.z = lax.axis_index("section"), lax.axis_index("expert")
+        self.s, self.z = lax.axis_index(SECTION), lax.axis_index(EXPERT)
         self.shards, self.outs, self.sems = shards, outs, sems
         self.source = self.hands = self.s == self.layer
         self.count = len(shards)
@@ -612,7 +628,7 @@
         return [dma((2,)), dma((self.nz,)), dma((2, self.nz)), dma((2, self.nt))]
 
     def bind(self, ins, outs, sems):
-        self.s, self.z, self.t = (lax.axis_index(a) for a in ("section", "expert", "tensor"))
+        self.s, self.z, self.t = (lax.axis_index(a) for a in (SECTION, EXPERT, TENSOR))
         self.src, (self.out, self.rows_out), self.sems = ins[0], outs, sems
         rows, self.cols = self.rows_out.shape[2:]
         self.rows = rows
@@ -702,7 +718,7 @@
         return [dma((1,)), dma((self.nz,)), dma((2, self.nz))]
 
     def bind(self, ins, outs, sems):
-        self.s, self.z = lax.axis_index("section"), lax.axis_index("expert")
+        self.s, self.z = lax.axis_index(SECTION), lax.axis_index(EXPERT)
         self.src, self.out, self.sems = (ins or (None,))[0], outs[0], sems
         return self
 
@@ -769,7 +785,7 @@
         return [dma((1,)), dma((1,)), dma((1,))]
 
     def bind(self, ins, outs, sems):
-        self.s, self.sems = lax.axis_index("section"), sems
+        self.s, self.sems = lax.axis_index(SECTION), sems
         self.src, self.out = (ins or (None,))[0], outs[0]
         return self
 
@@ -825,7 +841,7 @@
         return [pltpu.SemaphoreType.DMA((1,)), pltpu.SemaphoreType.DMA((2, self.nz))]
 
     def bind(self, ins, outs, sems):
-        self.z, self.t = lax.axis_index("expert"), lax.axis_index("tensor")
+        self.z, self.t = lax.axis_index(EXPERT), lax.axis_index(TENSOR)
         self.src, self.out, self.sems = ins[0], outs[0], sems
         return self
 
@@ -895,38 +911,75 @@
         self.shape = rows, block, width
 
     def scratch(self):
-        return [pltpu.SemaphoreType.DMA((2,))] + RowSum.scratch(self.nz, *self.shape)
+        rows, block, width = self.shape
+        half = width // 2
+        return [
+            pltpu.SemaphoreType.DMA((2,)),
+            pltpu.SemaphoreType.DMA((2, 5)),
+            pltpu.VMEM((self.nz, block, width), BF16),
+            pltpu.VMEM((self.nz, 2 * rows, half), BF16),
+            pltpu.VMEM((2, self.nz, rows, half), BF16),
+            pltpu.VMEM((2, self.nz, rows, half), BF16),
+            pltpu.VMEM((2, self.nz, rows, half), BF16),
+            pltpu.VMEM((self.nz, rows, width), BF16),
+        ]
 
     def bind(self, ins, outs, scratch):
-        self.src, self.out, self.sems = ins[0], outs[0], scratch[0]
+        self.src, self.out = ins[0], outs[0]
+        self.sems, self.sem = scratch[:2]
+        self.parts, self.from_y, self.from_x, self.pairs, self.came, self.result = scratch[2:]
         self.sq = Square(self.nz, self.nt, self.shape[0], self.shape[2])
-        self.sums = RowSum(self.sq, scratch[1:])
         return self
 
+    def load(self):
+        return pltpu.make_async_copy(self.src, self.parts, self.sems.at[0])
+
+    def save(self):
+        return pltpu.make_async_copy(self.result, self.out, self.sems.at[1])
+
+    def copy(self, i):
+        sq = self.sq
+        if i < 3:
+            window, cols = ((sq.y_pair, sq.first), (sq.across_rows, sq.second), (sq.x_rows, sq.second))[i]
+            src = self.src.at[:, window, cols]
+            dst = (self.from_y, self.from_x.at[1], self.from_x.at[0])[i]
+        else:
+            src, dst = self.pairs.at[i - 3], self.came.at[i - 3]
+        peer = sq.near[(1, 0, 0, 0, 1)[i]]
+        return remote(src, dst, self.sem.at[0, i], self.sem.at[1, i], tensor=peer)
+
     def start(self):
-        load = pltpu.make_async_copy(self.src, self.sums.outgoing, self.sems.at[0])
-        load.start()
-        load.wait()
-        for k in range(self.nz):
-            self.sums.send(k)
+        self.load().start()
+        for i in range(3):
+            self.copy(i).start()
 
     def poll(self, turn):
+        sq = self.sq
         if turn == 1:
-            for k in range(self.nz):
-                self.sums.pair_up(jnp.int32(k))
+            self.load().wait()
+            self.copy(0).wait_recv()
+            kept = self.parts[:, sq.x_rows, sq.first].astype(F32)
+            self.pairs[0] = (kept + self.from_y[:, sq.pair_x].astype(F32)).astype(BF16)
+            self.copy(3).start()
+            self.copy(1).wait_recv()
+            kept = self.parts[:, sq.y_rows, sq.second].astype(F32)
+            self.pairs[1] = (kept + self.from_x[1].astype(F32)).astype(BF16)
+            self.copy(4).start()
         if turn == 2:
-            for k in range(self.nz):
-                left, right = self.sums.collect(jnp.int32(k))
-                self.sums.passed[k, :, self.sq.first] = left.astype(BF16)
-                self.sums.passed[k, :, self.sq.second] = right.astype(BF16)
+            for i in (2, 3, 4):
+                self.copy(i).wait_recv()
+            left = self.parts[:, sq.mine, sq.first].astype(F32)
+            left = left + self.from_y[:, sq.pair_mine].astype(F32) + self.came[0].astype(F32)
+            right = self.parts[:, sq.mine, sq.second].astype(F32)
+            right = right + self.from_x[0].astype(F32) + self.came[1].astype(F32)
+            self.result[:, :, sq.first] = left.astype(BF16)
+            self.result[:, :, sq.second] = right.astype(BF16)
             self.save().start()
-
-    def save(self):
-        return pltpu.make_async_copy(self.sums.passed, self.out, self.sems.at[1])
 
     def finish(self):
         self.save().wait()
-        self.sums.leave(False)
+        for i in range(5):
+            self.copy(i).wait_send()
 
 
 class SumFar:
@@ -943,7 +996,7 @@
         ]
 
     def bind(self, ins, outs, scratch):
-        self.z = lax.axis_index("expert")
+        self.z = lax.axis_index(EXPERT)
         self.src, self.rows_ref = ins
         self.out = outs[0]
         self.came, self.result, self.sems, self.far_sem = scratch
@@ -992,7 +1045,7 @@
         return [pltpu.VMEM(self.shape, BF16), dma((1,)), dma((2, self.nt))] + self.near.scratch()
 
     def bind(self, ins, outs, scratch):
-        self.t = lax.axis_index("tensor")
+        self.t = lax.axis_index(TENSOR)
         self.src = ins[0]
         self.whole, self.load_sem, self.spread_sem = scratch[:3]
         self.near.bind([self.whole], outs, scratch[3:])
@@ -1043,7 +1096,7 @@
     return pltpu.roll(value, value.shape[-1] // 2, value.ndim - 1)
 
 
-def attend_body(t, nt, heads, x_ref, tables, gains, outs, scratch, wait_qkv, wait_out):
+def attend_body(t, nt, heads, x_ref, tables, gains, outs, scratch, wait_qkv, wait_out, at):
     (h1_ref, b_ref, a_ref, q_ref, k_ref, v_ref, qr_ref, kr_ref, o_ref) = outs
     (wq_s, wk_s, wv_s, wo_s, part, outgoing, came, s_sem, r_sem) = scratch
     block, width = x_ref.shape
@@ -1074,7 +1127,7 @@
     o_ref[...] = rows_to_heads(o, heads, block)
     wait_out()
     part[...] = dot(o_ref[...], wo_s[...])
-    total = reduce_rows(t, nt, rows, part, outgoing, came, s_sem, r_sem)
+    total = reduce_rows(t, nt, rows, part, outgoing, came, s_sem, r_sem, at)
     h1 = x_ref[rows_at(t * rows, rows)].astype(F32) + total
     h1_ref[...] = h1
     b_ref[...] = (unit_rows(h1)[0] * g_moe).astype(BF16)
@@ -1111,7 +1164,7 @@
 
 
 def start_attend_kernel(nz, nt, heads, relay, hello, at, ins, outs, scratch):
-    s, z, t = lax.axis_index("section"), lax.axis_index("expert"), lax.axis_index("tensor")
+    s, z, t = lax.axis_index(SECTION), lax.axis_index(EXPERT), lax.axis_index(TENSOR)
     lengths, ids, route_weights, boundary, gains, wq, wk, wv, wo, wg, wu, wd = ins
     edges, tabs_out, gates_out, gains_out = outs[:4]
     gathered, (sg, su, sd), results = outs[4:8], outs[8:11], outs[11:]
@@ -1178,6 +1231,7 @@
         copy.wait()
     for i in range(3):
         sibling(i, pairs[i][0], pairs[i][2]).wait_recv()
+    at(TABLES)
     loads = [
         pltpu.make_async_copy(edges.at[0], x_s, in_sem.at[0]),
         pltpu.make_async_copy(tabs_out.at[0], tabs_s, in_sem.at[1]),
@@ -1209,17 +1263,18 @@
             bring(a).start()
         for a in range(3):
             bring(a).wait()
+        at(QKV)
 
     def wait_out():
         for k in range(1, nz):
             relay.step(3, k)
-        at("shards")
+        at(SHARDS)
         relay.settle(3)
         bring(3).start()
         bring(3).wait()
 
     tables = (tabs_s[0], tabs_s[1], tabs_s[2])
-    attend_body(t, nt, heads, x_s, tables, gains_s[...], results, attn_scratch, wait_qkv, wait_out)
+    attend_body(t, nt, heads, x_s, tables, gains_s[...], results, attn_scratch, wait_qkv, wait_out, at)
     for i in range(6):
         sibling(i, *pairs[i][:2]).wait_send()
     for i in range(3, 6):
@@ -1229,11 +1284,11 @@
         gate_copy(d, k, True).wait_recv()
     for a in range(4):
         relay.end(a)
-    at("end")
+    at(END)
 
 
 def attend_kernel(layer, nz, nt, heads, hello, at, ins, outs, scratch):
-    s, z, t = lax.axis_index("section"), lax.axis_index("expert"), lax.axis_index("tensor")
+    s, z, t = lax.axis_index(SECTION), lax.axis_index(EXPERT), lax.axis_index(TENSOR)
     x_ref, tabs, gains, wq, wk, wv, wo = ins
     w_sem, tabs_s, gains_s, attn_scratch = scratch[0], scratch[1], scratch[2], scratch[3:]
     loads = [
@@ -1247,25 +1302,25 @@
     for load in small:
         load.start()
     hello(all_peers(s, z, t, nz, nt))
-    at("begin")
+    at(BEGIN)
     for load in small:
         load.wait()
 
     def wait_qkv():
-        at("qkv")
+        at(QKV)
         for load in loads[:3]:
             load.start()
         for load in loads[:3]:
             load.wait()
 
     def wait_out():
-        at("out")
+        at(OUT)
         loads[3].start()
         loads[3].wait()
 
     tables = (tabs_s[0], tabs_s[1], tabs_s[2])
-    attend_body(t, nt, heads, x_ref, tables, gains_s[...], outs, attn_scratch, wait_qkv, wait_out)
-    at("end")
+    attend_body(t, nt, heads, x_ref, tables, gains_s[...], outs, attn_scratch, wait_qkv, wait_out, at)
+    at(END)
 
 
 def load_experts(layer, s, own, sibling, scratch, sems):
@@ -1286,7 +1341,7 @@
 
 
 def experts_kernel(layer, nz, nt, local_experts, hello, at, ins, outs, scratch):
-    s, z, t = lax.axis_index("section"), lax.axis_index("expert"), lax.axis_index("tensor")
+    s, z, t = lax.axis_index(SECTION), lax.axis_index(EXPERT), lax.axis_index(TENSOR)
     b_ref, h1_ref, gates, wg, wu, wd, sg, su, sd = ins
     y_ref, b_out, g_out, u_out = outs
     wg_s, wu_s, wd_s, g_s, u_s, gates_s, w_sem, o_sem = scratch[:8]
@@ -1322,17 +1377,17 @@
         save.start()
     whole[rows_at(t * rows, rows)] = (h1_ref[...] + total[...]).astype(BF16)
     wait = spread_rows(t, nt, rows, whole, spread_sem.at[0], spread_sem.at[1])
-    at("spread")
+    at(SPREAD)
     finish()
     wait()
     y_ref[...] = whole[...]
     for save in saves:
         save.wait()
-    at("end")
+    at(END)
 
 
 def experts_back_kernel(layer, nz, nt, local_experts, hello, at, ins, outs, scratch):
-    s, z, t = lax.axis_index("section"), lax.axis_index("expert"), lax.axis_index("tensor")
+    s, z, t = lax.axis_index(SECTION), lax.axis_index(EXPERT), lax.axis_index(TENSOR)
     dy_ref, h1_ref, gains, gates, g_in, u_in, wg, wu, wd, sg, su, sd = ins
     dat_ref, dh1_ref, term_ref, dy_out, hid_out, dg_out, du_out = outs
     wg_s, wu_s, wd_s, g_s, u_s, hid_s, dg_s, du_s, w_sem, g_sem, u_sem, o_sem = scratch[:12]
@@ -1396,19 +1451,23 @@
     dh1 = dy_ref[...].astype(F32) + back
     dh1_ref[...] = dh1
     term_ref[...] = term
-    whole[rows_at(t * rows, rows)] = dh1.astype(BF16)
+    mine = rows_at(t * rows, rows)
+    whole[mine] = dh1.astype(BF16)
+    dat_ref[mine] = dh1.astype(BF16)
     wait = spread_rows(t, nt, rows, whole, spread_sem.at[0], spread_sem.at[1])
-    at("spread")
+    at(SPREAD)
     finish()
     wait()
-    dat_ref[...] = whole[...]
+    for j in range(1, nt):
+        theirs = rows_at(partner(t, jnp.int32(j), nt) * rows, rows)
+        dat_ref[theirs] = whole[theirs]
     for save in saves:
         save.wait()
-    at("end")
+    at(END)
 
 
 def experts_both_kernel(layer, nz, nt, local_experts, hello, at, ins, outs, scratch):
-    s, z, t = lax.axis_index("section"), lax.axis_index("expert"), lax.axis_index("tensor")
+    s, z, t = lax.axis_index(SECTION), lax.axis_index(EXPERT), lax.axis_index(TENSOR)
     b_ref, h1_ref, dy_ref, gains, gates, dy_all, wg, wu, wd, sg, su, sd = ins
     dat_ref, dh1_ref, term_ref, b_out, y_out, hid_out, dg_out, du_out = outs
     wg_s, wu_s, wd_s, dy_s, y_s, hid_s, dg_s, du_s, w_sem, dy_sem, y_sem, o_sem = scratch[:12]
@@ -1477,21 +1536,25 @@
     dh1 = dy_ref[...].astype(F32) + back
     dh1_ref[...] = dh1
     term_ref[...] = term
-    whole[rows_at(t * rows, rows)] = dh1.astype(BF16)
+    mine = rows_at(t * rows, rows)
+    whole[mine] = dh1.astype(BF16)
+    dat_ref[mine] = dh1.astype(BF16)
     wait = spread_rows(t, nt, rows, whole, spread_sem.at[0], spread_sem.at[1])
-    at("spread")
+    at(SPREAD)
     finish()
     wait()
-    dat_ref[...] = whole[...]
+    for j in range(1, nt):
+        theirs = rows_at(partner(t, jnp.int32(j), nt) * rows, rows)
+        dat_ref[theirs] = whole[theirs]
     for save in saves:
         save.wait()
     store(jnp.int32(nz - 2)).wait()
     store(jnp.int32(nz - 1)).wait()
-    at("end")
+    at(END)
 
 
 def attend_back_kernel(layer, source, nz, nt, heads, hello, at, ins, outs, scratch):
-    s, z, t = lax.axis_index("section"), lax.axis_index("expert"), lax.axis_index("tensor")
+    s, z, t = lax.axis_index(SECTION), lax.axis_index(EXPERT), lax.axis_index(TENSOR)
     (x_ref, tabs, gains, dat_ref, dh1_ref, term_moe, q_ref, k_ref, v_ref, qr_ref, kr_ref) = ins[:11]
     wq, wk, wv, wo = ins[11:15]
     dx_ref, dqkv_ref, terms_ref = outs[:3]
@@ -1515,9 +1578,9 @@
         load.start()
     hello(all_peers(s, z, t, nz, nt))
     if layer == 0:
-        late = [at.moves[name] for name in ("dqkv_0", "dx_0", "terms_0")]
+        late = [at.moves[name] for name in (MOVE_DQKV_0, MOVE_DX_0, MOVE_TERMS_0)]
         late[0].src, late[1].src, late[2].src = dqkv_ref, whole, terms_ref
-    at("begin")
+    at(BEGIN)
 
     size = tabs.shape[-1]
     g_attn, _, g_query, g_key = split_gains(gains[layer], model_width, size)
@@ -1549,12 +1612,12 @@
     dqkv_ref[:, (heads + 1) * size :] = dv
     if layer == 0:
         late[0].start()
-    at("dqkv")
+    at(DQKV)
     for load in loads[1:]:
         load.wait()
     part[...] = dot_nt(dq, wq_s[...]) + dot_nt(dk, wk_s[...]) + dot_nt(dv, wv_s[...])
-    total = reduce_rows(t, nt, rows, part, outgoing, came, s_sem, r_sem)
-    at("reduced")
+    total = reduce_rows(t, nt, rows, part, outgoing, came, s_sem, r_sem, at)
+    at(REDUCED)
     x_copy.wait()
     unit, factor = unit_rows(x_s[...].astype(F32))
     back, term_attn = norm_back(total, g_attn, unit, factor)
@@ -1564,7 +1627,7 @@
     write_terms(terms_ref, 8, term_attn)
     terms_ref[16:17, :size] = term_query
     terms_ref[16:17, size : 2 * size] = term_key
-    at("terms")
+    at(TERMS)
     if layer == 1:
         dx_ref[...] = dx
     else:
@@ -1615,15 +1678,16 @@
         for j in range(1, nt):
             near(j).wait_send()
         terms_out[...] = sums
+        at(TAIL)
         late[0].finish()
         late[1].finish()
         late[2].leave()
         dx_ref[...] = dx
-    at("end")
+    at(END)
 
 
 def expert_grads_kernel(nz, step, ins, outs, scratch):
-    s = lax.axis_index("section")
+    s = lax.axis_index(SECTION)
     own, near = (ins[0:5], ins[5:10]), (ins[10:15], ins[15:20])
     left, right, stage, in_sem, out_sem = scratch
 
@@ -1678,7 +1742,7 @@
 
 
 def attend_grads_kernel(q_cols, size, ins, outs, scratch):
-    s = lax.axis_index("section")
+    s = lax.axis_index(SECTION)
     spaces, sems = scratch[:4], scratch[4]
     a_s, o_s, t_s, d_s = spaces
 
@@ -1749,10 +1813,10 @@
 
 
 USUAL = {
-    "second": None,
-    "looped": 1, "out": 1, "dqkv": 1,
-    "collected": 2, "reduced": 2,
-    "spread": 3, "terms": 3,
+    SECOND: None,
+    LOOPED: 1, OUT: 1, DQKV: 1,
+    COLLECTED: 2, REDUCED: 2,
+    SPREAD: 3, TERMS: 3,
 }
 
 
@@ -1766,13 +1830,13 @@
         self.stages.append((name, body, ins, list(zip(slots, [spec for _, spec in outs])), scratch))
         return slots
 
-    def move(self, name, stage, move, ins, outs, plan, start="begin", manual=False):
+    def move(self, name, stage, move, ins, outs, plan, start=BEGIN, manual=False):
         slots = [Slot(shape) for shape in outs]
         self.moves[name] = (stage, move, ins, [(slot, ANY) for slot in slots])
         if not self.fused:
             plan = []
             if not manual:
-                plan = [(stage, start, lambda m: m.start()), (stage, "end", lambda m: m.finish())]
+                plan = [(stage, start, lambda m: m.start()), (stage, END, lambda m: m.finish())]
                 for point, turn in USUAL.items():
                     if turn:
                         plan.append((stage, point, lambda m, turn=turn: m.poll(turn)))
@@ -1786,7 +1850,7 @@
             return
         for i, stage in enumerate(self.stages):
             names = [name for name, entry in self.moves.items() if entry[0] == stage[0]]
-            self.launch(stage[0], self.number + i, [stage], names)
+            self.launch(self.name + str(i), self.number + i, [stage], names)
 
     def launch(self, name, number, stages, names):
         moves = [self.moves[n] for n in names]
@@ -1798,13 +1862,13 @@
             where = []
             for value, spec in pairs:
                 if id(value) in out_at:
-                    where.append(("out", out_at[id(value)]))
+                    where.append((True, out_at[id(value)]))
                     continue
                 key = (id(value), id(spec))
                 if key not in in_at:
                     in_at[key] = len(ins)
                     ins.append((value.value if isinstance(value, Slot) else value, spec))
-                where.append(("in", in_at[key]))
+                where.append((False, in_at[key]))
             return where
 
         def reserve(items):
@@ -1828,7 +1892,7 @@
         def body(in_refs, out_refs, scratch_refs):
             def pick(places):
                 where, results, spaces = places
-                refs = [(out_refs if kind == "out" else in_refs)[i] for kind, i in where]
+                refs = [(out_refs if made else in_refs)[i] for made, i in where]
                 return refs, [out_refs[i] for i in results], [scratch_refs[i] for i in spaces]
 
             bound = {n: m[1].bind(*pick(at)) for n, m, at in zip(names, moves, move_at)}
@@ -1871,11 +1935,11 @@
 
     def attend_spaces(own):
         return [
-            ("wq", pltpu.VMEM((width, q_cols), BF16)),
-            ("wk", pltpu.VMEM((width, size), BF16)),
-            ("wv", pltpu.VMEM((width, size), BF16)),
-            ("wo", pltpu.VMEM((q_cols, width), BF16)),
-            ("part", pltpu.VMEM((block, width), F32)),
+            (SHARED_WQ, pltpu.VMEM((width, q_cols), BF16)),
+            (SHARED_WK, pltpu.VMEM((width, size), BF16)),
+            (SHARED_WV, pltpu.VMEM((width, size), BF16)),
+            (SHARED_WO, pltpu.VMEM((q_cols, width), BF16)),
+            (SHARED_PART, pltpu.VMEM((block, width), F32)),
             pltpu.VMEM((block, width), BF16),
             pltpu.VMEM((nt, rows, width), BF16),
             dma((nt,)),
@@ -1899,9 +1963,9 @@
         shape_of((block, size), BF16),
         shape_of((block, q_cols), BF16),
     )
-    expert_scratch = [("wg", pltpu.VMEM((hidden, width), BF16)), ("wu", pltpu.VMEM((hidden, width), BF16))]
-    expert_scratch += [("wd", pltpu.VMEM((hidden, width), BF16))]
-    hid_scratch = [(n, pltpu.VMEM((nz, block, hidden), BF16)) for n in ("hid", "dg", "du")]
+    expert_scratch = [(SHARED_WG, pltpu.VMEM((hidden, width), BF16)), (SHARED_WU, pltpu.VMEM((hidden, width), BF16))]
+    expert_scratch += [(SHARED_WD, pltpu.VMEM((hidden, width), BF16))]
+    hid_scratch = [(n, pltpu.VMEM((nz, block, hidden), BF16)) for n in (SHARED_HID, SHARED_DG, SHARED_DU)]
     all_tokens = shape_of((nz, block, width), BF16)
     all_hidden = shape_of((nz, block, hidden), BF16)
     cols = width // nz
@@ -1933,7 +1997,7 @@
     fore = Group("forward", 0, fused)
     relay = Relay(0, (0, 0, 0, 1), nz)
     started = fore.stage(
-        "attend_0",
+        ATTEND_0,
         functools.partial(start_attend_kernel, nz, nt, heads, relay),
         [(seq_lengths[0, :, 0], SM)]
         + vm(expert_ids[0], route_weights[0])
@@ -1964,7 +2028,7 @@
     h1_0, b_0, a_0, q_0, k_0, v_0, qr_0, kr_0, o_0 = started[11:]
 
     x_1, ball_0, gp_0, up_0 = fore.stage(
-        "experts_0",
+        EXPERTS_0,
         functools.partial(experts_kernel, 0, nz, nt, local_experts),
         vm(b_0, h1_0) + any_place(gates_all, *expert_weights),
         vm(shape_of((block, width), BF16))
@@ -1980,49 +2044,45 @@
     )
 
     weights_1 = fore.move(
-        "weights_1", "experts_0", Relay(1, (0, 0, 0, 1), nz), any_place(wq, wk, wv, wo), gathered,
+        MOVE_WEIGHTS_1, EXPERTS_0, Relay(1, (0, 0, 0, 1), nz), any_place(wq, wk, wv, wo), gathered,
         [
-            ("attend_0", "shards", begins(0, 1, 2)),
-            ("experts_0", "begin", steps((0, 1, 2), 1)),
-            ("experts_0", "begin", begins(3)),
-            ("experts_0", "second", steps((0, 1, 2), 2)),
-            ("experts_0", "looped", steps((3,), 1)),
-            ("experts_0", "collected", steps((0, 1, 2), 3)),
-            ("experts_0", "spread", steps((3,), 2)),
-            ("attend_1", "qkv", settles(0, 1, 2)),
-            ("attend_1", "out", steps((3,), 3)),
-            ("attend_1", "out", settles(3)),
-            ("attend_1", "end", ends_of),
+            (ATTEND_0, SHARDS, begins(0, 1, 2)),
+            (ATTEND_0, SENT, steps((0, 1, 2), 1)),
+            (ATTEND_0, SENT, begins(3)),
+            (EXPERTS_0, ARRIVED, steps((0, 1, 2), 2)),
+            (EXPERTS_0, ARRIVED, steps((3,), 1)),
+            (EXPERTS_0, LOOPED, steps((0, 1, 2), 3)),
+            (EXPERTS_0, LOOPED, steps((3,), 2)),
+            (ATTEND_1, QKV, settles(0, 1, 2)),
+            (ATTEND_1, OUT, steps((3,), 3)),
+            (ATTEND_1, OUT, settles(3)),
+            (ATTEND_1, END, ends_of),
         ],
     )
 
     (dy_rows,) = fore.move(
-        "dy_rows", "attend_0", RowsFar(1, nz, nt), any_place(edges), [shape_of((nz, rows, width), BF16)],
-        [("experts_0", "looped", start), ("attend_1", "begin", finish)],
-        "shards",
+        MOVE_DY_ROWS, ATTEND_0, RowsFar(1, nz, nt), any_place(edges), [shape_of((nz, rows, width), BF16)],
+        [(ATTEND_0, TABLES, start), (ATTEND_0, QKV, finish)],
+        SHARDS,
     )
     (dyall_1,) = fore.move(
-        "dy_all", "experts_0", Spread(nz, nt), any_place(dy_rows), [all_tokens],
-        [("attend_1", "begin", start), ("attend_1", "out", poll(1)), ("attend_1", "end", finish)],
+        MOVE_DY_ALL, EXPERTS_0, Spread(nz, nt), any_place(dy_rows), [all_tokens],
+        [(ATTEND_0, QKV, start), (ATTEND_0, SHARDS, poll(1)), (EXPERTS_0, END, finish)],
     )
 
     h1_1, b_1, a_1, q_1, k_1, v_1, qr_1, kr_1, o_1 = fore.stage(
-        "attend_1",
+        ATTEND_1,
         functools.partial(attend_kernel, 1, nz, nt, heads),
         vm(x_1) + any_place(tabs_all, gains_all, *weights_1),
         attend_outs,
         [dma((6,)), pltpu.VMEM((3, block, size), F32), pltpu.VMEM(gains.shape, F32)] + attend_spaces(1),
     )
-    aall_0, _ = fore.move(
-        "a_0", "attend_1", Slice(0, nz, nt), any_place(a_0), sliced,
-        [("attend_1", "begin", start), ("attend_1", "out", poll(1)), ("attend_1", "end", finish)],
-    )
     fore.run()
 
     back = Group("backward", 8, fused)
-    dy_1 = lax.dynamic_slice_in_dim(edges.value[1], lax.axis_index("tensor") * rows, rows, 0)
+    dy_1 = lax.dynamic_slice_in_dim(edges.value[1], lax.axis_index(TENSOR) * rows, rows, 0)
     dat_1, dh1_1, tm_1, ball_1, yparts_1, hid_1, dg_1, du_1 = back.stage(
-        "both_1",
+        BOTH_1,
         functools.partial(experts_both_kernel, 1, nz, nt, local_experts),
         vm(b_1, h1_1, dy_1, gains_all) + any_place(gates_all, dyall_1, *expert_weights),
         vm(
@@ -2034,7 +2094,7 @@
         expert_scratch
         + [pltpu.VMEM((2, block, width), BF16)] * 2
         + hid_scratch
-        + [dma((4,)), dma((2,)), dma((2,)), dma((4,)), ("gates", pltpu.VMEM((nz, block, LANES), F32))]
+        + [dma((4,)), dma((2,)), dma((2,)), dma((4,)), (SHARED_GATES, pltpu.VMEM((nz, block, LANES), F32))]
         + exchange_scratch(nz, nt, rows, block, width),
     )
 
@@ -2059,18 +2119,18 @@
             ]
             ins += any_place(others)
         return back.stage(
-            f"attend_back_{layer}",
+            ATTEND_BACK_1 if layer else ATTEND_BACK_0,
             functools.partial(attend_back_kernel, layer, source, nz, nt, heads),
             ins,
             outs,
             scratch,
         )
 
-    last = ("attend_back_0", "end", finish)
+    last = (ATTEND_BACK_0, END, finish)
     kept_1, kept_0 = (q_1, k_1, v_1, qr_1, kr_1), (q_0, k_0, v_0, qr_0, kr_0)
     dx_1, dqkv_1, terms_1 = attend_back(1, x_1, None, dat_1, dh1_1, tm_1, kept_1, weights_1)
     dat_0, dh1_0, tm_0, dyall_0, hid_0, dg_0, du_0 = back.stage(
-        "experts_back_0",
+        EXPERTS_BACK_0,
         functools.partial(experts_back_kernel, 0, nz, nt, local_experts),
         vm(dx_1, h1_0, gains_all) + any_place(gates_all, gp_0, up_0, *expert_weights),
         vm(
@@ -2082,7 +2142,7 @@
         expert_scratch
         + [pltpu.VMEM((2, block, hidden), F32)] * 2
         + hid_scratch
-        + [dma((4,)), dma((2,)), dma((2,)), dma((4,)), ("gates", pltpu.VMEM((nz, block, LANES), F32))]
+        + [dma((4,)), dma((2,)), dma((2,)), dma((4,)), (SHARED_GATES, pltpu.VMEM((nz, block, LANES), F32))]
         + exchange_scratch(nz, nt, rows, block, width),
     )
 
@@ -2092,74 +2152,85 @@
             [begin + (start,), end], begin[1],
         )
 
+    def line(name, stage, layer, value, begin, *points):
+        plan = [begin + (start,)]
+        plan += [point + (steps((0,), k + 1),) for k, point in enumerate(points)]
+        plan += [(ATTEND_BACK_0, END, settles(0)), (ATTEND_BACK_0, END, lambda m: m.end(0))]
+        return back.move(
+            name, stage, Line(layer, nz), any_place(value), [like(value, (2, nz))], plan, begin[1]
+        )
+
     def near(name, stage, layer, value):
         return back.move(
-            name, stage, Near(layer), any_place(value), [like(value)], [(stage, "begin", start), last]
+            name, stage, Near(layer), any_place(value), [like(value)], [(stage, BEGIN, start), last]
         )
 
     def columns(name, stage, layer, value, begin, middle):
         return back.move(
             name, stage, Slice(layer, nz, nt), any_place(value), sliced,
-            [begin + (start,), middle + (poll(1),), last], begin[1] if begin[0] == stage else "begin",
-        )
-
-    (bnear_0,) = near("b_0", "both_1", 0, ball_0)
-    (oall_0,) = gather("o_0", "both_1", 0, o_0, ("both_1", "arrived"))
+            [begin + (start,), middle + (poll(1),), last], begin[1] if begin[0] == stage else BEGIN,
+        )
+
+    (bnear_0,) = near(MOVE_B_0, BOTH_1, 0, ball_0)
+    (oall_0,) = gather(MOVE_O_0, BOTH_1, 0, o_0, (BOTH_1, ARRIVED))
+    aall_0, _ = columns(
+        MOVE_A_0, BOTH_1, 0, a_0, (ATTEND_BACK_1, BEGIN), (EXPERTS_BACK_0, BEGIN)
+    )
     aall_1, _ = columns(
-        "a_1", "both_1", 1, a_1, ("both_1", "looped"), ("attend_back_1", "dqkv")
-    )
-    (oall_1,) = gather("o_1", "attend_back_1", 1, o_1, ("attend_back_1", "begin"))
+        MOVE_A_1, BOTH_1, 1, a_1, (ATTEND_BACK_1, BEGIN), (EXPERTS_BACK_0, BEGIN)
+    )
+    (oall_1,) = gather(MOVE_O_1, ATTEND_BACK_1, 1, o_1, (ATTEND_BACK_1, BEGIN))
     near_1 = [
-        near(f"near_1_{i}", "attend_back_1", 1, value)[0]
+        near(NEAR_1 + i, ATTEND_BACK_1, 1, value)[0]
         for i, value in enumerate((dg_1, du_1, hid_1, ball_1, dyall_1))
     ]
     datall_1, _ = columns(
-        "dat_1", "attend_back_1", 1, dat_1, ("attend_back_1", "begin"), ("attend_back_1", "reduced")
+        MOVE_DAT_1, ATTEND_BACK_1, 1, dat_1, (BOTH_1, SPREAD), (ATTEND_BACK_1, DQKV)
     )
     (ysums_1,) = back.move(
-        "y_near", "attend_back_1", SumNear(nz, nt, rows, block, width), any_place(yparts_1),
+        MOVE_Y_NEAR, ATTEND_BACK_1, SumNear(nz, nt, rows, block, width), any_place(yparts_1),
         [shape_of((nz, rows, width), BF16)],
         [
-            ("attend_back_1", "begin", start),
-            ("attend_back_1", "dqkv", poll(1)),
-            ("attend_back_1", "end", poll(2)),
-            ("attend_back_1", "end", finish),
+            (ATTEND_BACK_1, BEGIN, start),
+            (EXPERTS_BACK_0, BEGIN, poll(1)),
+            (EXPERTS_BACK_0, LOOPED, poll(2)),
+            (EXPERTS_BACK_0, COLLECTED, finish),
         ],
     )
-    (dqkvall_1,) = gather("dqkv_1", "experts_back_0", 1, dqkv_1, ("experts_back_0", "arrived"))
+    (dqkvall_1,) = gather(MOVE_DQKV_1, EXPERTS_BACK_0, 1, dqkv_1, (EXPERTS_BACK_0, ARRIVED))
     (termsall_1,) = gather(
-        "terms_1", "experts_back_0", 1, terms_1, ("experts_back_0", "begin"),
-        ("attend_back_0", "begin", finish),
+        MOVE_TERMS_1, EXPERTS_BACK_0, 1, terms_1, (EXPERTS_BACK_0, BEGIN),
+        (ATTEND_BACK_0, BEGIN, finish),
     )
     (yrows_1,) = back.move(
-        "y_far", "experts_back_0", SumFar(nz, rows, width), any_place(ysums_1) + vm(h1_1),
+        MOVE_Y_FAR, EXPERTS_BACK_0, SumFar(nz, rows, width), any_place(ysums_1) + vm(h1_1),
         [shape_of((rows, width), BF16)],
         [
-            ("experts_back_0", "arrived", start),
-            ("experts_back_0", "spread", poll(2)),
-            ("experts_back_0", "end", finish),
+            (EXPERTS_BACK_0, SPREAD, start),
+            (ATTEND_BACK_0, SENT, poll(2)),
+            (ATTEND_BACK_0, SENT, finish),
         ],
     )
     _, dqkv_0, terms_0, terms = attend_back(
         0, edges, 0, dat_0, dh1_0, tm_0, kept_0, weights_0, termsall_1
     )
     datall_0, _ = columns(
-        "dat_0", "attend_back_0", 0, dat_0, ("attend_back_0", "begin"), ("attend_back_0", "reduced")
+        MOVE_DAT_0, ATTEND_BACK_0, 0, dat_0, (EXPERTS_BACK_0, SPREAD), (ATTEND_BACK_0, DQKV)
     )
     near_0 = [bnear_0] + [
-        near(f"near_0_{i}", "attend_back_0", 0, value)[0]
+        near(NEAR_0 + i, ATTEND_BACK_0, 0, value)[0]
         for i, value in enumerate((dyall_0, dg_0, du_0, hid_0))
     ]
     (ends_1,) = back.move(
-        "y_spread", "attend_back_0", SpreadNear(1, nt, block, width), any_place(yrows_1),
+        MOVE_Y_SPREAD, ATTEND_BACK_0, SpreadNear(1, nt, block, width), any_place(yrows_1),
         [shape_of((2, block, width), BF16)],
-        [("attend_back_0", "begin", start), ("attend_back_0", "dqkv", poll(1)), last],
-    )
-    hand = [("dqkv_0", Gather(0, nz), like(dqkv_0, (2, nz)))]
-    hand += [("dx_0", Near(0, True), shape_of((2, block, width), BF16))]
-    hand += [("terms_0", Gather(0, nz), like(terms_0, (2, nz)))]
+        [(ATTEND_BACK_0, TERMS, start), (ATTEND_BACK_0, TAIL, poll(1)), last],
+    )
+    hand = [(MOVE_DQKV_0, Gather(0, nz), like(dqkv_0, (2, nz)))]
+    hand += [(MOVE_DX_0, Near(0, True), shape_of((2, block, width), BF16))]
+    hand += [(MOVE_TERMS_0, Gather(0, nz), like(terms_0, (2, nz)))]
     dqkvall_0, ends_0, _ = (
-        back.move(name, "attend_back_0", move, [], [shape], [], manual=True)[0]
+        back.move(name, ATTEND_BACK_0, move, [], [shape], [], manual=True)[0]
         for name, move, shape in hand
     )
     back.run()
@@ -2206,7 +2277,7 @@
         ),
         [pltpu.VMEM(o.shape, o.dtype) for o in operands[:4]] + [dma((4,))],
     )
-    ends = jnp.where(lax.axis_index("section") == 0, ends_0.value, ends_1.value)
+    ends = jnp.where(lax.axis_index(SECTION) == 0, ends_0.value, ends_1.value)
     return (
         ends[None],
         terms[8:16].reshape(1, width),
@@ -2228,35 +2299,35 @@
         on_device,
         mesh=mesh,
         in_specs=(
-            P("section", None, "expert", None),
-            P("section", None, "expert", None),
-            P("section", None, "expert", None),
-            P("section", None, "expert", None),
-            P("section", None),
-            P("section", None),
-            P("section", None),
-            P("section", None),
-            P("section", "expert", "tensor"),
-            P("section", "expert", "tensor"),
-            P("section", "expert", "tensor"),
-            P("section", "tensor", "expert"),
-            P("section", "expert", "tensor", None),
-            P("section", "expert", "tensor", None),
-            P("section", "expert", "tensor", None),
+            P(SECTION, None, EXPERT, None),
+            P(SECTION, None, EXPERT, None),
+            P(SECTION, None, EXPERT, None),
+            P(SECTION, None, EXPERT, None),
+            P(SECTION, None),
+            P(SECTION, None),
+            P(SECTION, None),
+            P(SECTION, None),
+            P(SECTION, EXPERT, TENSOR),
+            P(SECTION, EXPERT, TENSOR),
+            P(SECTION, EXPERT, TENSOR),
+            P(SECTION, TENSOR, EXPERT),
+            P(SECTION, EXPERT, TENSOR, None),
+            P(SECTION, EXPERT, TENSOR, None),
+            P(SECTION, EXPERT, TENSOR, None),
         ),
         out_specs=(
-            P("section", None, "expert", None),
-            P("section", None),
-            P("section", None),
-            P("section", None),
-            P("section", None),
-            P("section", "expert", "tensor"),
-            P("section", "expert", "tensor"),
-            P("section", "expert", "tensor"),
-            P("section", "tensor", "expert"),
-            P("section", "expert", "tensor", None),
-            P("section", "expert", "tensor", None),
-            P("section", "expert", "tensor", None),
+            P(SECTION, None, EXPERT, None),
+            P(SECTION, None),
+            P(SECTION, None),
+            P(SECTION, None),
+            P(SECTION, None),
+            P(SECTION, EXPERT, TENSOR),
+            P(SECTION, EXPERT, TENSOR),
+            P(SECTION, EXPERT, TENSOR),
+            P(SECTION, TENSOR, EXPERT),
+            P(SECTION, EXPERT, TENSOR, None),
+            P(SECTION, EXPERT, TENSOR, None),
+            P(SECTION, EXPERT, TENSOR, None),
         ),
         check_vma=False,
     )

time: 507 us -> 480 us (0.947)
  Pallas kernels: 488 us -> 460 us
    pallas_call x4, Pallas kernels: 488 us -> 460 us  [call(): pl.pallas_call(kernel, out_shape=tuple((shape_of(o.shape, o.dtype) for o,...]
where the time goes in v5:
time: 480 us; the launch traced here: 471 us
  Pallas kernels  460 us (96%)
  local copies, waits for them, and re-layouts  6.46 us (1%)
    pallas_call x4, Pallas kernels, call(): pl.pallas_call(kernel, out_shape=tuple((shape_of(o.shape, o.dtype) for o,...  460 us

profile of v5, /device:TPU:0, one launch (start us, length us, event | category | flops | bytes accessed | tf_op | source)
XLA Modules:
  0.0 471.2 jit_solution(10808836242729095280)
XLA Ops:
  0.7 1.4 pad_maximum_fusion.refs_4_
  2.0 1.5 copy.27
  3.5 1.5 copy.28
  5.0 224.1 %forward.1 = (bf16[2,128,2048]{2,1,0:T(8,128)(2,1)}, f32[2,3,128,128]{3,2,1,0:T(8,128)}, f32[2,4,128,128]{3,2,1,0:T(8,128)}, f32[2,1,4352]{2,1,0:T(1,128)}, bf16...) custom-call(s32[2,4]{1,0:T(2,128)} %bitcast.45, ...), custom_call_target="tpu_custom_call" | custom-call | tf_op jit(solution)/shard_map/forward/pallas_call | solution.py:1788
  229.1 1.1 slice.15
  230.2 0.7 dynamic-slice_bitcast_fusion.refs_2_
  230.8 212.1 %backward.1 = (bf16[128,2048]{1,0:T(8,128)(2,1)}, f32[32,2048]{1,0:T(8,128)}, f32[1,2048]{1,0:T(1,128)}, bf16[4,128,2048]{2,1,0:T(8,128)(2,1)}, bf16[4,128,2048]...) custom-call(bf16[32,2048]{1,0:T(8,128)(2,1)} %get-tuple-element.85.r, ...), custom_call_target="tpu_custom_call" | custom-call | tf_op jit(solution)/shard_map/backward/pallas_call | solution.py:1788
  443.0 0.0 copy-start
  443.0 2.3 select_bitcast_fusion
  445.3 0.0 copy-done
  445.3 0.5 fusion
  445.8 0.6 copy.30
  446.4 0.6 copy.29
  447.0 7.7 %attend_grads.1 = (f32[512,1024]{1,0:T(8,128)}, f32[512,128]{1,0:T(8,128)}, f32[512,128]{1,0:T(8,128)}, f32[1024,512]{1,0:T(8,128)}) custom-call(bf16[2,4,128,512]{3,2,1,0:T(8,128)(2,1)} %get-tuple-element.125.refs_0_, bf16[2,4,128,1024]{3,2,1,0:T(8,128)(2,1)} %get-tuple-element.126.refs_1_, bf16[2,4,128,512]{3,2,1,0:T(8,128)(2,1)} %get-tuple-element.127.refs_2_, ...), custom_call_target="tpu_custom_call" | custom-call | tf_op jit(solution)/shard_map/attend_grads/pallas_call | solution.py:1788
  454.8 16.0 %expert_grads.1 = (f32[768,2048]{1,0:T(8,128)}, f32[768,2048]{1,0:T(8,128)}, f32[768,2048]{1,0:T(8,128)}) custom-call(bf16[4,128,768]{2,1,0:T(8,128)(2,1)} %get-tuple-element.137.refs_0_, bf16[4,128,768]{2,1,0:T(8,128)(2,1)} %get-tuple-element.138.refs_1_, bf16[4,128,768]{2,1,0:T(8,128)(2,1)} %get-tuple-element.139.refs_2_, ...), custom_call_target="tpu_custom_call" | custom-call | tf_op jit(solution)/shard_map/expert_grads/pallas_call | solution.py:1788
  (1 shorter events, 0.0 us)
Async XLA Ops:
  443.0 2.3 copy-start

commit v6 on v5

--- a/solution.py
+++ b/solution.py
@@ -1165,13 +1165,17 @@
 
 def start_attend_kernel(nz, nt, heads, relay, hello, at, ins, outs, scratch):
     s, z, t = lax.axis_index(SECTION), lax.axis_index(EXPERT), lax.axis_index(TENSOR)
-    lengths, ids, route_weights, boundary, gains, wq, wk, wv, wo, wg, wu, wd = ins
+    lengths, ids, route_weights, g_attn, g_moe, g_query, g_key, boundary, wq, wk, wv, wo, wg, wu, wd = ins
     edges, tabs_out, gates_out, gains_out = outs[:4]
     gathered, (sg, su, sd), results = outs[4:8], outs[8:11], outs[11:]
-    x_s, tabs_s, gains_s, tabs, gates = scratch[:5]
-    w_sem, in_sem, own_sem, sib_send, sib_recv, gate_send, gate_recv = scratch[5:12]
-    relay.bind((wq, wk, wv, wo), gathered, scratch[12:19])
-    attn_scratch = scratch[19:]
+    x_s, tabs_s, gains_s, gains, tabs, gates = scratch[:6]
+    w_sem, in_sem, own_sem, sib_send, sib_recv, gate_send, gate_recv = scratch[6:13]
+    relay.bind((wq, wk, wv, wo), gathered, scratch[13:20])
+    attn_scratch = scratch[20:]
+    column = 0
+    for gain in (g_attn, g_moe, g_query, g_key):
+        gains[:, column : column + gain.shape[1]] = gain[...]
+        column += gain.shape[1]
     other = 1 - s
     i32 = jnp.int32
 
@@ -1468,15 +1472,18 @@
 
 def experts_both_kernel(layer, nz, nt, local_experts, hello, at, ins, outs, scratch):
     s, z, t = lax.axis_index(SECTION), lax.axis_index(EXPERT), lax.axis_index(TENSOR)
-    b_ref, h1_ref, dy_ref, gains, gates, dy_all, wg, wu, wd, sg, su, sd = ins
+    b_ref, h1_ref, gains, edges, gates, dy_all, wg, wu, wd, sg, su, sd = ins
     dat_ref, dh1_ref, term_ref, b_out, y_out, hid_out, dg_out, du_out = outs
     wg_s, wu_s, wd_s, dy_s, y_s, hid_s, dg_s, du_s, w_sem, dy_sem, y_sem, o_sem = scratch[:12]
-    gates_s, scratch = scratch[12], scratch[:12] + scratch[13:]
+    gates_s, dy_ref, scratch = scratch[12], scratch[13], scratch[:12] + scratch[14:]
     spaces = scratch[12:]
     rows, model_width = b_ref.shape
     loads = load_experts(layer, s, (wg, wu, wd), (sg, su, sd), (wg_s, wu_s, wd_s), w_sem)
     loads.append(pltpu.make_async_copy(gates.at[layer], gates_s, w_sem.at[3]))
     loads[3].start()
+    own_rows = edges.at[layer, rows_at(t * rows, rows)]
+    loads.append(pltpu.make_async_copy(own_rows, dy_ref, w_sem.at[4]))
+    loads[4].start()
 
     def cotangent(turn):
         origin, slot = partner(z, lax.rem(turn + 1, nz), nz), lax.rem(turn, 2)
@@ -1686,91 +1693,113 @@
     at(END)
 
 
-def expert_grads_kernel(nz, step, ins, outs, scratch):
-    s = lax.axis_index(SECTION)
-    own, near = (ins[0:5], ins[5:10]), (ins[10:15], ins[15:20])
-    left, right, stage, in_sem, out_sem = scratch
-
-    def loads(layer):
-        out = []
-        for i in range(5):
-            target = left.at[i] if i < 3 else right.at[i - 3]
-            out.append(
-                (
-                    pltpu.make_async_copy(own[layer][i], target.at[pl.ds(0, nz)], in_sem.at[i, 0]),
-                    pltpu.make_async_copy(near[layer][i], target.at[pl.ds(nz, nz)], in_sem.at[i, 1]),
-                )
-            )
-        return out
-
-    order = (3, 0, 1, 4, 2)
-    for layer in range(2):
-
-        @pl.when(s == layer)
-        def _():
-            copies = loads(layer)
-            for i in order:
-                for copy in copies[i]:
-                    copy.start()
-
-    waits = loads(0)
-    width = right.shape[-1]
-    tokens = 2 * nz * right.shape[2]
-    cols = left.shape[-1]
-    done = set()
-
-    def need(i):
-        if i not in done:
-            for copy in waits[i]:
-                copy.wait()
-            done.add(i)
-
-    turn = 0
-    for i, r in ((0, 0), (1, 0), (2, 1)):
-        need(3 + r)
-        need(i)
-        for c in range(0, cols, step):
-            slot = turn % 2
-            if turn >= 2:
-                pltpu.make_async_copy(stage.at[slot], outs[0].at[pl.ds(0, step)], out_sem.at[slot]).wait()
-            lhs = left[i, :, :, c : c + step].reshape(tokens, step)
-            stage[slot] = dot_tn(lhs, right[r].reshape(tokens, width))
-            pltpu.make_async_copy(stage.at[slot], outs[i].at[pl.ds(c, step)], out_sem.at[slot]).start()
-            turn += 1
-    for slot in range(2):
-        pltpu.make_async_copy(stage.at[slot], outs[0].at[pl.ds(0, step)], out_sem.at[slot]).wait()
-
-
-def attend_grads_kernel(q_cols, size, ins, outs, scratch):
-    s = lax.axis_index(SECTION)
-    spaces, sems = scratch[:4], scratch[4]
-    a_s, o_s, t_s, d_s = spaces
-
-    def loads(layer):
-        refs = ins[4 * layer : 4 * layer + 4]
-        return [pltpu.make_async_copy(r, d, sems.at[i]) for i, (r, d) in enumerate(zip(refs, spaces))]
-
-    for layer in range(2):
-
-        @pl.when(s == layer)
-        def _():
-            for load in loads(layer):
-                load.start()
-
-    waits = loads(0)
-
-    def flat(ref):
-        return ref[...].reshape(-1, ref.shape[-1])
-
-    waits[0].wait()
-    waits[3].wait()
-    grad = dot_tn(flat(a_s), flat(d_s))
-    outs[0][...] = grad[:, :q_cols]
-    outs[1][...] = grad[:, q_cols : q_cols + size]
-    outs[2][...] = grad[:, q_cols + size :]
-    waits[1].wait()
-    waits[2].wait()
-    outs[3][...] = dot_tn(flat(o_s), flat(t_s))
+class ExpertGrads:
+    def __init__(self, nz, step):
+        self.nz, self.step = nz, step
+
+    def begin(self, ins, outs, scratch):
+        s = lax.axis_index(SECTION)
+        own, near = (ins[0:5], ins[5:10]), (ins[10:15], ins[15:20])
+        left, right, _, in_sem, _ = scratch
+
+        def loads(layer):
+            out = []
+            for i in range(5):
+                target = left.at[i] if i < 3 else right.at[i - 3]
+                for j, src in enumerate((own[layer][i], near[layer][i])):
+                    half = target.at[pl.ds(j * self.nz, self.nz)]
+                    out.append(pltpu.make_async_copy(src, half, in_sem.at[i, j]))
+            return out
+
+        for layer in range(2):
+
+            @pl.when(s == layer)
+            def _():
+                copies = loads(layer)
+                for i in (3, 0, 1, 4, 2):
+                    copies[2 * i].start()
+                    copies[2 * i + 1].start()
+
+        self.waits, self.outs, self.scratch = loads(0), outs, scratch
+
+    def work(self):
+        left, right, stage, _, out_sem = self.scratch
+        step, outs = self.step, self.outs
+        width, cols = right.shape[-1], left.shape[-1]
+        tokens = 2 * self.nz * right.shape[2]
+
+        def need(i):
+            self.waits[2 * i].wait()
+            self.waits[2 * i + 1].wait()
+
+        def stored(slot):
+            return pltpu.make_async_copy(stage.at[slot], outs[0].at[pl.ds(0, step)], out_sem.at[slot])
+
+        turn = 0
+        for i, r in ((0, 0), (1, 0), (2, 1)):
+            if i != 1:
+                need(3 + r)
+            need(i)
+            for c in range(0, cols, step):
+                slot = turn % 2
+                if turn >= 2:
+                    stored(slot).wait()
+                lhs = left[i, :, :, c : c + step].reshape(tokens, step)
+                stage[slot] = dot_tn(lhs, right[r].reshape(tokens, width))
+                pltpu.make_async_copy(
+                    stage.at[slot], outs[i].at[pl.ds(c, step)], out_sem.at[slot]
+                ).start()
+                turn += 1
+        for slot in range(2):
+            stored(slot).wait()
+
+
+class AttendGrads:
+    def __init__(self, width, q_cols, size):
+        self.width, self.q_cols, self.size = width, q_cols, size
+
+    def begin(self, ins, outs, scratch):
+        s = lax.axis_index(SECTION)
+        self.spaces, sems = scratch[:4], scratch[4]
+        self.terms, self.outs = ins[10], outs
+
+        def loads(layer):
+            refs = ins[5 * layer : 5 * layer + 5]
+            targets = list(self.spaces) + [outs[0]]
+            return [
+                pltpu.make_async_copy(r, d, sems.at[i]) for i, (r, d) in enumerate(zip(refs, targets))
+            ]
+
+        for layer in range(2):
+
+            @pl.when(s == layer)
+            def _():
+                for load in loads(layer):
+                    load.start()
+
+        self.waits = loads(0)
+
+    def work(self):
+        (_, attn, moe, query, key, g_query, g_key, g_value, g_output) = self.outs
+        terms, size, q_cols = self.terms, self.size, self.q_cols
+        for i in range(self.width // TERM_COLS):
+            cols = slice(i * TERM_COLS, (i + 1) * TERM_COLS)
+            moe[:, cols] = terms[i : i + 1, :]
+            attn[:, cols] = terms[8 + i : 9 + i, :]
+        query[...] = terms[16:17, :size]
+        key[...] = terms[16:17, size : 2 * size]
+        for wait in self.waits:
+            wait.wait()
+
+        def flat(ref):
+            return ref[...].reshape(-1, ref.shape[-1])
+
+        a_s, o_s, t_s, d_s = self.spaces
+        grad = dot_tn(flat(a_s), flat(d_s))
+        g_query[...] = grad[:, :q_cols]
+        g_key[...] = grad[:, q_cols : q_cols + size]
+        g_value[...] = grad[:, q_cols + size :]
+        g_output[...] = dot_tn(flat(o_s), flat(t_s))
 
 
 def shape_of(shape, dtype):
@@ -1931,7 +1960,7 @@
 
     wg, wu, wd = (w[0].reshape(hidden, width) for w in (w_gate, w_up, w_down))
     wq, wk, wv, wo = w_query[0], key_weight[0], value_weight[0], w_output[0]
-    gains = jnp.concatenate([attn_gain, moe_gain, query_gain, key_norm_gain], axis=1)
+    gains = shape_of((1, 2 * width + 2 * size), F32)
 
     def attend_spaces(own):
         return [
@@ -2000,8 +2029,8 @@
         ATTEND_0,
         functools.partial(start_attend_kernel, nz, nt, heads, relay),
         [(seq_lengths[0, :, 0], SM)]
-        + vm(expert_ids[0], route_weights[0])
-        + any_place(boundary[0], gains, wq, wk, wv, wo, wg, wu, wd),
+        + vm(expert_ids[0], route_weights[0], attn_gain, moe_gain, query_gain, key_norm_gain)
+        + any_place(boundary[0], wq, wk, wv, wo, wg, wu, wd),
         any_place(
             shape_of((2, block, width), BF16),
             shape_of((2, 3, block, size), F32),
@@ -2014,6 +2043,7 @@
         [
             pltpu.VMEM((block, width), BF16),
             pltpu.VMEM((3, block, size), F32),
+            pltpu.VMEM(gains.shape, F32),
             pltpu.VMEM(gains.shape, F32),
             pltpu.VMEM((2, 3, block, size), F32),
             pltpu.VMEM((2, block, LANES), F32),
@@ -2080,11 +2110,10 @@
     fore.run()
 
     back = Group("backward", 8, fused)
-    dy_1 = lax.dynamic_slice_in_dim(edges.value[1], lax.axis_index(TENSOR) * rows, rows, 0)
     dat_1, dh1_1, tm_1, ball_1, yparts_1, hid_1, dg_1, du_1 = back.stage(
         BOTH_1,
         functools.partial(experts_both_kernel, 1, nz, nt, local_experts),
-        vm(b_1, h1_1, dy_1, gains_all) + any_place(gates_all, dyall_1, *expert_weights),
+        vm(b_1, h1_1, gains_all) + any_place(edges, gates_all, dyall_1, *expert_weights),
         vm(
             shape_of((block, width), BF16),
             shape_of((rows, width), F32),
@@ -2094,7 +2123,8 @@
         expert_scratch
         + [pltpu.VMEM((2, block, width), BF16)] * 2
         + hid_scratch
-        + [dma((4,)), dma((2,)), dma((2,)), dma((4,)), (SHARED_GATES, pltpu.VMEM((nz, block, LANES), F32))]
+        + [dma((5,)), dma((2,)), dma((2,)), dma((4,)), (SHARED_GATES, pltpu.VMEM((nz, block, LANES), F32))]
+        + [pltpu.VMEM((rows, width), BF16)]
         + exchange_scratch(nz, nt, rows, block, width),
     )
 
@@ -2235,12 +2265,9 @@
     )
     back.run()
 
-    step = 256
     flat = shape_of((hidden, width), F32)
-    grad_gate, grad_up, grad_down = call(
-        functools.partial(expert_grads_kernel, nz, step),
-        "expert_grads",
-        None,
+    experts_part = (
+        ExpertGrads(nz, 256),
         any_place(
             *(
                 slot.value
@@ -2256,38 +2283,51 @@
         [
             pltpu.VMEM((3, 2 * nz, block, hidden), BF16),
             pltpu.VMEM((2, 2 * nz, block, width), BF16),
-            pltpu.VMEM((2, step, width), F32),
+            pltpu.VMEM((2, 256, width), F32),
             dma((5, 2)),
             dma((2,)),
         ],
     )
-    operands = (aall_0, oall_0, datall_0, dqkvall_0, aall_1, oall_1, datall_1, dqkvall_1)
-    operands = tuple(slot.value for slot in operands)
-    terms = terms.value
-    grad_query, grad_key, grad_value, grad_output = call(
-        functools.partial(attend_grads_kernel, q_cols, size),
-        "attend_grads",
-        None,
-        any_place(*operands),
+    operands = (aall_0, oall_0, datall_0, dqkvall_0, ends_0, aall_1, oall_1, datall_1, dqkvall_1, ends_1)
+    attend_part = (
+        AttendGrads(width, q_cols, size),
+        any_place(*(slot.value for slot in operands)) + vm(terms.value),
         vm(
+            operands[4],
+            shape_of((1, width), F32),
+            shape_of((1, width), F32),
+            shape_of((1, size), F32),
+            shape_of((1, size), F32),
             shape_of(wq.shape, F32),
             shape_of(wk.shape, F32),
             shape_of(wv.shape, F32),
             shape_of(wo.shape, F32),
         ),
-        [pltpu.VMEM(o.shape, o.dtype) for o in operands[:4]] + [dma((4,))],
-    )
-    ends = jnp.where(lax.axis_index(SECTION) == 0, ends_0.value, ends_1.value)
+        [pltpu.VMEM(o.shape, o.dtype) for o in operands[:4]] + [dma((5,))],
+    )
+
+    def gradients(name, parts):
+        def body(ins, outs, scratch):
+            for work, part_ins, part_outs, part_scratch in parts:
+                work.begin(ins[: len(part_ins)], outs[: len(part_outs)], scratch[: len(part_scratch)])
+                ins, outs = ins[len(part_ins) :], outs[len(part_outs) :]
+                scratch = scratch[len(part_scratch) :]
+            for part in parts:
+                part[0].work()
+
+        joined = [sum((list(part[i]) for part in parts), []) for i in (1, 2, 3)]
+        return call(body, name, None, *joined)
+
+    if fused:
+        results = gradients("grads", [experts_part, attend_part])
+    else:
+        results = gradients("expert_grads", [experts_part])
+        results = list(results) + list(gradients("attend_grads", [attend_part]))
+    grad_gate, grad_up, grad_down, ends = results[:4]
     return (
         ends[None],
-        terms[8:16].reshape(1, width),
-        terms[:8].reshape(1, width),
-        terms[16:17, :size],
-        terms[16:17, size : 2 * size],
-        grad_query[None],
-        grad_key[None],
-        grad_value[None],
-        grad_output[None],
+        *results[4:8],
+        *(grad[None] for grad in results[8:]),
         grad_gate.reshape(w_gate.shape),
         grad_up.reshape(w_gate.shape),
         grad_down.reshape(w_gate.shape),

time: 480 us -> 470 us (0.979)
    pallas_call x4 -> x3, Pallas kernels: 460 us -> 457 us  [call(): pl.pallas_call(kernel, out_shape=tuple((shape_of(o.shape, o.dtype) for o,...]
where the time goes in v6:
time: 470 us; the launch traced here: 461 us
  Pallas kernels  457 us (97%)
    pallas_call x3, Pallas kernels, call(): pl.pallas_call(kernel, out_shape=tuple((shape_of(o.shape, o.dtype) for o,...  457 us

profile of v6, /device:TPU:0, one launch (start us, length us, event | category | flops | bytes accessed | tf_op | source)
XLA Modules:
  0.0 460.7 jit_solution(17826400458813182755)
XLA Ops:
  0.6 1.5 copy.27
  2.1 1.5 copy.28
  3.6 223.6 %forward.1 = (bf16[2,128,2048]{2,1,0:T(8,128)(2,1)}, f32[2,3,128,128]{3,2,1,0:T(8,128)}, f32[2,4,128,128]{3,2,1,0:T(8,128)}, f32[2,1,4352]{2,1,0:T(1,128)}, bf16...) custom-call(s32[2,4]{1,0:T(2,128)} %bitcast.32, ...), custom_call_target="tpu_custom_call" | custom-call | tf_op jit(solution)/shard_map/forward/pallas_call | solution.py:1817
  227.2 212.2 %backward.1 = (bf16[128,2048]{1,0:T(8,128)(2,1)}, f32[32,2048]{1,0:T(8,128)}, f32[1,2048]{1,0:T(1,128)}, bf16[4,128,2048]{2,1,0:T(8,128)(2,1)}, bf16[4,128,2048]...) custom-call(bf16[32,2048]{1,0:T(8,128)(2,1)} %get-tuple-element.90.r, ...), custom_call_target="tpu_custom_call" | custom-call | tf_op jit(solution)/shard_map/backward/pallas_call | solution.py:1817
  439.4 20.8 %grads.1 = (f32[768,2048]{1,0:T(8,128)}, f32[768,2048]{1,0:T(8,128)}, f32[768,2048]{1,0:T(8,128)}, bf16[2,128,2048]{2,1,0:T(8,128)(2,1)}, f32[1,2048]{1,0:T(1,12...) custom-call(bf16[4,128,768]{2,1,0:T(8,128)(2,1)} %get-tuple-element., ...), custom_call_target="tpu_custom_call" | custom-call | tf_op jit(solution)/shard_map/grads/pallas_call | solution.py:1817

commit v7 on v6

--- a/solution.py
+++ b/solution.py
@@ -2179,7 +2179,7 @@
     def gather(name, stage, layer, value, begin, end=last):
         return back.move(
             name, stage, Gather(layer, nz), any_place(value), [like(value, (2, nz))],
-            [begin + (start,), end], begin[1],
+            [begin + (start,), end], begin[1] if begin[0] == stage else BEGIN,
         )
 
     def line(name, stage, layer, value, begin, *points):
@@ -2204,12 +2204,12 @@
     (bnear_0,) = near(MOVE_B_0, BOTH_1, 0, ball_0)
     (oall_0,) = gather(MOVE_O_0, BOTH_1, 0, o_0, (BOTH_1, ARRIVED))
     aall_0, _ = columns(
-        MOVE_A_0, BOTH_1, 0, a_0, (ATTEND_BACK_1, BEGIN), (EXPERTS_BACK_0, BEGIN)
+        MOVE_A_0, BOTH_1, 0, a_0, (BOTH_1, ARRIVED), (BOTH_1, SPREAD)
     )
     aall_1, _ = columns(
-        MOVE_A_1, BOTH_1, 1, a_1, (ATTEND_BACK_1, BEGIN), (EXPERTS_BACK_0, BEGIN)
-    )
-    (oall_1,) = gather(MOVE_O_1, ATTEND_BACK_1, 1, o_1, (ATTEND_BACK_1, BEGIN))
+        MOVE_A_1, BOTH_1, 1, a_1, (BOTH_1, ARRIVED), (BOTH_1, SPREAD)
+    )
+    (oall_1,) = gather(MOVE_O_1, ATTEND_BACK_1, 1, o_1, (EXPERTS_BACK_0, BEGIN))
     near_1 = [
         near(NEAR_1 + i, ATTEND_BACK_1, 1, value)[0]
         for i, value in enumerate((dg_1, du_1, hid_1, ball_1, dyall_1))
@@ -2227,7 +2227,7 @@
             (EXPERTS_BACK_0, COLLECTED, finish),
         ],
     )
-    (dqkvall_1,) = gather(MOVE_DQKV_1, EXPERTS_BACK_0, 1, dqkv_1, (EXPERTS_BACK_0, ARRIVED))
+    (dqkvall_1,) = gather(MOVE_DQKV_1, EXPERTS_BACK_0, 1, dqkv_1, (ATTEND_BACK_1, DQKV))
     (termsall_1,) = gather(
         MOVE_TERMS_1, EXPERTS_BACK_0, 1, terms_1, (EXPERTS_BACK_0, BEGIN),
         (ATTEND_BACK_0, BEGIN, finish),

time: 470 us -> 465 us (0.989)
  Pallas kernels: 457 us -> 452 us
    pallas_call x3, Pallas kernels: 457 us -> 452 us  [call(): pl.pallas_call(kernel, out_shape=tuple((shape_of(o.shape, o.dtype) for o,...]
where the time goes in v7:
time: 465 us; the launch traced here: 456 us
  Pallas kernels  452 us (97%)
    pallas_call x3, Pallas kernels, call(): pl.pallas_call(kernel, out_shape=tuple((shape_of(o.shape, o.dtype) for o,...  452 us

profile of v7, /device:TPU:0, one launch (start us, length us, event | category | flops | bytes accessed | tf_op | source)
XLA Modules:
  0.0 455.9 jit_solution(17260613656758866292)
XLA Ops:
  0.6 1.5 copy.27
  2.1 1.5 copy.28
  3.6 223.6 %forward.1 = (bf16[2,128,2048]{2,1,0:T(8,128)(2,1)}, f32[2,3,128,128]{3,2,1,0:T(8,128)}, f32[2,4,128,128]{3,2,1,0:T(8,128)}, f32[2,1,4352]{2,1,0:T(1,128)}, bf16...) custom-call(s32[2,4]{1,0:T(2,128)} %bitcast.32, ...), custom_call_target="tpu_custom_call" | custom-call | tf_op jit(solution)/shard_map/forward/pallas_call | solution.py:1817
  227.2 207.4 %backward.1 = (bf16[128,2048]{1,0:T(8,128)(2,1)}, f32[32,2048]{1,0:T(8,128)}, f32[1,2048]{1,0:T(1,128)}, bf16[4,128,2048]{2,1,0:T(8,128)(2,1)}, bf16[4,128,2048]...) custom-call(bf16[32,2048]{1,0:T(8,128)(2,1)} %get-tuple-element.90.r, ...), custom_call_target="tpu_custom_call" | custom-call | tf_op jit(solution)/shard_map/backward/pallas_call | solution.py:1817
  434.6 20.8 %grads.1 = (f32[768,2048]{1,0:T(8,128)}, f32[768,2048]{1,0:T(8,128)}, f32[768,2048]{1,0:T(8,128)}, bf16[2,128,2048]{2,1,0:T(8,128)(2,1)}, f32[1,2048]{1,0:T(1,12...) custom-call(bf16[4,128,768]{2,1,0:T(8,128)(2,1)} %get-tuple-element., ...), custom_call_target="tpu_custom_call" | custom-call | tf_op jit(solution)/shard_map/grads/pallas_call | solution.py:1817
